TPU v7x, 512 devices: a whole 4x8x8 slice. The times are simulated.
512 devices in a mesh: dp: 16 (over y, core), cuts: 32 (over x, z).
Axes of the slice: x: 4, y: 8, z: 8, core: 2. Of those that a mesh axis runs over, the one named last changes fastest.
Arguments:
- tokens: bfloat16 [1024, 6144], P('cuts', 'dp'), may hold values from -6 to 6
- cotangent: bfloat16 [1024, 6144], P('cuts', 'dp'), may hold values from -6 to 6
- w_gate: bfloat16 [2, 6144, 16384], P(None, 'dp', 'cuts'), may hold values from -0.078125 to 0.078125
- w_up: bfloat16 [2, 6144, 16384], P(None, 'dp', 'cuts'), may hold values from -0.078125 to 0.078125
- w_down: bfloat16 [2, 16384, 6144], P(None, 'cuts', 'dp'), may hold values from -0.046875 to 0.046875
- row_token: int32 [1024], replicated, may hold values from 0 to 1023, each once
- block_expert: int32 [8, 1], replicated, may hold values from 0 to 1; in each aligned block of 8 rows (0 to 7, 8 to 15, ...) at most 6 rows name the same one
- gate_weight: float32 [1024], replicated, may hold values from 0.1 to 1
Outputs:
- token_grad: bfloat16 [1024, 6144], P('cuts', 'dp')
- grad_gate: bfloat16 [2, 6144, 16384], P(None, 'dp', 'cuts')
- grad_up: bfloat16 [2, 6144, 16384], P(None, 'dp', 'cuts')
- grad_down: bfloat16 [2, 16384, 6144], P(None, 'cuts', 'dp')
Inputs may be any that keep to these rules, and one draw needn't show every extreme that they name: `row_token`: each token is held by exactly one row. `block_expert`: no expert serves more than 6 blocks, and one serves exactly 6.
All inputs are finite; a program needn't handle non-finite values.
Results may differ from a plain program's by a relative error of at most 0.0057.
Values may be sent and summed in bfloat16 or wider, within the bound.
No kernel may reach another device: no remote copies, remote signals or barrier semaphores. Data moves between devices by JAX's collectives and lax.ppermute only.
A program may use at most 64 MiB of HBM per device.

v0:
```python
import jax
import jax.numpy as jnp
from jax import lax
from jax.sharding import PartitionSpec as P

BLK = 128


def activate(gate_pre, up_pre, down_grad):
    sigmoid_val = jax.nn.sigmoid(gate_pre)
    swish_val = gate_pre * sigmoid_val
    hidden = (swish_val * up_pre).astype(jnp.bfloat16)
    slope_val = sigmoid_val * (1.0 + gate_pre * (1.0 - sigmoid_val))
    gate_grad = (down_grad * up_pre * slope_val).astype(jnp.bfloat16)
    up_grad = (down_grad * swish_val).astype(jnp.bfloat16)
    return (hidden, gate_grad, up_grad)


def per_device(tokens, cotangent, w_gate, w_up, w_down, row_token, block_expert, gate_weight):
    tok_all, cot_all = (
        lax.all_gather(tokens, "cuts", axis=0, tiled=True),
        lax.all_gather(cotangent, "cuts", axis=0, tiled=True),
    )
    n_rows, feature_cols = tok_all.shape
    experts, _, hidden_cols = w_gate.shape
    n_blocks = n_rows // BLK
    token_rows = tok_all[row_token]
    cot_rows = (cot_all[row_token].astype(jnp.float32) * gate_weight[:, None]).astype(jnp.bfloat16)
    expert_of_block = block_expert[:, 0]
    capacity = n_blocks - n_blocks // 4
    block_ids = jnp.arange(n_blocks, dtype=jnp.int32)
    sorted_blocks = jnp.argsort(expert_of_block * n_blocks + block_ids)
    onehot = (expert_of_block[:, None] == jnp.arange(experts, dtype=jnp.int32)[None, :]).astype(
        jnp.int32
    )
    counts = jnp.sum(onehot, axis=0)
    starts = jnp.cumsum(counts) - counts
    slot_pos = jnp.arange(capacity, dtype=jnp.int32)
    slot_valid = slot_pos[None, :] < counts[:, None]
    slot_block = sorted_blocks[jnp.minimum(starts[:, None] + slot_pos[None, :], n_blocks - 1)]
    block_rank = jnp.argsort(sorted_blocks)
    block_slot = expert_of_block * capacity + block_rank - starts[expert_of_block]
    slot_mask = slot_valid.astype(jnp.bfloat16)[:, :, None, None]

    def to_slots(rows):
        blocks = rows.reshape(n_blocks, BLK, rows.shape[1])
        return blocks[slot_block] * slot_mask

    def to_rows(slots):
        flat = slots.reshape(experts * capacity, BLK, slots.shape[-1])
        return flat[block_slot].reshape(n_rows, slots.shape[-1])

    tok_slots = to_slots(token_rows)
    cot_slots = to_slots(cot_rows)
    gate_part = to_rows(
        jnp.einsum("ecbd,edf->ecbf", tok_slots, w_gate, preferred_element_type=jnp.float32)
    )
    up_part = to_rows(
        jnp.einsum("ecbd,edf->ecbf", tok_slots, w_up, preferred_element_type=jnp.float32)
    )
    down_part = to_rows(
        jnp.einsum("ecbd,efd->ecbf", cot_slots, w_down, preferred_element_type=jnp.float32)
    )
    gate_pre, up_pre, down_grad = lax.psum((gate_part, up_part, down_part), "dp")
    hidden, gate_grad, up_grad = activate(gate_pre, up_pre, down_grad)
    hid_slots = to_slots(hidden)
    gg_slots = to_slots(gate_grad)
    ug_slots = to_slots(up_grad)
    grad_down = jnp.einsum(
        "ecbf,ecbd->efd", hid_slots, cot_slots, preferred_element_type=jnp.float32
    )
    grad_gate = jnp.einsum(
        "ecbd,ecbf->edf", tok_slots, gg_slots, preferred_element_type=jnp.float32
    )
    grad_up = jnp.einsum("ecbd,ecbf->edf", tok_slots, ug_slots, preferred_element_type=jnp.float32)
    term_slots = jnp.einsum("ecbf,edf->ecbd", gg_slots, w_gate, preferred_element_type=jnp.float32)
    term_slots = term_slots + jnp.einsum(
        "ecbf,edf->ecbd", ug_slots, w_up, preferred_element_type=jnp.float32
    )
    row_part = to_rows(term_slots)
    inverse = jnp.argsort(row_token)
    token_part = row_part[inverse]
    token_grad = lax.psum_scatter(token_part, "cuts", scatter_dimension=0, tiled=True).astype(
        jnp.bfloat16
    )
    return (
        token_grad,
        grad_gate.astype(jnp.bfloat16),
        grad_up.astype(jnp.bfloat16),
        grad_down.astype(jnp.bfloat16),
    )


def solution(mesh):
    return jax.shard_map(
        per_device,
        mesh=mesh,
        in_specs=(
            P("cuts", "dp"),
            P("cuts", "dp"),
            P(None, "dp", "cuts"),
            P(None, "dp", "cuts"),
            P(None, "cuts", "dp"),
            P(),
            P(),
            P(),
        ),
        out_specs=(
            P("cuts", "dp"),
            P(None, "dp", "cuts"),
            P(None, "dp", "cuts"),
            P(None, "cuts", "dp"),
        ),
        check_vma=False,
    )
```

profile of v0, /device:TPU:1, one launch (start us, length us, event | category | flops | bytes accessed | tf_op | source)
XLA Modules:
  0.0 539.7 jit_solution(5017530233611683371)
XLA Ops:
  7.2 0.0 copy-start
  7.2 0.0 copy-start.11
  7.2 0.0 all-reduce.3.cloned.1.call-start
  7.2 0.7 iota_add_fusion
  8.0 0.7 fusion.39
  8.6 0.8 fusion.38
  9.4 0.1 compare_convert_fusion
  9.5 0.2 reduce-window.7
  9.6 0.1 compare_select_fusion.3
  9.7 0.1 reshape.177
  9.8 1.0 sort.48
  10.8 0.7 gather_fusion.1
  11.4 0.1 gather.46
  11.5 0.1 reshape.185
  11.6 0.7 fusion.36
  12.3 44.5 %all_gather.7 = bf16[1024,384]{1,0:T(8,128)(2,1)S(1)} all-gather(bf16[32,384]{1,0:T(8,128)(2,1)} %param.8), channel_id=1, replica_groups=mesh['dp'=16,'cuts'=32] {'cuts'}, dimensions={0}, use_global_device_ids=true | all-gather | bytes 811008 | tf_op jit(solution)/shard_map/all_gather | solution.py:21
  56.9 0.6 gather_fusion.3
  57.5 1.0 sort.49
  58.5 0.0 copy-done.11
  58.5 3.9 gather_fusion.5
  62.4 0.0 copy-start.6
  62.4 0.8 gather_fusion.6
  63.2 0.3 copy-done.6
  63.6 2.8 fusion.19
  66.3 0.0 copy-done
  66.3 2.7 fusion.15
  69.0 3.9 gather_fusion.7
  72.9 3.9 gather_fusion.8
  76.8 0.0 copy-done.9
  76.8 37.1 %all_gather.6 = bf16[1024,384]{1,0:T(8,128)(2,1)S(1)} all-gather(bf16[32,384]{1,0:T(8,128)(2,1)S(1)} %copy-done.9), channel_id=1, replica_groups=mesh['dp'=16,'cuts'=32] {'cuts'}, dimensions={0}, use_global_device_ids=true | all-gather | bytes 811008 | tf_op jit(solution)/shard_map/all_gather | solution.py:22
  113.9 3.9 gather_fusion
  117.9 0.9 fusion.1
  118.8 0.0 copy-start.8
  118.8 1.8 gather_fusion.2
  120.5 0.0 copy-done.8
  120.5 4.0 fusion.12
  124.5 4.0 gather_fusion.4
  128.5 0.0 all-reduce.3.cloned.1.call-update
  128.5 0.2 reduce-scatter.2.cloned.1.call-start
  128.7 0.4 copy-done.10
  129.2 4.4 sort.50
  133.5 147.9 %all-reduce.3.cloned.1.call-done = (f32[1024,512]{1,0:T(8,128)}, f32[1024,512]{1,0:T(8,128)}, f32[1024,512]{1,0:T(8,128)}) async-done(((f32[1024,512]{1,0:T(8,128)}, f32[1024,512]{1,0:T(8,128)}, f32[1024,512]{1,0:T(8,128)}), (f32[1024,512]{1,0:T(8,128)}, f32[1024,512]{1,0:T(8,128)}, f32[1024,512]{1,0:T(8,128)})) %all-reduce.3.cloned.1.call-update) | async-done | bytes 6291472 | tf_op jit(solution)/shard_map/psum | solution.py:64
  281.4 5.6 %multiply_convert_fusion = (bf16[1024,512]{1,0:T(8,128)(2,1)}, bf16[1024,512]{1,0:T(8,128)(2,1)}, bf16[1024,512]{1,0:T(8,128)(2,1)S(1)}) fusion(f32[1024,512]{1,0:T(8,128)} %get-tuple-element.12, f32[1024,512]{1,0:T(8,128)} %get-tuple-element.10, f32[1024,512]{1,0:T(8,128)} %get-tuple-element.11), kind=kLoop, calls=%fused_computation.14 | loop fusion | flops 7864320 | bytes 9437184 | tf_op jit(solution)/shard_map/convert_element_type | solution.py:12
  287.0 3.1 gather_fusion.9
  290.1 2.6 copy.27
  292.7 4.2 fusion.9
  296.9 1.8 gather_fusion.10
  298.7 1.9 copy.29
  300.6 0.0 copy-start.3
  300.6 5.3 convolution_add_fusion
  305.9 0.0 copy-done.3
  305.9 2.3 gather_fusion.11
  308.2 4.8 gather_fusion.12
  313.0 0.0 reduce-scatter.2.cloned.1.call-update
  313.0 1.2 copy-done.1
  314.2 1.9 gather_fusion.13
  316.1 2.8 copy.35
  318.9 1.9 bitcast_convert_fusion.1
  320.8 0.0 copy-done.2
  320.8 2.0 bitcast_convert_fusion.2
  322.8 0.0 copy-done.5
  322.8 1.9 bitcast_convert_fusion
  324.7 206.7 %reduce-scatter.2.cloned.1.call-done = f32[32,384]{1,0:T(8,128)} async-done(((f32[1024,384]{1,0:T(8,128)}), f32[32,384]{1,0:T(8,128)}) %reduce-scatter.2.cloned.1.call-update) | async-done | bytes 49168 | tf_op jit(solution)/shard_map/reduce_scatter | solution.py:83
  531.4 1.4 convert_element_type.49
  (20 shorter events, 0.1 us)
Async XLA Ops:
  7.2 59.1 %copy-start = (bf16[2,384,512]{2,1,0:T(8,128)(2,1)S(1)}, bf16[2,384,512]{2,1,0:T(8,128)(2,1)}, u32[]{:S(2)}) copy-start(bf16[2,384,512]{2,1,0:T(8,128)(2,1)} %param.10) | copy-start | bytes 2359300
  7.2 51.3 %copy-start.11 = (s32[8,1]{0,1:T(1,128)S(1)}, s32[8,1]{0,1:T(1,128)}, u32[]{:S(2)}) copy-start(s32[8,1]{0,1:T(1,128)} %param.14) | copy-start | bytes 100
  7.2 274.2 %all-reduce.3.cloned.1.call-start = ((), (), s32[]{:S(2)}) async-start(), calls=%async_computation.2 | async-start | bytes 12582912 | tf_op jit(solution)/shard_map/psum | solution.py:64
  62.4 1.1 copy-start.6
  72.9 3.9 copy-start.9
  118.8 1.8 copy-start.8
  128.5 0.7 copy-start.10
  128.5 402.9 %reduce-scatter.2.cloned.1.call-start = ((), (), s32[]{:S(2)}) async-start(), calls=%async_computation.1 | async-start | bytes 1622016 | tf_op jit(solution)/shard_map/reduce_scatter | solution.py:83
  300.6 5.3 copy-start.3
  313.0 1.2 copy-start.1
  316.1 2.8 copy-start.4
  318.9 1.9 copy-start.2
  320.8 2.0 copy-start.5
  320.8 2.0 copy-start.7
Sparse Core Ops, SparseCore 0:
  128.6 152.7 all-reduce.2
  313.1 218.2 reduce-scatter.1
where the time goes:
time: 545 us; the launch traced here: 540 us
  waiting for transfers between devices  355 us (65%)
  blocking collectives  81.6 us (15%)
  local copies, waits for them, and re-layouts  46.9 us (9%)
  matrix products  24.7 us (5%)
  other arithmetic  17.4 us (3%)
  between operations  14.2 us (3%)
    reduce_scatter x1, waiting for transfers between devices, per_device(): lax.psum_scatter(token_part, 'cuts', scatter_dimension=0, tiled=True)  207 us
    psum x1, waiting for transfers between devices, per_device(): lax.psum((gate_part, up_part, down_part), 'dp')  148 us
    all_gather x1, blocking collectives, per_device(): lax.all_gather(tokens, 'cuts', axis=0, tiled=True)  44.5 us
    all_gather x1, blocking collectives, per_device(): lax.all_gather(cotangent, 'cuts', axis=0, tiled=True)  37.1 us
    gather x8, local copies, waits for them, and re-layouts, to_slots(): return blocks[slot_block] * slot_mask  16.6 us
    gather x4, local copies, waits for them, and re-layouts, to_rows(): return flat[block_slot].reshape(n_rows, slots.shape[-1])  14.1 us
  transfers between devices with their start and end apart: 2, of which 2 were waited for; matrix products, arithmetic and copies ran while one was open for 3% of the time, Pallas kernels for 0%

commit v1 on v0

v1 whole, which is shorter than its diff:
```python
import functools

import jax
import jax.numpy as jnp
from jax import lax
from jax.experimental import pallas as pl
from jax.experimental.pallas import tpu as pltpu
from jax.sharding import Mesh
from jax.sharding import PartitionSpec as P

BF = jnp.bfloat16
F32 = jnp.float32
ROWS = 256
VMEM_BYTES = 48 * 2**20


def dot(a, b, ca, cb):
    return lax.dot_general(a, b, (((ca,), (cb,)), ((), ())), preferred_element_type=F32)


def activate(gate_pre, up_pre, down_grad):
    sigmoid_val = jax.nn.sigmoid(gate_pre)
    swish_val = gate_pre * sigmoid_val
    slope_val = sigmoid_val * (1.0 + gate_pre * (1.0 - sigmoid_val))
    gate_grad = (down_grad * up_pre * slope_val).astype(BF)
    up_grad = (down_grad * swish_val).astype(BF)
    return gate_grad, up_grad


def call(body, outs, flops, args):
    in_specs = [
        pl.BlockSpec(memory_space=pltpu.SMEM if a.ndim == 1 else pltpu.VMEM) for a in args
    ]
    moved = sum(a.size * a.dtype.itemsize for a in (*args, *outs))
    return pl.pallas_call(
        body,
        out_shape=outs,
        in_specs=in_specs,
        out_specs=[pl.BlockSpec(memory_space=pltpu.VMEM) for _ in outs],
        compiler_params=pltpu.CompilerParams(vmem_limit_bytes=VMEM_BYTES),
        cost_estimate=pl.CostEstimate(flops=flops, bytes_accessed=moved, transcendentals=0),
    )(*args)


def by_expert(rows, expert, experts):
    return [jnp.where(expert == e, rows, jnp.zeros_like(rows)) for e in range(experts)]


def forward_body(cb, n_w, core_ref, x_ref, expert_ref, *refs):
    w_refs, (keep_ref, give_ref) = refs[:n_w], refs[n_w:]
    n_y, part, width = keep_ref.shape
    experts = w_refs[0].shape[0]
    hid = width // n_w
    core = core_ref[0]
    pairs = ROWS // (2 * part)

    @pl.loop(0, n_y // pairs)
    def _(i):
        at = pl.ds(pl.multiple_of(i * ROWS, ROWS), ROWS)
        masked = by_expert(x_ref[at, :], expert_ref[at, :], experts)
        for k, w_ref in enumerate(w_refs):
            out = dot(masked[0], w_ref[0], 1, cb)
            for e in range(1, experts):
                out = out + dot(masked[e], w_ref[e], 1, cb)
            for j in range(pairs):
                lo = out[2 * j * part : (2 * j + 1) * part]
                hi = out[(2 * j + 1) * part : (2 * j + 2) * part]
                cols = slice(k * hid, (k + 1) * hid)
                keep_ref[i * pairs + j, :, cols] = jnp.where(core == 0, lo, hi)
                give_ref[i * pairs + j, :, cols] = jnp.where(core == 0, hi, lo).astype(BF)


def terms_body(x_ref, expert_ref, gate_ref, up_ref, out_ref):
    experts, _, hid = gate_ref.shape

    @pl.loop(0, x_ref.shape[0] // ROWS)
    def _(i):
        at = pl.ds(pl.multiple_of(i * ROWS, ROWS), ROWS)
        expert = expert_ref[at, :]
        gates = by_expert(x_ref[at, :hid], expert, experts)
        ups = by_expert(x_ref[at, hid:], expert, experts)
        out = 0.0
        for e in range(experts):
            out = out + dot(gates[e], gate_ref[e], 1, 1) + dot(ups[e], up_ref[e], 1, 1)
        out_ref[at, :] = out.astype(BF)


def total_body(x_ref, out_ref):
    out = x_ref[0].astype(F32)
    for i in range(1, x_ref.shape[0]):
        out = out + x_ref[i].astype(F32)
    out_ref[...] = out.astype(BF)


def make(n_y, n_core, n_x, n_z):
    dp, cuts = ("y", "core"), ("x", "z")
    n_dp, n_cuts = n_y * n_core, n_x * n_z
    swap = [(i, n_core - 1 - i) for i in range(n_core)]

    def per_device(tokens, cotangent, w_gate, w_up, w_down, row_token, block_expert, gate_weight):
        own, cols = tokens.shape
        n_tok = row_token.shape[0]
        experts, _, hid = w_gate.shape
        blk = n_tok // block_expert.shape[0]
        part = n_tok // n_dp
        core = lax.axis_index("core").astype(jnp.int32).reshape(1)
        first = (lax.axis_index("x") * n_z + lax.axis_index("z")) * own
        work = 2 * n_tok * experts * cols * hid

        expert_row = jnp.repeat(block_expert[:, 0], blk)
        holds = row_token[None, :] == jnp.arange(n_tok, dtype=jnp.int32)[:, None]
        expert_tok = jnp.sum(jnp.where(holds, expert_row[None, :], 0), axis=1)[:, None]
        holds_own = row_token[None, :] == first + jnp.arange(own, dtype=jnp.int32)[:, None]
        weight_own = jnp.sum(jnp.where(holds_own, gate_weight[None, :], 0.0), axis=1)
        cot_own = (cotangent.astype(F32) * weight_own[:, None]).astype(BF)

        def spread(rows):
            return jnp.broadcast_to(rows[None], (n_cuts,) + rows.shape)

        def exchange(x, axes):
            return lax.all_to_all(x, axes, split_axis=0, concat_axis=0, tiled=True)

        def reduce_dp(x, cb, weights):
            shape = (n_y, part, len(weights) * hid)
            outs = [jax.ShapeDtypeStruct(shape, F32), jax.ShapeDtypeStruct(shape, BF)]
            body = functools.partial(forward_body, cb, len(weights))
            keep, give = call(body, outs, work * len(weights), (core, x, expert_tok, *weights))
            came = lax.ppermute(give, "core", swap)
            chip = (keep + came.astype(F32)).astype(BF)
            return jnp.sum(exchange(chip, "y").astype(F32), axis=0)

        tok = exchange(spread(tokens), cuts)
        tok, cot_spread = lax.optimization_barrier((tok, spread(cot_own)))
        cot = exchange(cot_spread, cuts).reshape(n_tok, cols)
        tok = tok.reshape(n_tok, cols)

        pre = reduce_dp(tok, 0, (w_gate, w_up))
        gate_pre, up_pre = pre[:, :hid], pre[:, hid:]
        hidden = (gate_pre * jax.nn.sigmoid(gate_pre) * up_pre).astype(BF)
        gate_pre, up_pre, hidden = lax.optimization_barrier((gate_pre, up_pre, hidden))
        hidden = lax.all_gather(hidden, dp, axis=0, tiled=True)
        down_grad = reduce_dp(cot, 1, (w_down,))
        grads = jnp.concatenate(activate(gate_pre, up_pre, down_grad), axis=1)
        grads = lax.all_gather(grads, dp, axis=0, tiled=True)

        outs = [jax.ShapeDtypeStruct((n_tok, cols), BF)]
        (terms,) = call(terms_body, outs, 2 * work, (grads, expert_tok, w_gate, w_up))
        terms = exchange(terms.reshape(n_cuts, own, cols), cuts)
        outs = [jax.ShapeDtypeStruct((own, cols), BF)]
        (token_grad,) = call(total_body, outs, terms.size, (terms,))

        masks = [expert_tok == e for e in range(experts)]
        tok_by = jnp.concatenate([jnp.where(m, tok, 0) for m in masks], axis=1)
        grad_gate = dot(tok_by, grads[:, :hid], 0, 0).astype(BF).reshape(w_gate.shape)
        grad_up = dot(tok_by, grads[:, hid:], 0, 0).astype(BF).reshape(w_up.shape)
        grad_down = [dot(hidden, jnp.where(m, cot, 0), 0, 0).astype(BF) for m in masks]
        return token_grad, grad_gate, grad_up, jnp.stack(grad_down)

    return per_device


def solution(mesh):
    n_y, n_core, n_x, n_z = 8, 2, 4, 8
    fine = Mesh(mesh.devices.reshape(n_y, n_core, n_x, n_z), ("y", "core", "x", "z"))
    dp, cuts = ("y", "core"), ("x", "z")
    return jax.shard_map(
        make(n_y, n_core, n_x, n_z),
        mesh=fine,
        in_specs=(
            P(cuts, dp),
            P(cuts, dp),
            P(None, dp, cuts),
            P(None, dp, cuts),
            P(None, cuts, dp),
            P(),
            P(),
            P(),
        ),
        out_specs=(P(cuts, dp), P(None, dp, cuts), P(None, dp, cuts), P(None, cuts, dp)),
        check_vma=False,
    )
```

time: 545 us -> 225 us (0.41)
  waiting for transfers between devices: 355 us -> 124 us
  blocking collectives: 81.6 us -> 0 us
  starting transfers between devices: 0.26 us -> 52.6 us
  local copies, waits for them, and re-layouts: 46.9 us -> 7.33 us
  matrix products: 24.7 us -> 6.71 us
  Pallas kernels: 0 us -> 9.77 us
  other arithmetic: 17.4 us -> 9.64 us
    reduce_scatter x1 -> x0, waiting for transfers between devices: 207 us -> none  [per_device(): lax.psum_scatter(token_part, 'cuts', scatter_dimension=0, tiled=True)]
    psum x1 -> x0, waiting for transfers between devices: 148 us -> none  [per_device(): lax.psum((gate_part, up_part, down_part), 'dp')]
    all_gather x2 -> x0, blocking collectives: 81.6 us -> none  [the longest x1 44.5 us: per_device(): lax.all_gather(tokens, 'cuts', axis=0, tiled=True)]
    all_gather x0 -> x2, waiting for transfers between devices: none -> 69.4 us  [the longest x1 46 us: per_device(): grads = lax.all_gather(grads, dp, axis=0, tiled=True)]
    all_to_all x0 -> x5, waiting for transfers between devices: none -> 50.1 us  [exchange(): return lax.all_to_all(x, axes, split_axis=0, concat_axis=0, tiled=True)]
    gather x18 -> x0, local copies, waits for them, and re-layouts: 44.7 us -> none  [the longest x8 16.6 us: to_slots(): return blocks[slot_block] * slot_mask]
    all_to_all x0 -> x5, starting transfers between devices: none -> 42.4 us  [exchange(): return lax.all_to_all(x, axes, split_axis=0, concat_axis=0, tiled=True)]
    dot_general x8 -> x4, matrix products: 24.7 us -> 6.71 us  [dot(): lax.dot_general(a, b, (((ca,), (cb,)), ((), ())), preferred_element_type=...]
  transfers between devices with their start and end apart: 2 -> 9, of which waited for: 2 -> 8; matrix products, arithmetic and copies ran while one was open for 3% -> 7% of each run, Pallas kernels for 0% -> 4%
where the time goes in v1:
time: 225 us; the launch traced here: 224 us
  waiting for transfers between devices  124 us (55%)
  starting transfers between devices  52.6 us (23%)
  between operations  14.3 us (6%)
  Pallas kernels  9.77 us (4%)
  other arithmetic  9.64 us (4%)
  local copies, waits for them, and re-layouts  7.33 us (3%)
  matrix products  6.71 us (3%)
    all_to_all x5, waiting for transfers between devices, exchange(): return lax.all_to_all(x, axes, split_axis=0, concat_axis=0, tiled=True)  50.1 us
    all_gather x1, waiting for transfers between devices, per_device(): grads = lax.all_gather(grads, dp, axis=0, tiled=True)  46 us
    all_to_all x5, starting transfers between devices, exchange(): return lax.all_to_all(x, axes, split_axis=0, concat_axis=0, tiled=True)  42.4 us
    all_gather x1, waiting for transfers between devices, per_device(): hidden = lax.all_gather(hidden, dp, axis=0, tiled=True)  23.5 us
    ppermute x2, starting transfers between devices, reduce_dp(): came = lax.ppermute(give, 'core', swap)  10 us
    pallas_call x4, Pallas kernels, call(): pl.pallas_call(body, out_shape=outs, in_specs=in_specs, out_specs=[pl.Blo...  9.77 us
    dot_general x4, matrix products, dot(): lax.dot_general(a, b, (((ca,), (cb,)), ((), ())), preferred_element_type=...  6.71 us
  transfers between devices with their start and end apart: 9, of which 8 were waited for; matrix products, arithmetic and copies ran while one was open for 7% of the time, Pallas kernels for 4%

profile of v1, /device:TPU:1, one launch (start us, length us, event | category | flops | bytes accessed | tf_op | source)
XLA Modules:
  0.0 224.4 jit_solution(8859565057713980771)
XLA Ops:
  7.2 0.0 copy-start
  7.2 0.0 copy-start.11
  7.2 0.0 copy-start.12
  7.2 0.0 copy-start.10
  7.2 1.7 broadcast_in_dim.76
  8.9 13.8 %all-to-all-start = ((bf16[32,32,384]{2,1,0:T(8,128)(2,1)}), bf16[32,32,384]{2,1,0:T(8,128)(2,1)S(1)}, u32[]{:S(2)}, u32[]{:S(2)}) async-start(bf16[32,32,384]{2,1,0:T(8,128)(2,1)} %broadcast_in_dim.76), calls=%async_computation | async-start | bytes 1572864 | tf_op jit(solution)/shard_map/all_to_all | solution.py:121
  22.8 0.0 copy-done
  22.8 0.1 broadcast_bitcast_fusion
  22.9 0.0 copy-done.11
  22.9 0.5 select_reduce_fusion
  23.4 0.2 copy.15.expert_ref
  23.6 0.0 copy-done.12
  23.6 0.2 select_reduce_fusion.1
  23.8 0.0 copy-done.10
  23.8 0.1 multiply_convert_fusion.3
  23.9 18.1 %all-to-all-done = bf16[32,32,384]{2,1,0:T(8,128)(2,1)S(1)} async-done(((bf16[32,32,384]{2,1,0:T(8,128)(2,1)}), bf16[32,32,384]{2,1,0:T(8,128)(2,1)S(1)}, u32[]{:S(2)}, u32[]{:S(2)}) %all-to-all-start) | async-done | bytes 786464 | tf_op jit(solution)/shard_map/all_to_all | solution.py:121
  42.0 0.9 broadcast_in_dim.79
  43.0 8.4 %all-to-all-start.1 = ((bf16[32,32,384]{2,1,0:T(8,128)(2,1)}), bf16[32,32,384]{2,1,0:T(8,128)(2,1)S(1)}, u32[]{:S(2)}, u32[]{:S(2)}) async-start(bf16[32,32,384]{2,1,0:T(8,128)(2,1)} %broadcast_in_dim.79), calls=%async_computation.1 | async-start | bytes 1572864 | tf_op jit(solution)/shard_map/all_to_all | solution.py:121
  51.3 0.0 copy-done.4
  51.4 0.0 copy-start.6
  51.4 1.1 copy-done.6
  52.5 3.1 %shard_map.112 = (f32[8,64,1024]{2,1,0:T(8,128)S(1)}, bf16[8,64,1024]{2,1,0:T(8,128)(2,1)S(1)}) custom-call(s32[1]{0:T(128)} %bitcast.core_ref, bf16[1024,384]{1,0:T(8,128)(2,1)S(1)} %bitcast.19, s32[1024,1]{1,0:T(8,128)S(1)} %copy.15.expert_ref, bf16[2,384,512]{2,1,0:T(8,128)(2,1)S(1)} %copy-done.4, bf16[2,384,512]{2,1,0:T(8,128)(2,1)S(1)} %copy-done.6), custom_call_target="tpu_custom_call" | custom-call | flops 1610612736 | bytes 5509124 | tf_op jit(solution)/shard_map/pallas_call | solution.py:35
  55.6 3.4 %collective-permute-start.1 = (bf16[8,64,1024]{2,1,0:T(8,128)(2,1)S(1)}, bf16[8,64,1024]{2,1,0:T(8,128)(2,1)S(1)}, u32[]{:S(2)}, u32[]{:S(2)}) collective-permute-start(bf16[8,64,1024]{2,1,0:T(8,128)(2,1)S(1)} %get-tuple-element.18), channel_id=1, source_target_pairs={{0,32},{32,0},{1,33},{33,1},{2,34},{34,2},{3,35},{35,3},{4,36},{36... | collective-permute-start | bytes 3145736 | tf_op jit(solution)/shard_map/ppermute | solution.py:128
  58.9 2.3 %collective-permute-done.1 = bf16[8,64,1024]{2,1,0:T(8,128)(2,1)S(1)} collective-permute-done((bf16[8,64,1024]{2,1,0:T(8,128)(2,1)S(1)}, bf16[8,64,1024]{2,1,0:T(8,128)(2,1)S(1)}, u32[]{:S(2)}, u32[]{:S(2)}) %collective-permute-start.1) | collective-permute-done | bytes 1048608 | tf_op jit(solution)/shard_map/ppermute | solution.py:128
  61.2 1.4 add_convert_fusion
  62.6 8.6 %all-to-all-done.1 = bf16[32,32,384]{2,1,0:T(8,128)(2,1)S(1)} async-done(((bf16[32,32,384]{2,1,0:T(8,128)(2,1)}), bf16[32,32,384]{2,1,0:T(8,128)(2,1)S(1)}, u32[]{:S(2)}, u32[]{:S(2)}) %all-to-all-start.1) | async-done | bytes 786464 | tf_op jit(solution)/shard_map/all_to_all | solution.py:121
  71.1 6.8 %all-to-all-start.3 = ((bf16[8,64,1024]{2,1,0:T(8,128)(2,1)}), bf16[8,64,1024]{2,1,0:T(8,128)(2,1)}, u32[]{:S(2)}, u32[]{:S(2)}) async-start(bf16[8,64,1024]{2,1,0:T(8,128)(2,1)} %add_convert_fusion), calls=%async_computation.3 | async-start | bytes 2097152 | tf_op jit(solution)/shard_map/all_to_all | solution.py:121
  78.0 0.0 copy-done.3
  78.0 2.0 shard_map.111
  79.9 6.7 %collective-permute-start = (bf16[8,64,512]{2,1,0:T(8,128)(2,1)S(1)}, bf16[8,64,512]{2,1,0:T(8,128)(2,1)S(1)}, u32[]{:S(2)}, u32[]{:S(2)}) collective-permute-start(bf16[8,64,512]{2,1,0:T(8,128)(2,1)S(1)} %get-tuple-element.15), channel_id=1, source_target_pairs={{0,32},{32,0},{1,33},{33,1},{2,34},{34,2},{3,35},{35,3},{4,36},{36... | collective-permute-start | bytes 1572872 | tf_op jit(solution)/shard_map/ppermute | solution.py:128
  86.6 1.5 collective-permute-done
  88.1 1.0 add_convert_fusion.1
  89.1 14.1 %all-to-all-done.3 = bf16[8,64,1024]{2,1,0:T(8,128)(2,1)} async-done(((bf16[8,64,1024]{2,1,0:T(8,128)(2,1)}), bf16[8,64,1024]{2,1,0:T(8,128)(2,1)}, u32[]{:S(2)}, u32[]{:S(2)}) %all-to-all-start.3) | async-done | bytes 1048608 | tf_op jit(solution)/shard_map/all_to_all | solution.py:121
  103.2 3.5 %all-to-all-start.2 = ((bf16[8,64,512]{2,1,0:T(8,128)(2,1)}), bf16[8,64,512]{2,1,0:T(8,128)(2,1)S(1)}, u32[]{:S(2)}, u32[]{:S(2)}) async-start(bf16[8,64,512]{2,1,0:T(8,128)(2,1)} %add_convert_fusion.1), calls=%async_computation.2 | async-start | bytes 1048576 | tf_op jit(solution)/shard_map/all_to_all | solution.py:121
  106.7 0.0 all-gather.3.cloned.1.call-start
  106.7 1.4 convert_reduce_fusion
  108.2 0.7 multiply_convert_fusion.2
  108.8 9.4 %all-to-all-done.2 = bf16[8,64,512]{2,1,0:T(8,128)(2,1)S(1)} async-done(((bf16[8,64,512]{2,1,0:T(8,128)(2,1)}), bf16[8,64,512]{2,1,0:T(8,128)(2,1)S(1)}, u32[]{:S(2)}, u32[]{:S(2)}) %all-to-all-start.2) | async-done | bytes 524320 | tf_op jit(solution)/shard_map/all_to_all | solution.py:121
  118.2 0.1 convert_reduce_fusion.1
  118.3 1.0 multiply_convert_fusion.1
  119.3 0.7 pad_maximum_fusion.4
  119.9 0.0 all-gather.3.cloned.1.call-update
  120.0 0.0 all-gather.5.cloned.1.call-start
  120.0 0.7 all-gather.5.cloned.1.call-update
  120.7 46.0 %all-gather.3.cloned.1.call-done.x_ref = bf16[1024,1024]{1,0:T(8,128)(2,1)} async-done(((bf16[64,1024]{1,0:T(8,128)(2,1)}), bf16[1024,1024]{1,0:T(8,128)(2,1)}) %all-gather.3.cloned.1.call-update) | async-done | bytes 2097168 | tf_op jit(solution)/shard_map/all_gather | solution.py:144
  166.7 0.0 copy-done.5
  166.7 1.6 copy-done.1
  168.3 1.1 copy-done.7
  169.4 4.0 %shard_map.113 = bf16[1024,384]{1,0:T(8,128)(2,1)} custom-call(bf16[1024,1024]{1,0:T(8,128)(2,1)S(1)} %copy-done.1, s32[1024,1]{1,0:T(8,128)S(1)} %copy.15.expert_ref, bf16[2,384,512]{2,1,0:T(8,128)(2,1)S(1)} %copy-done.5, bf16[2,384,512]{2,1,0:T(8,128)(2,1)S(1)} %copy-done.7), custom_call_target="tpu_custom_call" | custom-call | flops 1610612736 | bytes 4460544 | tf_op jit(solution)/shard_map/pallas_call | solution.py:35
  173.4 9.9 %all-to-all-start.4 = ((bf16[32,32,384]{2,1,0:T(8,128)(2,1)}), bf16[32,32,384]{2,1,0:T(8,128)(2,1)S(1)}, u32[]{:S(2)}, u32[]{:S(2)}) async-start(bf16[32,32,384]{2,1,0:T(8,128)(2,1)} %bitcast.6), calls=%async_computation.4 | async-start | bytes 1572864 | tf_op jit(solution)/shard_map/all_to_all | solution.py:121
  183.4 1.7 broadcast_select_fusion.1
  185.1 23.5 %all-gather.5.cloned.1.call-done = bf16[1024,512]{1,0:T(8,128)(2,1)} async-done(((bf16[64,512]{1,0:T(8,128)(2,1)}), bf16[1024,512]{1,0:T(8,128)(2,1)}) %all-gather.5.cloned.1.call-update) | async-done | bytes 1048592 | tf_op jit(solution)/shard_map/all_gather | solution.py:141
  208.6 2.1 fusion.1
  210.7 0.0 copy-done.13
  210.7 0.0 copy-start.8
  210.7 0.0 copy-start.9
  210.7 0.8 fusion
  211.5 1.0 pad_maximum_fusion.3
  212.5 0.0 copy-done.8
  212.5 0.5 copy-done.9
  213.0 1.9 convolution_convert_fusion.1
  214.9 1.9 convolution_convert_fusion
  216.8 0.0 all-to-all-done.4.x_ref
  216.8 0.7 shard_map.114
  (10 shorter events, 0.0 us)
Async XLA Ops:
  7.2 15.6 %copy-start = (s32[8,1]{0,1:T(1,128)S(1)}, s32[8,1]{0,1:T(1,128)}, u32[]{:S(2)}) copy-start(s32[8,1]{0,1:T(1,128)} %param.14) | copy-start | bytes 100
  7.2 15.7 %copy-start.11 = (s32[1024]{0:T(1024)S(1)}, s32[1024]{0:T(1024)}, u32[]{:S(2)}) copy-start(s32[1024]{0:T(1024)} %param.13) | copy-start | bytes 12292
  7.2 16.4 %copy-start.12 = (f32[1024]{0:T(1024)S(1)}, f32[1024]{0:T(1024)}, u32[]{:S(2)}) copy-start(f32[1024]{0:T(1024)} %param.15) | copy-start | bytes 12292
  7.2 16.6 %copy-start.10 = (bf16[32,384]{1,0:T(8,128)(2,1)S(1)}, bf16[32,384]{1,0:T(8,128)(2,1)}, u32[]{:S(2)}) copy-start(bf16[32,384]{1,0:T(8,128)(2,1)} %param.9) | copy-start | bytes 73732
  8.9 42.4 %copy-start.4 = (bf16[2,384,512]{2,1,0:T(8,128)(2,1)S(1)}, bf16[2,384,512]{2,1,0:T(8,128)(2,1)}, u32[]{:S(2)}) copy-start(bf16[2,384,512]{2,1,0:T(8,128)(2,1)} %gate_ref.1) | copy-start | bytes 2359300
  8.9 33.1 %all-to-all-start = ((bf16[32,32,384]{2,1,0:T(8,128)(2,1)}), bf16[32,32,384]{2,1,0:T(8,128)(2,1)S(1)}, u32[]{:S(2)}, u32[]{:S(2)}) async-start(bf16[32,32,384]{2,1,0:T(8,128)(2,1)} %broadcast_in_dim.76), calls=%async_computation | async-start | bytes 1572864 | tf_op jit(solution)/shard_map/all_to_all | solution.py:121
  43.0 28.2 %all-to-all-start.1 = ((bf16[32,32,384]{2,1,0:T(8,128)(2,1)}), bf16[32,32,384]{2,1,0:T(8,128)(2,1)S(1)}, u32[]{:S(2)}, u32[]{:S(2)}) async-start(bf16[32,32,384]{2,1,0:T(8,128)(2,1)} %broadcast_in_dim.79), calls=%async_computation.1 | async-start | bytes 1572864 | tf_op jit(solution)/shard_map/all_to_all | solution.py:121
  51.4 1.1 copy-start.6
  55.6 5.6 %collective-permute-start.1 = (bf16[8,64,1024]{2,1,0:T(8,128)(2,1)S(1)}, bf16[8,64,1024]{2,1,0:T(8,128)(2,1)S(1)}, u32[]{:S(2)}, u32[]{:S(2)}) collective-permute-start(bf16[8,64,1024]{2,1,0:T(8,128)(2,1)S(1)} %get-tuple-element.18), channel_id=1, source_target_pairs={{0,32},{32,0},{1,33},{33,1},{2,34},{34,2},{3,35},{35,3},{4,36},{36... | collective-permute-start | bytes 3145736 | tf_op jit(solution)/shard_map/ppermute | solution.py:128
  62.6 15.4 %copy-start.3 = (bf16[2,512,384]{2,1,0:T(8,128)(2,1)S(1)}, bf16[2,512,384]{2,1,0:T(8,128)(2,1)}, u32[]{:S(2)}) copy-start(bf16[2,512,384]{2,1,0:T(8,128)(2,1)} %refs_0_.2) | copy-start | bytes 2359300
  71.1 32.0 %all-to-all-start.3 = ((bf16[8,64,1024]{2,1,0:T(8,128)(2,1)}), bf16[8,64,1024]{2,1,0:T(8,128)(2,1)}, u32[]{:S(2)}, u32[]{:S(2)}) async-start(bf16[8,64,1024]{2,1,0:T(8,128)(2,1)} %add_convert_fusion), calls=%async_computation.3 | async-start | bytes 2097152 | tf_op jit(solution)/shard_map/all_to_all | solution.py:121
  79.9 8.2 %collective-permute-start = (bf16[8,64,512]{2,1,0:T(8,128)(2,1)S(1)}, bf16[8,64,512]{2,1,0:T(8,128)(2,1)S(1)}, u32[]{:S(2)}, u32[]{:S(2)}) collective-permute-start(bf16[8,64,512]{2,1,0:T(8,128)(2,1)S(1)} %get-tuple-element.15), channel_id=1, source_target_pairs={{0,32},{32,0},{1,33},{33,1},{2,34},{34,2},{3,35},{35,3},{4,36},{36... | collective-permute-start | bytes 1572872 | tf_op jit(solution)/shard_map/ppermute | solution.py:128
  89.1 77.6 %copy-start.5 = (bf16[2,384,512]{2,1,0:T(8,128)(2,1)S(1)}, bf16[2,384,512]{2,1,0:T(8,128)(2,1)}, u32[]{:S(2)}) copy-start(bf16[2,384,512]{2,1,0:T(8,128)(2,1)} %gate_ref.1) | copy-start | bytes 2359300
  103.2 15.1 %all-to-all-start.2 = ((bf16[8,64,512]{2,1,0:T(8,128)(2,1)}), bf16[8,64,512]{2,1,0:T(8,128)(2,1)S(1)}, u32[]{:S(2)}, u32[]{:S(2)}) async-start(bf16[8,64,512]{2,1,0:T(8,128)(2,1)} %add_convert_fusion.1), calls=%async_computation.2 | async-start | bytes 1048576 | tf_op jit(solution)/shard_map/all_to_all | solution.py:121
  106.7 60.0 %all-gather.3.cloned.1.call-start = ((), (), s32[]{:S(2)}) async-start(), calls=%async_computation.5 | async-start | bytes 2228224 | tf_op jit(solution)/shard_map/all_gather | solution.py:144
  120.0 88.6 %all-gather.5.cloned.1.call-start = ((), (), s32[]{:S(2)}) async-start(), calls=%async_computation.6 | async-start | bytes 1114112 | tf_op jit(solution)/shard_map/all_gather | solution.py:141
  166.7 1.6 copy-start.1
  168.3 1.1 copy-start.7
  173.4 43.4 %all-to-all-start.4 = ((bf16[32,32,384]{2,1,0:T(8,128)(2,1)}), bf16[32,32,384]{2,1,0:T(8,128)(2,1)S(1)}, u32[]{:S(2)}, u32[]{:S(2)}) async-start(bf16[32,32,384]{2,1,0:T(8,128)(2,1)} %bitcast.6), calls=%async_computation.4 | async-start | bytes 1572864 | tf_op jit(solution)/shard_map/all_to_all | solution.py:121
  208.6 2.1 copy-start.13
  210.7 1.8 copy-start.2
  210.7 1.8 copy-start.8
  210.7 2.3 %copy-start.9 = (bf16[1024,384]{1,0:T(8,128)(2,1)S(1)}, bf16[1024,384]{1,0:T(8,128)(2,1)}, u32[]{:S(2)}) copy-start(bf16[1024,384]{1,0:T(8,128)(2,1)} %get-tuple-element.23) | copy-start | bytes 2359300
Sparse Core Ops, SparseCore 0:
  120.1 46.5 all-gather.2
  168.8 39.7 all-gather.4

commit v2 on v1

v2 whole, which is shorter than its diff:
```python
import functools

import jax
import jax.numpy as jnp
from jax import lax
from jax.experimental import pallas as pl
from jax.experimental.pallas import tpu as pltpu
from jax.sharding import Mesh
from jax.sharding import PartitionSpec as P

BF = jnp.bfloat16
F32 = jnp.float32
ROWS = 256
VMEM_BYTES = 20 * 2**20


def dot(a, b, ca, cb):
    return lax.dot_general(a, b, (((ca,), (cb,)), ((), ())), preferred_element_type=F32)


def activate(gate_pre, up_pre, down_grad):
    sigmoid_val = jax.nn.sigmoid(gate_pre)
    swish_val = gate_pre * sigmoid_val
    hidden = (swish_val * up_pre).astype(BF)
    slope_val = sigmoid_val * (1.0 + gate_pre * (1.0 - sigmoid_val))
    gate_grad = (down_grad * up_pre * slope_val).astype(BF)
    up_grad = (down_grad * swish_val).astype(BF)
    return hidden, gate_grad, up_grad


def call(body, outs, flops, args):
    in_specs = [
        pl.BlockSpec(memory_space=pltpu.SMEM if a.ndim == 1 else pltpu.VMEM) for a in args
    ]
    moved = sum(a.size * a.dtype.itemsize for a in (*args, *outs))
    return pl.pallas_call(
        body,
        out_shape=outs,
        in_specs=in_specs,
        out_specs=[pl.BlockSpec(memory_space=pltpu.VMEM) for _ in outs],
        compiler_params=pltpu.CompilerParams(vmem_limit_bytes=VMEM_BYTES),
        cost_estimate=pl.CostEstimate(flops=flops, bytes_accessed=moved, transcendentals=0),
    )(*args)


def by_expert(rows, expert, experts):
    return [jnp.where(expert == e, rows, jnp.zeros_like(rows)) for e in range(experts)]


def forward_body(core_ref, expert_ref, wg_ref, wu_ref, wd_ref, *refs):
    chunks, (tok_ref, cot_ref, keep_ref, give_ref) = refs[:-4], refs[-4:]
    n_y, part, _ = keep_ref.shape
    experts, cols, hid = wg_ref.shape
    n_z = len(chunks) - 1
    step = tok_ref.shape[0] // n_z
    core = core_ref[0]
    pairs = ROWS // (2 * part)
    far = n_z // 2
    for i in range(n_z):
        at = slice(i * step, (i + 1) * step)
        if i == far:
            tok, cot = chunks[far][...], chunks[n_z][...]
        else:
            tok, cot = chunks[i][:, 0], chunks[i][:, 1]
        tok_ref[at, :] = tok.reshape(step, cols)
        cot_ref[at, :] = cot.reshape(step, cols)

    @pl.loop(0, n_y // pairs)
    def _(i):
        at = pl.ds(pl.multiple_of(i * ROWS, ROWS), ROWS)
        expert = expert_ref[at, :]
        toks = by_expert(tok_ref[at, :], expert, experts)
        cots = by_expert(cot_ref[at, :], expert, experts)
        for k, (xs, w_ref, cb) in enumerate(((toks, wg_ref, 0), (toks, wu_ref, 0), (cots, wd_ref, 1))):
            out = dot(xs[0], w_ref[0], 1, cb)
            for e in range(1, experts):
                out = out + dot(xs[e], w_ref[e], 1, cb)
            for j in range(pairs):
                lo = out[2 * j * part : (2 * j + 1) * part]
                hi = out[(2 * j + 1) * part : (2 * j + 2) * part]
                to = slice(k * hid, (k + 1) * hid)
                keep_ref[i * pairs + j, :, to] = jnp.where(core == 0, lo, hi)
                give_ref[i * pairs + j, :, to] = jnp.where(core == 0, hi, lo).astype(BF)


def terms_body(at_ref, expert_ref, gate_ref, up_ref, own_ref, other_ref, grads_ref, out_ref):
    experts, _, hid = gate_ref.shape
    n_y, n_core, part, width = grads_ref.shape
    n_x, n_z, own, cols = out_ref.shape
    y, core, z = at_ref[0], at_ref[1], at_ref[2]
    for i in range(n_y):
        to = lax.rem(y + i, n_y)
        grads_ref[to, core] = own_ref[i]
        grads_ref[to, 1 - core] = other_ref[i]
    per_y = n_core * part
    per_z = n_x * own

    @pl.loop(0, n_y * per_y // ROWS)
    def _(i):
        at = pl.ds(pl.multiple_of(i * ROWS, ROWS), ROWS)
        expert = expert_ref[at, :]
        rows = grads_ref[pl.ds(i * (ROWS // per_y), ROWS // per_y)].reshape(ROWS, width)
        gates = by_expert(rows[:, :hid], expert, experts)
        ups = by_expert(rows[:, hid:], expert, experts)
        out = 0.0
        for e in range(experts):
            out = out + dot(gates[e], gate_ref[e], 1, 1) + dot(ups[e], up_ref[e], 1, 1)
        out = out.astype(BF)
        for j in range(ROWS // per_z):
            to = lax.rem(z + i * (ROWS // per_z) + j, n_z)
            for x in range(n_x):
                out_ref[x, to] = out[j * per_z + x * own : j * per_z + (x + 1) * own]


def total_body(x_ref, out_ref):
    out = x_ref[0].astype(F32)
    for i in range(1, x_ref.shape[0]):
        out = out + x_ref[i].astype(F32)
    out_ref[...] = out.astype(BF)


def ring(x, axis, n, first, second):
    up = [(i, (i + 1) % n) for i in range(n)]
    down = [(i, (i - 1) % n) for i in range(n)]
    got = [x] + [None] * (n - 1)
    a = b = x
    for s in range(1, n // 2):
        a, b = lax.ppermute(a, axis, up), lax.ppermute(b, axis, down)
        got[n - s], got[s] = a, b
    got[n // 2] = (lax.ppermute(first(a), axis, up), lax.ppermute(second(b), axis, down))
    return got


def make(n_y, n_core, n_x, n_z):
    dp, cuts = ("y", "core"), ("x", "z")
    n_dp, n_cuts = n_y * n_core, n_x * n_z
    swap = [(i, n_core - 1 - i) for i in range(n_core)]

    def per_device(tokens, cotangent, w_gate, w_up, w_down, row_token, block_expert, gate_weight):
        own, cols = tokens.shape
        n_tok = row_token.shape[0]
        experts, _, hid = w_gate.shape
        blk = n_tok // block_expert.shape[0]
        part = n_tok // n_dp
        place = [lax.axis_index(a).astype(jnp.int32) for a in ("y", "core", "x", "z")]
        y, core, x, z = place
        work = 2 * n_tok * experts * cols * hid

        def exchange(v, axes):
            return lax.all_to_all(v, axes, split_axis=0, concat_axis=0, tiled=True)

        first = (x * n_z + z) * own
        holds_own = row_token[None, :] == first + jnp.arange(own, dtype=jnp.int32)[:, None]
        weight_own = jnp.sum(jnp.where(holds_own, gate_weight[None, :], 0.0), axis=1)
        cot_own = (cotangent.astype(F32) * weight_own[:, None]).astype(BF)
        both = jnp.stack([tokens, cot_own])
        both = exchange(jnp.broadcast_to(both[None], (n_x,) + both.shape), "x")
        chunks = ring(both, "z", n_z, lambda v: v[:, 0], lambda v: v[:, 1])
        far = chunks[n_z // 2]
        chunks[n_z // 2] = far[0]
        chunks.append(far[1])

        from_z = lax.rem(z + jnp.arange(n_z, dtype=jnp.int32), n_z)[:, None, None]
        from_x = jnp.arange(n_x, dtype=jnp.int32)[None, :, None]
        row_id = (from_x * n_z + from_z) * own + jnp.arange(own, dtype=jnp.int32)[None, None, :]
        row_id = row_id.reshape(n_tok)
        expert_row = jnp.repeat(block_expert[:, 0], blk)
        holds = row_token[None, :] == row_id[:, None]
        expert_tok = jnp.sum(jnp.where(holds, expert_row[None, :], 0), axis=1)[:, None]

        outs = [
            jax.ShapeDtypeStruct((n_tok, cols), BF),
            jax.ShapeDtypeStruct((n_tok, cols), BF),
            jax.ShapeDtypeStruct((n_y, part, 3 * hid), F32),
            jax.ShapeDtypeStruct((n_y, part, 3 * hid), BF),
        ]
        args = (core.reshape(1), expert_tok, w_gate, w_up, w_down, *chunks)
        tok, cot, keep, give = call(forward_body, outs, 3 * work, args)
        came = lax.ppermute(give, "core", swap)
        chip = (keep + came.astype(F32)).astype(BF)
        pre = jnp.sum(exchange(chip, "y").astype(F32), axis=0)
        hidden, gate_grad, up_grad = activate(
            pre[:, :hid], pre[:, hid : 2 * hid], pre[:, 2 * hid :]
        )
        hidden = lax.all_gather(hidden, dp, axis=0, tiled=True)
        grads = jnp.concatenate([gate_grad, up_grad], axis=1)
        parts = ring(grads, "y", n_y, lambda v: v[:, :hid], lambda v: v[:, hid:])
        parts[n_y // 2] = jnp.concatenate(parts[n_y // 2], axis=1)
        mine = jnp.stack(parts)
        others = lax.ppermute(mine, "core", swap)

        outs = [
            jax.ShapeDtypeStruct((n_y, n_core, part, 2 * hid), BF),
            jax.ShapeDtypeStruct((n_x, n_z, own, cols), BF),
        ]
        args = (jnp.stack([y, core, z]), expert_tok, w_gate, w_up, mine, others)
        grads, terms = call(terms_body, outs, 2 * work, args)
        grads, hidden = lax.optimization_barrier((grads.reshape(n_tok, 2 * hid), hidden))
        terms = exchange(terms.reshape(n_cuts, own, cols), cuts)
        outs = [jax.ShapeDtypeStruct((own, cols), BF)]
        (token_grad,) = call(total_body, outs, terms.size, (terms,))

        masks = [expert_tok == e for e in range(experts)]
        tok_by = jnp.concatenate([jnp.where(m, tok, 0) for m in masks], axis=1)
        grad_gate = dot(tok_by, grads[:, :hid], 0, 0).astype(BF).reshape(w_gate.shape)
        grad_up = dot(tok_by, grads[:, hid:], 0, 0).astype(BF).reshape(w_up.shape)
        grad_down = [dot(hidden, jnp.where(m, cot, 0), 0, 0).astype(BF) for m in masks]
        return token_grad, grad_gate, grad_up, jnp.stack(grad_down)

    return per_device


def solution(mesh):
    n_y, n_core, n_x, n_z = 8, 2, 4, 8
    fine = Mesh(mesh.devices.reshape(n_y, n_core, n_x, n_z), ("y", "core", "x", "z"))
    dp, cuts = ("y", "core"), ("x", "z")
    return jax.shard_map(
        make(n_y, n_core, n_x, n_z),
        mesh=fine,
        in_specs=(
            P(cuts, dp),
            P(cuts, dp),
            P(None, dp, cuts),
            P(None, dp, cuts),
            P(None, cuts, dp),
            P(),
            P(),
            P(),
        ),
        out_specs=(P(cuts, dp), P(None, dp, cuts), P(None, dp, cuts), P(None, cuts, dp)),
        check_vma=False,
    )
```

time: 225 us -> 213 us (0.947); the launches traced: 224 us -> 209 us
  waiting for transfers between devices: 124 us -> 29.9 us
  blocking collectives: 0 us -> 45.8 us
  starting transfers between devices: 52.6 us -> 83.6 us
    ppermute x2 -> x18, starting transfers between devices: 10 us -> 71.8 us  [the longest x12 42.4 us: ring(): a, b = (lax.ppermute(a, axis, up), lax.ppermute(b, axis, down))]
    all_gather x1 -> x0, waiting for transfers between devices: 46 us -> none  [per_device(): grads = lax.all_gather(grads, dp, axis=0, tiled=True)]
    all_to_all x0 -> x1, blocking collectives: none -> 45.8 us  [exchange(): return lax.all_to_all(v, axes, split_axis=0, concat_axis=0, tiled=True)]
    all_to_all x5 -> x2, waiting for transfers between devices: 50.1 us -> 14.7 us  [exchange(): return lax.all_to_all(v, axes, split_axis=0, concat_axis=0, tiled=True)]
    all_to_all x5 -> x2, starting transfers between devices: 42.4 us -> 11.7 us  [exchange(): return lax.all_to_all(v, axes, split_axis=0, concat_axis=0, tiled=True)]
    all_gather x1, waiting for transfers between devices: 23.5 us -> 0.01 us  [per_device(): hidden = lax.all_gather(hidden, dp, axis=0, tiled=True)]
    ppermute x2 -> x18, waiting for transfers between devices: 3.78 us -> 15.1 us  [the longest x12 4.78 us: ring(): a, b = (lax.ppermute(a, axis, up), lax.ppermute(b, axis, down))]
    convert_element_type x5 -> x2, other arithmetic: 4.08 us -> 1.18 us  [the longest x1 0.7 us: activate(): hidden = (swish_val * up_pre).astype(BF)]
  transfers between devices with their start and end apart: 9 -> 21, of which waited for: 8 -> 13; matrix products, arithmetic and copies ran while one was open for 7% -> 6% of each run, Pallas kernels for 4% -> 3%
where the time goes in v2:
time: 213 us; the launch traced here: 209 us
  starting transfers between devices  83.6 us (39%)
  blocking collectives  45.8 us (22%)
  waiting for transfers between devices  29.9 us (14%)
  between operations  14.5 us (7%)
  Pallas kernels  10.5 us (5%)
  local copies, waits for them, and re-layouts  8.96 us (4%)
  other arithmetic  8.63 us (4%)
  matrix products  6.73 us (3%)
    all_to_all x1, blocking collectives, exchange(): return lax.all_to_all(v, axes, split_axis=0, concat_axis=0, tiled=True)  45.8 us
    ppermute x12, starting transfers between devices, ring(): a, b = (lax.ppermute(a, axis, up), lax.ppermute(b, axis, down))  42.4 us
    all_to_all x2, waiting for transfers between devices, exchange(): return lax.all_to_all(v, axes, split_axis=0, concat_axis=0, tiled=True)  14.7 us
    all_to_all x2, starting transfers between devices, exchange(): return lax.all_to_all(v, axes, split_axis=0, concat_axis=0, tiled=True)  11.7 us
    pallas_call x3, Pallas kernels, call(): pl.pallas_call(body, out_shape=outs, in_specs=in_specs, out_specs=[pl.Blo...  10.5 us
    ppermute x2, starting transfers between devices, ring(): lax.ppermute(second(b), axis, down)  9.13 us
    ppermute x1, starting transfers between devices, per_device(): came = lax.ppermute(give, 'core', swap)  8.32 us
    ppermute x1, starting transfers between devices, per_device(): others = lax.ppermute(mine, 'core', swap)  8.19 us
  transfers between devices with their start and end apart: 21, of which 13 were waited for; matrix products, arithmetic and copies ran while one was open for 6% of the time, Pallas kernels for 3%

profile of v2, /device:TPU:1, one launch (start us, length us, event | category | flops | bytes accessed | tf_op | source)
XLA Modules:
  0.0 208.5 jit_solution(4305763025983474297)
XLA Ops:
  7.2 1.0 select_reduce_fusion.1
  8.2 0.8 fusion.12
  9.0 0.7 pad_maximum_fusion.5
  9.8 0.7 broadcast_in_dim.79
  10.5 4.8 %all-to-all-start = ((bf16[4,2,32,384]{3,2,1,0:T(8,128)(2,1)}), bf16[4,2,32,384]{3,2,1,0:T(8,128)(2,1)S(1)}, u32[]{:S(2)}, u32[]{:S(2)}) async-start(bf16[4,2,32,384]{3,2,1,0:T(8,128)(2,1)} %broadcast_in_dim.79), calls=%async_computation | async-start | bytes 393216 | tf_op jit(solution)/shard_map/all_to_all | solution.py:150
  15.4 5.2 %all-to-all-done.refs_0_ = bf16[4,2,32,384]{3,2,1,0:T(8,128)(2,1)S(1)} async-done(((bf16[4,2,32,384]{3,2,1,0:T(8,128)(2,1)}), bf16[4,2,32,384]{3,2,1,0:T(8,128)(2,1)S(1)}, u32[]{:S(2)}, u32[]{:S(2)}) %all-to-all-start) | async-done | bytes 196640 | tf_op jit(solution)/shard_map/all_to_all | solution.py:150
  20.5 4.0 %collective-permute-start.3 = (bf16[4,2,32,384]{3,2,1,0:T(8,128)(2,1)S(1)}, bf16[4,2,32,384]{3,2,1,0:T(8,128)(2,1)S(1)}, u32[]{:S(2)}, u32[]{:S(2)}) collective-permute-start(bf16[4,2,32,384]{3,2,1,0:T(8,128)(2,1)S(1)} %all-to-all-done.refs_0_), channel_id=1, source_target_pairs={{0,1},{1,2},{2,3},{3,4},{4,5},{5,6},{6,7},{7,0},{8,9},{9,10},{10,1... | collective-permute-start | bytes 589832 | tf_op jit(solution)/shard_map/ppermute | solution.py:128
  24.6 8.6 %collective-permute-start = (bf16[4,2,32,384]{3,2,0,1:T(8,128)(2,1)S(1)}, bf16[4,2,32,384]{3,2,0,1:T(8,128)(2,1)S(1)}, u32[]{:S(2)}, u32[]{:S(2)}) collective-permute-start(bf16[4,2,32,384]{3,2,0,1:T(8,128)(2,1)S(1)} %copy.34), channel_id=1, source_target_pairs={{0,7},{1,0},{2,1},{3,2},{4,3},{5,4},{6,5},{7,6},{8,15},{9,8},{10,9... | collective-permute-start | bytes 589832 | tf_op jit(solution)/shard_map/ppermute | solution.py:128
  33.2 1.0 collective-permute-done.3.refs_7_
  34.2 1.9 collective-permute-start.4
  36.1 0.1 iota_add_fusion
  36.2 0.1 add.79
  36.3 4.6 %collective-permute-start.1 = (bf16[4,2,32,384]{3,2,0,1:T(8,128)(2,1)S(1)}, bf16[4,2,32,384]{3,2,0,1:T(8,128)(2,1)S(1)}, u32[]{:S(2)}, u32[]{:S(2)}) collective-permute-start(bf16[4,2,32,384]{3,2,0,1:T(8,128)(2,1)S(1)} %collective-permute-done), channel_id=1, source_target_pairs={{0,7},{1,0},{2,1},{3,2},{4,3},{5,4},{6,5},{7,6},{8,15},{9,8},{10,9... | collective-permute-start | bytes 589832 | tf_op jit(solution)/shard_map/ppermute | solution.py:128
  40.9 1.0 collective-permute-done.4.refs_6_
  41.8 1.9 collective-permute-start.5
  43.8 4.6 %collective-permute-start.2 = (bf16[4,2,32,384]{3,2,0,1:T(8,128)(2,1)S(1)}, bf16[4,2,32,384]{3,2,0,1:T(8,128)(2,1)S(1)}, u32[]{:S(2)}, u32[]{:S(2)}) collective-permute-start(bf16[4,2,32,384]{3,2,0,1:T(8,128)(2,1)S(1)} %collective-permute-done.1), channel_id=1, source_target_pairs={{0,7},{1,0},{2,1},{3,2},{4,3},{5,4},{6,5},{7,6},{8,15},{9,8},{10,9... | collective-permute-start | bytes 589832 | tf_op jit(solution)/shard_map/ppermute | solution.py:128
  48.5 1.0 collective-permute-done.5.refs_5_
  49.5 1.9 collective-permute-start.6
  51.4 0.7 slice_bitcast_fusion
  52.1 4.7 %collective-permute-start.7 = (bf16[4,32,384]{2,1,0:T(8,128)(2,1)}, bf16[4,32,384]{2,1,0:T(8,128)(2,1)S(1)}, u32[]{:S(2)}, u32[]{:S(2)}) collective-permute-start(bf16[4,32,384]{2,1,0:T(8,128)(2,1)} %slice_bitcast_fusion), channel_id=1, source_target_pairs={{0,7},{1,0},{2,1},{3,2},{4,3},{5,4},{6,5},{7,6},{8,15},{9,8},{10,9... | collective-permute-start | bytes 294920 | tf_op jit(solution)/shard_map/ppermute | solution.py:130
  56.7 1.2 select_reduce_fusion
  58.0 0.2 copy.39.expert_ref
  58.4 0.3 collective-permute-done.7.refs_8_
  58.7 0.6 copy-done.9
  59.3 1.1 copy-done.3
  60.5 0.9 copy-done.6
  61.4 0.9 copy-done.8
  62.3 0.9 copy-done.10
  63.2 4.4 %shard_map.111 = (bf16[1024,384]{1,0:T(8,128)(2,1)S(1)}, bf16[1024,384]{1,0:T(8,128)(2,1)S(1)}, f32[8,64,1536]{2,1,0:T(8,128)S(1)}, bf16[8,64,1536]{2,1,0:T(8,128)(2,1)S(1)}) custom-call(s32[1]{0:T(128)} %bitcast.1.core_ref, s32[1024,1]{1,0:T(8,128)S(1)} %copy.39.expert_ref, bf16[2,384,512]{2,1,0:T(8,128)(2,1)S(1)} %copy-done.2, ...), custom_call_target="tpu_custom_call" | custom-call | flops 2415919104 | bytes 10227716 | tf_op jit(solution)/shard_map/pallas_call | solution.py:36
  67.6 8.3 %collective-permute-start.8 = (bf16[8,64,1536]{2,1,0:T(8,128)(2,1)S(1)}, bf16[8,64,1536]{2,1,0:T(8,128)(2,1)S(1)}, u32[]{:S(2)}, u32[]{:S(2)}) collective-permute-start(bf16[8,64,1536]{2,1,0:T(8,128)(2,1)S(1)} %get-tuple-element.13), channel_id=1, source_target_pairs={{0,32},{32,0},{1,33},{33,1},{2,34},{34,2},{3,35},{35,3},{4,36},{36... | collective-permute-start | bytes 4718600 | tf_op jit(solution)/shard_map/ppermute | solution.py:179
  76.0 3.0 %collective-permute-done.8 = bf16[8,64,1536]{2,1,0:T(8,128)(2,1)S(1)} collective-permute-done((bf16[8,64,1536]{2,1,0:T(8,128)(2,1)S(1)}, bf16[8,64,1536]{2,1,0:T(8,128)(2,1)S(1)}, u32[]{:S(2)}, u32[]{:S(2)}) %collective-permute-start.8) | collective-permute-done | bytes 1572896 | tf_op jit(solution)/shard_map/ppermute | solution.py:179
  79.0 0.5 add_convert_fusion
  79.5 45.8 %all_to_all.15 = bf16[8,64,1536]{2,1,0:T(8,128)(2,1)S(1)} all-to-all(bf16[8,64,1536]{2,1,0:T(8,128)(2,1)S(1)} %add_convert_fusion), channel_id=1, replica_groups=mesh['y'=8,'core'=2,'x'=4,'z'=8] {'y'}, dimensions={0} | all-to-all | bytes 3145728 | tf_op jit(solution)/shard_map/all_to_all | solution.py:150
  125.2 0.2 convert_reduce_fusion
  125.5 0.7 multiply_convert_fusion
  126.2 0.7 pad_maximum_fusion.4
  126.8 1.9 collective-permute-start.9
  128.7 3.4 %collective-permute-start.12 = (bf16[64,1024]{1,0:T(8,128)(2,1)}, bf16[64,1024]{1,0:T(8,128)(2,1)S(1)}, u32[]{:S(2)}, u32[]{:S(2)}) collective-permute-start(bf16[64,1024]{1,0:T(8,128)(2,1)} %pad_maximum_fusion.4), channel_id=1, source_target_pairs={{0,64},{64,128},{128,192},{192,256},{256,320},{320,384},{384,448},... | collective-permute-start | bytes 393224 | tf_op jit(solution)/shard_map/ppermute | solution.py:128
  132.2 0.6 collective-permute-done.9
  132.7 3.1 %collective-permute-start.10 = (bf16[64,1024]{1,0:T(8,128)(2,1)S(1)}, bf16[64,1024]{1,0:T(8,128)(2,1)S(1)}, u32[]{:S(2)}, u32[]{:S(2)}) collective-permute-start(bf16[64,1024]{1,0:T(8,128)(2,1)S(1)} %collective-permute-done.9), channel_id=1, source_target_pairs={{0,448},{64,0},{128,64},{192,128},{256,192},{320,256},{384,320},{4... | collective-permute-start | bytes 393224 | tf_op jit(solution)/shard_map/ppermute | solution.py:128
  135.9 2.2 %collective-permute-start.13 = (bf16[64,1024]{1,0:T(8,128)(2,1)S(1)}, bf16[64,1024]{1,0:T(8,128)(2,1)S(1)}, u32[]{:S(2)}, u32[]{:S(2)}) collective-permute-start(bf16[64,1024]{1,0:T(8,128)(2,1)S(1)} %collective-permute-done.12), channel_id=1, source_target_pairs={{0,64},{64,128},{128,192},{192,256},{256,320},{320,384},{384,448},... | collective-permute-start | bytes 393224 | tf_op jit(solution)/shard_map/ppermute | solution.py:128
  138.1 0.4 collective-permute-done.10
  138.4 4.3 %collective-permute-start.11 = (bf16[64,1024]{1,0:T(8,128)(2,1)S(1)}, bf16[64,1024]{1,0:T(8,128)(2,1)S(1)}, u32[]{:S(2)}, u32[]{:S(2)}) collective-permute-start(bf16[64,1024]{1,0:T(8,128)(2,1)S(1)} %collective-permute-done.10), channel_id=1, source_target_pairs={{0,448},{64,0},{128,64},{192,128},{256,192},{320,256},{384,320},{4... | collective-permute-start | bytes 393224 | tf_op jit(solution)/shard_map/ppermute | solution.py:128
  142.8 1.9 collective-permute-start.14
  144.7 0.5 collective-permute-done.11
  145.2 4.4 %collective-permute-start.16 = (bf16[64,512]{1,0:T(8,128)(2,1)S(1)}, bf16[64,512]{1,0:T(8,128)(2,1)S(1)}, u32[]{:S(2)}, u32[]{:S(2)}) collective-permute-start(bf16[64,512]{1,0:T(8,128)(2,1)S(1)} %slice.42), channel_id=1, source_target_pairs={{0,448},{64,0},{128,64},{192,128},{256,192},{320,256},{384,320},{4... | collective-permute-start | bytes 196616 | tf_op jit(solution)/shard_map/ppermute | solution.py:130
  149.7 0.3 collective-permute-done.14
  150.0 1.9 collective-permute-start.15
  152.0 4.7 %collective-permute-done.15 = bf16[64,512]{1,0:T(8,128)(2,1)S(1)} collective-permute-done((bf16[64,512]{1,0:T(8,128)(2,1)S(1)}, bf16[64,512]{1,0:T(8,128)(2,1)S(1)}, u32[]{:S(2)}, u32[]{:S(2)}) %collective-permute-start.15) | collective-permute-done | bytes 65568 | tf_op jit(solution)/shard_map/ppermute | solution.py:130
  156.7 8.2 %collective-permute-start.17 = (bf16[8,64,1024]{2,1,0:T(8,128)(2,1)S(1)}, bf16[8,64,1024]{2,1,0:T(8,128)(2,1)}, u32[]{:S(2)}, u32[]{:S(2)}) collective-permute-start(bf16[8,64,1024]{2,1,0:T(8,128)(2,1)S(1)} %bitcast_dynamic-update-slice_fusion.own_ref), channel_id=1, source_target_pairs={{0,32},{32,0},{1,33},{33,1},{2,34},{34,2},{3,35},{35,3},{4,36},{36... | collective-permute-start | bytes 3145736 | tf_op jit(solution)/shard_map/ppermute | solution.py:190
  164.9 0.1 pad_add_fusion.at_ref
  165.0 2.3 %collective-permute-done.17.other_ref = bf16[8,64,1024]{2,1,0:T(8,128)(2,1)} collective-permute-done((bf16[8,64,1024]{2,1,0:T(8,128)(2,1)S(1)}, bf16[8,64,1024]{2,1,0:T(8,128)(2,1)}, u32[]{:S(2)}, u32[]{:S(2)}) %collective-permute-start.17) | collective-permute-done | bytes 1048608 | tf_op jit(solution)/shard_map/ppermute | solution.py:190
  167.3 1.1 copy-done.4
  168.5 5.4 %shard_map.112 = (bf16[8,2,64,1024]{3,2,1,0:T(8,128)(2,1)S(1)}, bf16[4,8,32,384]{3,2,1,0:T(8,128)(2,1)}) custom-call(s32[3]{0:T(128)S(1)} %pad_add_fusion.at_ref, s32[1024,1]{1,0:T(8,128)S(1)} %copy.39.expert_ref, bf16[2,384,512]{2,1,0:T(8,128)(2,1)S(1)} %copy-done.2, bf16[2,384,512]{2,1,0:T(8,128)(2,1)S(1)} %copy-done.4, ...), custom_call_target="tpu_custom_call" | custom-call | flops 1610612736 | bytes 6557708 | tf_op jit(solution)/shard_map/pallas_call | solution.py:36
  173.9 1.4 copy-done.11
  175.3 6.9 %all-to-all-start.2 = ((bf16[32,32,384]{2,1,0:T(8,128)(2,1)}), bf16[32,32,384]{2,1,0:T(8,128)(2,1)S(1)}, u32[]{:S(2)}, u32[]{:S(2)}) async-start(bf16[32,32,384]{2,1,0:T(8,128)(2,1)} %bitcast.18), calls=%async_computation.2 | async-start | bytes 1572864 | tf_op jit(solution)/shard_map/all_to_all | solution.py:150
  182.1 1.5 broadcast_select_fusion.1
  183.7 2.1 %fusion.1 = bf16[1,512,384]{2,1,0:T(8,128)(2,1)S(1)} fusion(bf16[1024,512]{1,0:T(8,128)(2,1)} %all-gather.2.cloned.1.call-done, bf16[1024,384]{1,0:T(8,128)(2,1)S(1)} %copy-done.14, pred[1024]{0:T(1024)(128)(4,1)S(1)} %get-tuple-element.26), kind=kOutput, calls=%fused_computation.9 | convolution fusion | flops 403243008 | bytes 2229248 | tf_op jit(solution)/shard_map/dot_general | solution.py:18
  185.8 0.8 fusion
  186.6 1.0 pad_maximum_fusion.3
  187.6 1.9 convolution_convert_fusion.1
  189.5 1.9 convolution_convert_fusion
  191.4 9.5 %all-to-all-done.2.x_ref = bf16[32,32,384]{2,1,0:T(8,128)(2,1)S(1)} async-done(((bf16[32,32,384]{2,1,0:T(8,128)(2,1)}), bf16[32,32,384]{2,1,0:T(8,128)(2,1)S(1)}, u32[]{:S(2)}, u32[]{:S(2)}) %all-to-all-start.2) | async-done | bytes 786464 | tf_op jit(solution)/shard_map/all_to_all | solution.py:150
  201.0 0.7 shard_map.113
  (58 shorter events, 0.5 us)
Async XLA Ops:
  7.2 36.6 %copy-start = (s32[8,1]{0,1:T(1,128)S(1)}, s32[8,1]{0,1:T(1,128)}, u32[]{:S(2)}) copy-start(s32[8,1]{0,1:T(1,128)} %param.14) | copy-start | bytes 100
  7.2 52.1 %copy-start.2 = (bf16[2,384,512]{2,1,0:T(8,128)(2,1)S(1)}, bf16[2,384,512]{2,1,0:T(8,128)(2,1)}, u32[]{:S(2)}) copy-start(bf16[2,384,512]{2,1,0:T(8,128)(2,1)} %gate_ref.1) | copy-start | bytes 2359300
  7.2 52.1 %copy-start.1 = (bf16[2,512,384]{2,1,0:T(8,128)(2,1)S(1)}, bf16[2,512,384]{2,1,0:T(8,128)(2,1)}, u32[]{:S(2)}) copy-start(bf16[2,512,384]{2,1,0:T(8,128)(2,1)} %wd_ref.1) | copy-start | bytes 2359300
  10.5 10.0 %all-to-all-start = ((bf16[4,2,32,384]{3,2,1,0:T(8,128)(2,1)}), bf16[4,2,32,384]{3,2,1,0:T(8,128)(2,1)S(1)}, u32[]{:S(2)}, u32[]{:S(2)}) async-start(bf16[4,2,32,384]{3,2,1,0:T(8,128)(2,1)} %broadcast_in_dim.79), calls=%async_computation | async-start | bytes 393216 | tf_op jit(solution)/shard_map/all_to_all | solution.py:150
  15.3 168.3 %all-gather.2.cloned.1.call-start = ((), (), s32[]{:S(2)}) async-start(), calls=%async_computation.3 | async-start | bytes 1114112 | tf_op jit(solution)/shard_map/all_gather | solution.py:185
  20.5 13.7 %collective-permute-start.3 = (bf16[4,2,32,384]{3,2,1,0:T(8,128)(2,1)S(1)}, bf16[4,2,32,384]{3,2,1,0:T(8,128)(2,1)S(1)}, u32[]{:S(2)}, u32[]{:S(2)}) collective-permute-start(bf16[4,2,32,384]{3,2,1,0:T(8,128)(2,1)S(1)} %all-to-all-done.refs_0_), channel_id=1, source_target_pairs={{0,1},{1,2},{2,3},{3,4},{4,5},{5,6},{6,7},{7,0},{8,9},{9,10},{10,1... | collective-permute-start | bytes 589832 | tf_op jit(solution)/shard_map/ppermute | solution.py:128
  24.6 11.7 %collective-permute-start = (bf16[4,2,32,384]{3,2,0,1:T(8,128)(2,1)S(1)}, bf16[4,2,32,384]{3,2,0,1:T(8,128)(2,1)S(1)}, u32[]{:S(2)}, u32[]{:S(2)}) collective-permute-start(bf16[4,2,32,384]{3,2,0,1:T(8,128)(2,1)S(1)} %copy.34), channel_id=1, source_target_pairs={{0,7},{1,0},{2,1},{3,2},{4,3},{5,4},{6,5},{7,6},{8,15},{9,8},{10,9... | collective-permute-start | bytes 589832 | tf_op jit(solution)/shard_map/ppermute | solution.py:128
  34.2 23.8 %copy-start.5 = (bf16[4,2,32,384]{3,2,1,0:T(8,128)(2,1)}, bf16[4,2,32,384]{3,2,1,0:T(8,128)(2,1)S(1)}, u32[]{:S(2)}) copy-start(bf16[4,2,32,384]{3,2,1,0:T(8,128)(2,1)S(1)} %collective-permute-done.3.refs_7_) | copy-start | bytes 589828
  34.2 7.6 %collective-permute-start.4 = (bf16[4,2,32,384]{3,2,1,0:T(8,128)(2,1)S(1)}, bf16[4,2,32,384]{3,2,1,0:T(8,128)(2,1)S(1)}, u32[]{:S(2)}, u32[]{:S(2)}) collective-permute-start(bf16[4,2,32,384]{3,2,1,0:T(8,128)(2,1)S(1)} %collective-permute-done.3.refs_7_), channel_id=1, source_target_pairs={{0,1},{1,2},{2,3},{3,4},{4,5},{5,6},{6,7},{7,0},{8,9},{9,10},{10,1... | collective-permute-start | bytes 589832 | tf_op jit(solution)/shard_map/ppermute | solution.py:128
  36.3 7.5 %collective-permute-start.1 = (bf16[4,2,32,384]{3,2,0,1:T(8,128)(2,1)S(1)}, bf16[4,2,32,384]{3,2,0,1:T(8,128)(2,1)S(1)}, u32[]{:S(2)}, u32[]{:S(2)}) collective-permute-start(bf16[4,2,32,384]{3,2,0,1:T(8,128)(2,1)S(1)} %collective-permute-done), channel_id=1, source_target_pairs={{0,7},{1,0},{2,1},{3,2},{4,3},{5,4},{6,5},{7,6},{8,15},{9,8},{10,9... | collective-permute-start | bytes 589832 | tf_op jit(solution)/shard_map/ppermute | solution.py:128
  41.8 16.2 %copy-start.7 = (bf16[4,2,32,384]{3,2,1,0:T(8,128)(2,1)}, bf16[4,2,32,384]{3,2,1,0:T(8,128)(2,1)S(1)}, u32[]{:S(2)}) copy-start(bf16[4,2,32,384]{3,2,1,0:T(8,128)(2,1)S(1)} %collective-permute-done.4.refs_6_) | copy-start | bytes 589828
  41.8 7.6 %collective-permute-start.5 = (bf16[4,2,32,384]{3,2,1,0:T(8,128)(2,1)S(1)}, bf16[4,2,32,384]{3,2,1,0:T(8,128)(2,1)S(1)}, u32[]{:S(2)}, u32[]{:S(2)}) collective-permute-start(bf16[4,2,32,384]{3,2,1,0:T(8,128)(2,1)S(1)} %collective-permute-done.4.refs_6_), channel_id=1, source_target_pairs={{0,1},{1,2},{2,3},{3,4},{4,5},{5,6},{6,7},{7,0},{8,9},{9,10},{10,1... | collective-permute-start | bytes 589832 | tf_op jit(solution)/shard_map/ppermute | solution.py:128
  43.8 7.6 %collective-permute-start.2 = (bf16[4,2,32,384]{3,2,0,1:T(8,128)(2,1)S(1)}, bf16[4,2,32,384]{3,2,0,1:T(8,128)(2,1)S(1)}, u32[]{:S(2)}, u32[]{:S(2)}) collective-permute-start(bf16[4,2,32,384]{3,2,0,1:T(8,128)(2,1)S(1)} %collective-permute-done.1), channel_id=1, source_target_pairs={{0,7},{1,0},{2,1},{3,2},{4,3},{5,4},{6,5},{7,6},{8,15},{9,8},{10,9... | collective-permute-start | bytes 589832 | tf_op jit(solution)/shard_map/ppermute | solution.py:128
  49.5 8.9 %collective-permute-start.6 = (bf16[4,32,384]{2,1,0:T(8,128)(2,1)S(1)}, bf16[4,32,384]{2,1,0:T(8,128)(2,1)S(1)}, u32[]{:S(2)}, u32[]{:S(2)}) collective-permute-start(bf16[4,32,384]{2,1,0:T(8,128)(2,1)S(1)} %slice_bitcast_fusion.1), channel_id=1, source_target_pairs={{0,1},{1,2},{2,3},{3,4},{4,5},{5,6},{6,7},{7,0},{8,9},{9,10},{10,1... | collective-permute-start | bytes 294920 | tf_op jit(solution)/shard_map/ppermute | solution.py:130
  52.1 6.6 %collective-permute-start.7 = (bf16[4,32,384]{2,1,0:T(8,128)(2,1)}, bf16[4,32,384]{2,1,0:T(8,128)(2,1)S(1)}, u32[]{:S(2)}, u32[]{:S(2)}) collective-permute-start(bf16[4,32,384]{2,1,0:T(8,128)(2,1)} %slice_bitcast_fusion), channel_id=1, source_target_pairs={{0,7},{1,0},{2,1},{3,2},{4,3},{5,4},{6,5},{7,6},{8,15},{9,8},{10,9... | collective-permute-start | bytes 294920 | tf_op jit(solution)/shard_map/ppermute | solution.py:130
  58.7 0.6 copy-start.9
  59.3 1.1 copy-start.3
  60.5 0.9 copy-start.6
  61.4 0.9 copy-start.8
  62.3 0.9 copy-start.10
  67.6 11.8 %copy-start.13 = (bf16[1024,384]{1,0:T(8,128)(2,1)}, bf16[1024,384]{1,0:T(8,128)(2,1)S(1)}, u32[]{:S(2)}) copy-start(bf16[1024,384]{1,0:T(8,128)(2,1)S(1)} %get-tuple-element.19) | copy-start | bytes 2359300
  67.6 11.3 %collective-permute-start.8 = (bf16[8,64,1536]{2,1,0:T(8,128)(2,1)S(1)}, bf16[8,64,1536]{2,1,0:T(8,128)(2,1)S(1)}, u32[]{:S(2)}, u32[]{:S(2)}) collective-permute-start(bf16[8,64,1536]{2,1,0:T(8,128)(2,1)S(1)} %get-tuple-element.13), channel_id=1, source_target_pairs={{0,32},{32,0},{1,33},{33,1},{2,34},{34,2},{3,35},{35,3},{4,36},{36... | collective-permute-start | bytes 4718600 | tf_op jit(solution)/shard_map/ppermute | solution.py:179
  126.8 5.9 %collective-permute-start.9 = (bf16[64,1024]{1,0:T(8,128)(2,1)}, bf16[64,1024]{1,0:T(8,128)(2,1)S(1)}, u32[]{:S(2)}, u32[]{:S(2)}) collective-permute-start(bf16[64,1024]{1,0:T(8,128)(2,1)} %pad_maximum_fusion.4), channel_id=1, source_target_pairs={{0,448},{64,0},{128,64},{192,128},{256,192},{320,256},{384,320},{4... | collective-permute-start | bytes 393224 | tf_op jit(solution)/shard_map/ppermute | solution.py:128
  128.7 7.1 %collective-permute-start.12 = (bf16[64,1024]{1,0:T(8,128)(2,1)}, bf16[64,1024]{1,0:T(8,128)(2,1)S(1)}, u32[]{:S(2)}, u32[]{:S(2)}) collective-permute-start(bf16[64,1024]{1,0:T(8,128)(2,1)} %pad_maximum_fusion.4), channel_id=1, source_target_pairs={{0,64},{64,128},{128,192},{192,256},{256,320},{320,384},{384,448},... | collective-permute-start | bytes 393224 | tf_op jit(solution)/shard_map/ppermute | solution.py:128
  132.7 5.7 %collective-permute-start.10 = (bf16[64,1024]{1,0:T(8,128)(2,1)S(1)}, bf16[64,1024]{1,0:T(8,128)(2,1)S(1)}, u32[]{:S(2)}, u32[]{:S(2)}) collective-permute-start(bf16[64,1024]{1,0:T(8,128)(2,1)S(1)} %collective-permute-done.9), channel_id=1, source_target_pairs={{0,448},{64,0},{128,64},{192,128},{256,192},{320,256},{384,320},{4... | collective-permute-start | bytes 393224 | tf_op jit(solution)/shard_map/ppermute | solution.py:128
  135.9 6.9 %collective-permute-start.13 = (bf16[64,1024]{1,0:T(8,128)(2,1)S(1)}, bf16[64,1024]{1,0:T(8,128)(2,1)S(1)}, u32[]{:S(2)}, u32[]{:S(2)}) collective-permute-start(bf16[64,1024]{1,0:T(8,128)(2,1)S(1)} %collective-permute-done.12), channel_id=1, source_target_pairs={{0,64},{64,128},{128,192},{192,256},{256,320},{320,384},{384,448},... | collective-permute-start | bytes 393224 | tf_op jit(solution)/shard_map/ppermute | solution.py:128
  138.4 6.8 %collective-permute-start.11 = (bf16[64,1024]{1,0:T(8,128)(2,1)S(1)}, bf16[64,1024]{1,0:T(8,128)(2,1)S(1)}, u32[]{:S(2)}, u32[]{:S(2)}) collective-permute-start(bf16[64,1024]{1,0:T(8,128)(2,1)S(1)} %collective-permute-done.10), channel_id=1, source_target_pairs={{0,448},{64,0},{128,64},{192,128},{256,192},{320,256},{384,320},{4... | collective-permute-start | bytes 393224 | tf_op jit(solution)/shard_map/ppermute | solution.py:128
  142.8 7.2 %collective-permute-start.14 = (bf16[64,1024]{1,0:T(8,128)(2,1)S(1)}, bf16[64,1024]{1,0:T(8,128)(2,1)S(1)}, u32[]{:S(2)}, u32[]{:S(2)}) collective-permute-start(bf16[64,1024]{1,0:T(8,128)(2,1)S(1)} %collective-permute-done.13), channel_id=1, source_target_pairs={{0,64},{64,128},{128,192},{192,256},{256,320},{320,384},{384,448},... | collective-permute-start | bytes 393224 | tf_op jit(solution)/shard_map/ppermute | solution.py:128
  145.2 6.7 %collective-permute-start.16 = (bf16[64,512]{1,0:T(8,128)(2,1)S(1)}, bf16[64,512]{1,0:T(8,128)(2,1)S(1)}, u32[]{:S(2)}, u32[]{:S(2)}) collective-permute-start(bf16[64,512]{1,0:T(8,128)(2,1)S(1)} %slice.42), channel_id=1, source_target_pairs={{0,448},{64,0},{128,64},{192,128},{256,192},{320,256},{384,320},{4... | collective-permute-start | bytes 196616 | tf_op jit(solution)/shard_map/ppermute | solution.py:130
  150.0 6.6 %collective-permute-start.15 = (bf16[64,512]{1,0:T(8,128)(2,1)S(1)}, bf16[64,512]{1,0:T(8,128)(2,1)S(1)}, u32[]{:S(2)}, u32[]{:S(2)}) collective-permute-start(bf16[64,512]{1,0:T(8,128)(2,1)S(1)} %slice.41), channel_id=1, source_target_pairs={{0,64},{64,128},{128,192},{192,256},{256,320},{320,384},{384,448},... | collective-permute-start | bytes 196616 | tf_op jit(solution)/shard_map/ppermute | solution.py:130
  156.7 10.6 %collective-permute-start.17 = (bf16[8,64,1024]{2,1,0:T(8,128)(2,1)S(1)}, bf16[8,64,1024]{2,1,0:T(8,128)(2,1)}, u32[]{:S(2)}, u32[]{:S(2)}) collective-permute-start(bf16[8,64,1024]{2,1,0:T(8,128)(2,1)S(1)} %bitcast_dynamic-update-slice_fusion.own_ref), channel_id=1, source_target_pairs={{0,32},{32,0},{1,33},{33,1},{2,34},{34,2},{3,35},{35,3},{4,36},{36... | collective-permute-start | bytes 3145736 | tf_op jit(solution)/shard_map/ppermute | solution.py:190
  167.3 1.1 copy-start.4
  173.9 1.4 copy-start.11
  175.3 8.4 %copy-start.14 = (bf16[1024,384]{1,0:T(8,128)(2,1)S(1)}, bf16[1024,384]{1,0:T(8,128)(2,1)}, u32[]{:S(2)}) copy-start(bf16[1024,384]{1,0:T(8,128)(2,1)} %copy-done.13) | copy-start | bytes 2359300
  175.3 25.7 %all-to-all-start.2 = ((bf16[32,32,384]{2,1,0:T(8,128)(2,1)}), bf16[32,32,384]{2,1,0:T(8,128)(2,1)S(1)}, u32[]{:S(2)}, u32[]{:S(2)}) async-start(bf16[32,32,384]{2,1,0:T(8,128)(2,1)} %bitcast.18), calls=%async_computation.2 | async-start | bytes 1572864 | tf_op jit(solution)/shard_map/all_to_all | solution.py:150
  183.7 2.1 %copy-start.16 = (bf16[1024,512]{1,0:T(8,128)(2,1)S(1)}, bf16[1024,512]{1,0:T(8,128)(2,1)}, u32[]{:S(2)}) copy-start(bf16[1024,512]{1,0:T(8,128)(2,1)} %all-gather.2.cloned.1.call-done) | copy-start | bytes 3145732
  185.8 1.8 copy-start.12
  185.8 1.8 copy-start.15
Sparse Core Ops, SparseCore 0:
  132.3 36.2 all-gather.1

commit v3 on v1

v3 whole, which is shorter than its diff:
```python
import functools

import jax
import jax.numpy as jnp
from jax import lax
from jax.experimental import pallas as pl
from jax.experimental.pallas import tpu as pltpu
from jax.sharding import Mesh
from jax.sharding import PartitionSpec as P

BF = jnp.bfloat16
F32 = jnp.float32
ROWS = 256
CUT = 256
VMEM_BYTES = 20 * 2**20


def dot(a, b, ca, cb):
    return lax.dot_general(a, b, (((ca,), (cb,)), ((), ())), preferred_element_type=F32)


def activate(gate_pre, up_pre, down_grad):
    sigmoid_val = jax.nn.sigmoid(gate_pre)
    swish_val = gate_pre * sigmoid_val
    hidden = (swish_val * up_pre).astype(BF)
    slope_val = sigmoid_val * (1.0 + gate_pre * (1.0 - sigmoid_val))
    gate_grad = (down_grad * up_pre * slope_val).astype(BF)
    up_grad = (down_grad * swish_val).astype(BF)
    return hidden, gate_grad, up_grad


def call(body, outs, flops, args):
    in_specs = [
        pl.BlockSpec(memory_space=pltpu.SMEM if a.ndim == 1 else pltpu.VMEM) for a in args
    ]
    moved = sum(a.size * a.dtype.itemsize for a in (*args, *outs))
    return pl.pallas_call(
        body,
        out_shape=outs,
        in_specs=in_specs,
        out_specs=[pl.BlockSpec(memory_space=pltpu.VMEM) for _ in outs],
        compiler_params=pltpu.CompilerParams(vmem_limit_bytes=VMEM_BYTES),
        cost_estimate=pl.CostEstimate(flops=flops, bytes_accessed=moved, transcendentals=0),
    )(*args)


def by_expert(rows, expert, experts):
    return [jnp.where(expert == e, rows, jnp.zeros_like(rows)) for e in range(experts)]


def forward_body(lo, hi, core_ref, expert_ref, got_ref, wg_ref, wu_ref, wd_ref, keep_ref, give_ref):
    n_y, part, _ = keep_ref.shape
    experts = wg_ref.shape[0]
    _, _, own, cols = got_ref.shape
    width = hi - lo
    core = core_ref[0]
    pairs = ROWS // (2 * part)
    owners = ROWS // own

    @pl.loop(0, n_y // pairs)
    def _(i):
        expert = expert_ref[pl.ds(pl.multiple_of(i * ROWS, ROWS), ROWS), :]
        src = pl.ds(i * owners, owners)
        toks = by_expert(got_ref[src, 0].reshape(ROWS, cols), expert, experts)
        cots = by_expert(got_ref[src, 1].reshape(ROWS, cols), expert, experts)
        for k in range(3):
            out = 0.0
            for e in range(experts):
                if k < 2:
                    out = out + dot(toks[e], (wg_ref, wu_ref)[k][e, :, lo:hi], 1, 0)
                else:
                    out = out + dot(cots[e], wd_ref[e, lo:hi, :], 1, 1)
            to = slice(k * width, (k + 1) * width)
            for j in range(pairs):
                even = out[2 * j * part : (2 * j + 1) * part]
                odd = out[(2 * j + 1) * part : (2 * j + 2) * part]
                keep_ref[i * pairs + j, :, to] = jnp.where(core == 0, even, odd)
                give_ref[i * pairs + j, :, to] = jnp.where(core == 0, odd, even).astype(BF)


def terms(rows, expert, gate_ref, up_ref, lo, hi):
    experts, width = gate_ref.shape[0], hi - lo
    gates = by_expert(rows[:, :width], expert, experts)
    ups = by_expert(rows[:, width : 2 * width], expert, experts)
    out = 0.0
    for e in range(experts):
        out = out + dot(gates[e], gate_ref[e, :, lo:hi], 1, 1)
        out = out + dot(ups[e], up_ref[e, :, lo:hi], 1, 1)
    return out


def head_body(lo, hi, expert_ref, gate_ref, up_ref, grads_ref, out_ref):
    @pl.loop(0, out_ref.shape[0] // ROWS)
    def _(i):
        at = pl.ds(pl.multiple_of(i * ROWS, ROWS), ROWS)
        out_ref[at, :] = terms(grads_ref[at, :], expert_ref[at, :], gate_ref, up_ref, lo, hi)


def tail_body(lo, hi, core_ref, expert_ref, gate_ref, up_ref, head_ref, own_ref, other_ref, grads_ref, out_ref):
    n_y, n_core, part, width = grads_ref.shape
    core = core_ref[0]
    for i in range(n_y):
        grads_ref[i, core] = own_ref[i]
        grads_ref[i, 1 - core] = other_ref[i]
    per_y = n_core * part

    @pl.loop(0, out_ref.shape[0] // ROWS)
    def _(i):
        at = pl.ds(pl.multiple_of(i * ROWS, ROWS), ROWS)
        rows = grads_ref[pl.ds(i * (ROWS // per_y), ROWS // per_y)].reshape(ROWS, width)
        out = head_ref[at, :] + terms(rows, expert_ref[at, :], gate_ref, up_ref, lo, hi)
        out_ref[at, :] = out.astype(BF)


def total_body(x_ref, out_ref):
    out = x_ref[0].astype(F32)
    for i in range(1, x_ref.shape[0]):
        out = out + x_ref[i].astype(F32)
    out_ref[...] = out.astype(BF)


def make(n_y, n_core, n_x, n_z):
    dp, cuts = ("y", "core"), ("x", "z")
    n_dp, n_cuts = n_y * n_core, n_x * n_z
    swap = [(i, n_core - 1 - i) for i in range(n_core)]

    def per_device(tokens, cotangent, w_gate, w_up, w_down, row_token, block_expert, gate_weight):
        own, cols = tokens.shape
        n_tok = row_token.shape[0]
        experts, _, hid = w_gate.shape
        blk = n_tok // block_expert.shape[0]
        part = n_tok // n_dp
        core = lax.axis_index("core").astype(jnp.int32).reshape(1)
        work = 2 * n_tok * experts * cols

        def exchange(v, axes):
            return lax.all_to_all(v, axes, split_axis=0, concat_axis=0, tiled=True)

        def spread(v, n):
            return jnp.broadcast_to(v[None], (n,) + v.shape)

        first = (lax.axis_index("x") * n_z + lax.axis_index("z")) * own
        holds_own = row_token[None, :] == first + jnp.arange(own, dtype=jnp.int32)[:, None]
        weight_own = jnp.sum(jnp.where(holds_own, gate_weight[None, :], 0.0), axis=1)
        expert_row = jnp.repeat(block_expert[:, 0], blk)
        holds = row_token[None, :] == jnp.arange(n_tok, dtype=jnp.int32)[:, None]
        expert_tok = jnp.sum(jnp.where(holds, expert_row[None, :], 0), axis=1)[:, None]

        cot_own = (cotangent.astype(F32) * weight_own[:, None]).astype(BF)
        got = exchange(spread(jnp.stack([tokens, cot_own]), n_cuts), cuts)

        def partial(lo, hi):
            shape = (n_y, part, 3 * (hi - lo))
            outs = [jax.ShapeDtypeStruct(shape, F32), jax.ShapeDtypeStruct(shape, BF)]
            args = (core, expert_tok, got, w_gate, w_up, w_down)
            keep, give = call(functools.partial(forward_body, lo, hi), outs, work * 3 * (hi - lo), args)
            came = lax.ppermute(give, "core", swap)
            return (keep + came.astype(F32)).astype(BF)

        def total(chip):
            pre = jnp.sum(exchange(chip, "y").astype(F32), axis=0)
            width = pre.shape[1] // 3
            hidden, gate_grad, up_grad = activate(
                pre[:, :width], pre[:, width : 2 * width], pre[:, 2 * width :]
            )
            return jnp.concatenate([gate_grad, up_grad, hidden], axis=1)

        chip_a, chip_b = partial(0, CUT), partial(CUT, hid)
        act_a = lax.all_gather(total(chip_a), dp, axis=0, tiled=True)
        act_b = exchange(spread(total(chip_b), n_y), "y")
        act_o = lax.ppermute(act_b, "core", swap)

        outs = [jax.ShapeDtypeStruct((n_tok, cols), F32)]
        args = (expert_tok, w_gate, w_up, act_a)
        (terms_a,) = call(functools.partial(head_body, 0, CUT), outs, 2 * work * CUT, args)
        outs = [
            jax.ShapeDtypeStruct((n_y, n_core, part, act_b.shape[2]), BF),
            jax.ShapeDtypeStruct((n_tok, cols), BF),
        ]
        args = (core, expert_tok, w_gate, w_up, terms_a, act_b, act_o)
        body = functools.partial(tail_body, CUT, hid)
        act_b, both = call(body, outs, 2 * work * (hid - CUT), args)
        act_b = act_b.reshape(n_tok, -1)
        both = exchange(both.reshape(n_cuts, own, cols), cuts)
        outs = [jax.ShapeDtypeStruct((own, cols), BF)]
        (token_grad,) = call(total_body, outs, both.size, (both,))

        def joined(k):
            rest = hid - CUT
            halves = [act_a[:, k * CUT : (k + 1) * CUT], act_b[:, k * rest : (k + 1) * rest]]
            return jnp.concatenate(halves, axis=1)

        tok, cot = got[:, 0].reshape(n_tok, cols), got[:, 1].reshape(n_tok, cols)
        masks = [expert_tok == e for e in range(experts)]
        tok_by = jnp.concatenate([jnp.where(m, tok, 0) for m in masks], axis=1)
        grad_gate = dot(tok_by, joined(0), 0, 0).astype(BF).reshape(w_gate.shape)
        grad_up = dot(tok_by, joined(1), 0, 0).astype(BF).reshape(w_up.shape)
        hidden = joined(2)
        grad_down = [dot(hidden, jnp.where(m, cot, 0), 0, 0).astype(BF) for m in masks]
        return token_grad, grad_gate, grad_up, jnp.stack(grad_down)

    return per_device


def solution(mesh):
    n_y, n_core, n_x, n_z = 8, 2, 4, 8
    fine = Mesh(mesh.devices.reshape(n_y, n_core, n_x, n_z), ("y", "core", "x", "z"))
    dp, cuts = ("y", "core"), ("x", "z")
    return jax.shard_map(
        make(n_y, n_core, n_x, n_z),
        mesh=fine,
        in_specs=(
            P(cuts, dp),
            P(cuts, dp),
            P(None, dp, cuts),
            P(None, dp, cuts),
            P(None, cuts, dp),
            P(),
            P(),
            P(),
        ),
        out_specs=(P(cuts, dp), P(None, dp, cuts), P(None, dp, cuts), P(None, cuts, dp)),
        check_vma=False,
    )
```

time: 225 us -> 213 us (0.947)
  waiting for transfers between devices: 124 us -> 86.5 us
  blocking collectives: 0 us -> 28.6 us
  starting transfers between devices: 52.6 us -> 41 us
  local copies, waits for them, and re-layouts: 7.33 us -> 12.4 us
  Pallas kernels: 9.77 us -> 12.4 us
    all_gather x2 -> x1, waiting for transfers between devices: 69.4 us -> 0.01 us  [per_device(): act_a = lax.all_gather(total(chip_a), dp, axis=0, tiled=True)]
    all_to_all x5 -> x4, waiting for transfers between devices: 50.1 us -> 82.7 us  [exchange(): return lax.all_to_all(v, axes, split_axis=0, concat_axis=0, tiled=True)]
    all_to_all x0 -> x1, blocking collectives: none -> 28.6 us  [exchange(): return lax.all_to_all(v, axes, split_axis=0, concat_axis=0, tiled=True)]
    all_to_all x5 -> x4, starting transfers between devices: 42.4 us -> 30.1 us  [exchange(): return lax.all_to_all(v, axes, split_axis=0, concat_axis=0, tiled=True)]
    unnamed x28, local copies, waits for them, and re-layouts: 4.38 us -> 9.13 us
    pallas_call x4 -> x5, Pallas kernels: 9.77 us -> 12.4 us  [call(): pl.pallas_call(body, out_shape=outs, in_specs=in_specs, out_specs=[pl.Blo...]
    ppermute x2 -> x3, starting transfers between devices: 10 us -> 10.9 us  [the longest x2 7.94 us: partial(): came = lax.ppermute(give, 'core', swap)]
  transfers between devices with their start and end apart: 9 -> 8, of which waited for: 8 -> 6; matrix products, arithmetic and copies ran while one was open for 7% -> 7% of each run, Pallas kernels for 4% -> 2%
where the time goes in v3:
time: 213 us; the launch traced here: 211 us
  waiting for transfers between devices  86.5 us (41%)
  starting transfers between devices  41 us (19%)
  blocking collectives  28.6 us (13%)
  between operations  14.3 us (7%)
  local copies, waits for them, and re-layouts  12.4 us (6%)
  Pallas kernels  12.4 us (6%)
  other arithmetic  10.4 us (5%)
  matrix products  5.25 us (2%)
    all_to_all x4, waiting for transfers between devices, exchange(): return lax.all_to_all(v, axes, split_axis=0, concat_axis=0, tiled=True)  82.7 us
    all_to_all x4, starting transfers between devices, exchange(): return lax.all_to_all(v, axes, split_axis=0, concat_axis=0, tiled=True)  30.1 us
    all_to_all x1, blocking collectives, exchange(): return lax.all_to_all(v, axes, split_axis=0, concat_axis=0, tiled=True)  28.6 us
    pallas_call x5, Pallas kernels, call(): pl.pallas_call(body, out_shape=outs, in_specs=in_specs, out_specs=[pl.Blo...  12.4 us
    unnamed x28, local copies, waits for them, and re-layouts  9.13 us
    ppermute x2, starting transfers between devices, partial(): came = lax.ppermute(give, 'core', swap)  7.94 us
    dot_general x4, matrix products, dot(): lax.dot_general(a, b, (((ca,), (cb,)), ((), ())), preferred_element_type=...  5.25 us
  transfers between devices with their start and end apart: 8, of which 6 were waited for; matrix products, arithmetic and copies ran while one was open for 7% of the time, Pallas kernels for 2%

profile of v3, /device:TPU:1, one launch (start us, length us, event | category | flops | bytes accessed | tf_op | source)
XLA Modules:
  0.0 210.9 jit_solution(7476270788222841301)
XLA Ops:
  7.2 0.0 copy-start
  7.2 0.9 select_reduce_fusion.1
  8.1 0.8 fusion.10
  8.9 0.7 pad_maximum_fusion.9
  9.7 1.4 broadcast_in_dim.83
  11.1 0.0 copy-start.13
  11.1 0.0 copy-start.3
  11.1 13.8 %all-to-all-start = ((bf16[32,2,32,384]{3,2,1,0:T(8,128)(2,1)}), bf16[32,2,32,384]{3,2,1,0:T(8,128)(2,1)S(1)}, u32[]{:S(2)}, u32[]{:S(2)}) async-start(bf16[32,2,32,384]{3,2,1,0:T(8,128)(2,1)} %broadcast_in_dim.83), calls=%async_computation | async-start | bytes 3145728 | tf_op jit(solution)/shard_map/all_to_all | solution.py:137
  24.9 0.0 copy-done
  24.9 0.1 broadcast_bitcast_fusion
  25.0 0.0 copy-done.13
  25.0 0.5 select_reduce_fusion
  25.5 0.2 copy.19.expert_ref
  25.7 36.0 %all-to-all-done.got_ref = bf16[32,2,32,384]{3,2,1,0:T(8,128)(2,1)S(1)} async-done(((bf16[32,2,32,384]{3,2,1,0:T(8,128)(2,1)}), bf16[32,2,32,384]{3,2,1,0:T(8,128)(2,1)S(1)}, u32[]{:S(2)}, u32[]{:S(2)}) %all-to-all-start) | async-done | bytes 1572896 | tf_op jit(solution)/shard_map/all_to_all | solution.py:137
  61.7 0.0 copy-done.3
  61.7 0.0 copy-start.4
  61.7 1.1 copy-done.4
  62.9 0.0 copy-start.9
  62.9 1.1 copy-done.9
  64.0 2.7 %shard_map.111 = (f32[8,64,768]{2,1,0:T(8,128)S(1)}, bf16[8,64,768]{2,1,0:T(8,128)(2,1)S(1)}) custom-call(s32[1]{0:T(128)} %bitcast.core_ref, s32[1024,1]{1,0:T(8,128)S(1)} %copy.19.expert_ref, bf16[32,2,32,384]{3,2,1,0:T(8,128)(2,1)S(1)} %all-to-all-done.got_ref, bf16[2,384,512]{2,1,0:T(8,128)(2,1)S(1)} %copy-done.3, bf16[2,384,512]{2,1,0:T(8,128)(2,1)S(1)} %copy-done.4, ...), custom_call_target="tpu_custom_call" | custom-call | flops 1207959552 | bytes 6295556 | tf_op jit(solution)/shard_map/pallas_call | solution.py:37
  66.7 5.4 %collective-permute-start = (bf16[8,64,768]{2,1,0:T(8,128)(2,1)S(1)}, bf16[8,64,768]{2,1,0:T(8,128)(2,1)S(1)}, u32[]{:S(2)}, u32[]{:S(2)}) collective-permute-start(bf16[8,64,768]{2,1,0:T(8,128)(2,1)S(1)} %get-tuple-element.11), channel_id=1, source_target_pairs={{0,32},{32,0},{1,33},{33,1},{2,34},{34,2},{3,35},{35,3},{4,36},{36... | collective-permute-start | bytes 2359304 | tf_op jit(solution)/shard_map/ppermute | solution.py:157
  72.1 1.9 collective-permute-done
  74.0 1.1 add_convert_fusion.1
  75.1 6.8 %all-to-all-start.1 = ((bf16[8,64,768]{2,1,0:T(8,128)(2,1)}), bf16[8,64,768]{2,1,0:T(8,128)(2,1)}, u32[]{:S(2)}, u32[]{:S(2)}) async-start(bf16[8,64,768]{2,1,0:T(8,128)(2,1)} %add_convert_fusion.1), calls=%async_computation.1 | async-start | bytes 1572864 | tf_op jit(solution)/shard_map/all_to_all | solution.py:137
  81.9 1.1 copy-done.5
  83.1 1.1 copy-done.10
  84.2 2.7 %shard_map.113 = (f32[8,64,768]{2,1,0:T(8,128)S(1)}, bf16[8,64,768]{2,1,0:T(8,128)(2,1)S(1)}) custom-call(s32[1]{0:T(128)} %bitcast.core_ref, s32[1024,1]{1,0:T(8,128)S(1)} %copy.19.expert_ref, bf16[32,2,32,384]{3,2,1,0:T(8,128)(2,1)S(1)} %all-to-all-done.got_ref, bf16[2,384,512]{2,1,0:T(8,128)(2,1)S(1)} %copy-done.3, bf16[2,384,512]{2,1,0:T(8,128)(2,1)S(1)} %copy-done.5, ...), custom_call_target="tpu_custom_call" | custom-call | flops 1207959552 | bytes 6295556 | tf_op jit(solution)/shard_map/pallas_call | solution.py:37
  86.9 2.6 %collective-permute-start.1 = (bf16[8,64,768]{2,1,0:T(8,128)(2,1)S(1)}, bf16[8,64,768]{2,1,0:T(8,128)(2,1)S(1)}, u32[]{:S(2)}, u32[]{:S(2)}) collective-permute-start(bf16[8,64,768]{2,1,0:T(8,128)(2,1)S(1)} %get-tuple-element.13), channel_id=1, source_target_pairs={{0,32},{32,0},{1,33},{33,1},{2,34},{34,2},{3,35},{35,3},{4,36},{36... | collective-permute-start | bytes 2359304 | tf_op jit(solution)/shard_map/ppermute | solution.py:157
  89.4 1.9 collective-permute-done.1
  91.3 1.1 add_convert_fusion
  92.4 13.2 %all-to-all-done.1 = bf16[8,64,768]{2,1,0:T(8,128)(2,1)} async-done(((bf16[8,64,768]{2,1,0:T(8,128)(2,1)}), bf16[8,64,768]{2,1,0:T(8,128)(2,1)}, u32[]{:S(2)}, u32[]{:S(2)}) %all-to-all-start.1) | async-done | bytes 786464 | tf_op jit(solution)/shard_map/all_to_all | solution.py:137
  105.6 4.2 %all-to-all-start.2 = ((bf16[8,64,768]{2,1,0:T(8,128)(2,1)}), bf16[8,64,768]{2,1,0:T(8,128)(2,1)}, u32[]{:S(2)}, u32[]{:S(2)}) async-start(bf16[8,64,768]{2,1,0:T(8,128)(2,1)} %add_convert_fusion), calls=%async_computation.2 | async-start | bytes 1572864 | tf_op jit(solution)/shard_map/all_to_all | solution.py:137
  109.8 0.0 all-gather.2.cloned.1.call-start
  109.9 1.3 convert_reduce_fusion.1
  111.2 0.6 pad_maximum_fusion.7
  111.8 0.0 all-gather.2.cloned.1.call-update
  111.9 21.5 %all-to-all-done.2 = bf16[8,64,768]{2,1,0:T(8,128)(2,1)} async-done(((bf16[8,64,768]{2,1,0:T(8,128)(2,1)}), bf16[8,64,768]{2,1,0:T(8,128)(2,1)}, u32[]{:S(2)}, u32[]{:S(2)}) %all-to-all-start.2) | async-done | bytes 786464 | tf_op jit(solution)/shard_map/all_to_all | solution.py:137
  133.4 1.3 convert_reduce_fusion
  134.7 0.1 broadcast_in_dim.84
  134.8 28.6 %all_to_all.25.own_ref = bf16[8,64,768]{2,1,0:T(8,128)(2,1)} all-to-all(bf16[8,64,768]{2,1,0:T(8,128)(2,1)S(1)} %broadcast_in_dim.84), channel_id=1, replica_groups=mesh['y'=8,'core'=2,'x'=4,'z'=8] {'y'}, dimensions={0} | all-to-all | bytes 1572864 | tf_op jit(solution)/shard_map/all_to_all | solution.py:137
  163.4 2.9 %collective-permute-start.2 = (bf16[8,64,768]{2,1,0:T(8,128)(2,1)}, bf16[8,64,768]{2,1,0:T(8,128)(2,1)}, u32[]{:S(2)}, u32[]{:S(2)}) collective-permute-start(bf16[8,64,768]{2,1,0:T(8,128)(2,1)} %all_to_all.25.own_ref), channel_id=1, source_target_pairs={{0,32},{32,0},{1,33},{33,1},{2,34},{34,2},{3,35},{35,3},{4,36},{36... | collective-permute-start | bytes 2359304 | tf_op jit(solution)/shard_map/ppermute | solution.py:171
  166.4 1.3 fusion.17
  167.7 1.4 copy-done.1
  169.1 1.1 copy-done.6
  170.2 1.9 shard_map.112.head_ref
  172.2 0.0 collective-permute-done.2.other_ref
  172.2 4.3 %shard_map.114 = (bf16[8,2,64,768]{3,2,1,0:T(8,128)(2,1)S(1)}, bf16[1024,384]{1,0:T(8,128)(2,1)}) custom-call(s32[1]{0:T(128)} %bitcast.core_ref, s32[1024,1]{1,0:T(8,128)S(1)} %copy.19.expert_ref, bf16[2,384,512]{2,1,0:T(8,128)(2,1)S(1)} %copy-done.3, bf16[2,384,512]{2,1,0:T(8,128)(2,1)S(1)} %copy-done.6, f32[1024,384]{1,0:T(8,128)S(1)} %shard_map.112.head_ref, ...), custom_call_target="tpu_custom_call" | custom-call | flops 805306368 | bytes 7081988 | tf_op jit(solution)/shard_map/pallas_call | solution.py:37
  176.5 1.1 copy-done.7
  177.7 5.3 %all-to-all-start.4 = ((bf16[32,32,384]{2,1,0:T(8,128)(2,1)}), bf16[32,32,384]{2,1,0:T(8,128)(2,1)S(1)}, u32[]{:S(2)}, u32[]{:S(2)}) async-start(bf16[32,32,384]{2,1,0:T(8,128)(2,1)} %bitcast.6), calls=%async_computation.4 | async-start | bytes 1572864 | tf_op jit(solution)/shard_map/all_to_all | solution.py:137
  182.9 0.0 copy-done.11
  183.0 0.0 copy-done.12
  183.0 0.0 copy-start.2
  183.0 0.0 copy-start.8
  183.0 1.0 bitcast_select_fusion.3
  184.0 0.4 copy-done.2
  184.4 0.5 copy-done.8
  184.8 0.2 fusion.15
  185.1 0.7 fusion
  185.8 0.7 fusion.1
  186.5 1.0 pad_maximum_fusion.4
  187.5 1.9 convolution_convert_fusion
  189.4 1.9 convolution_convert_fusion.1
  191.3 12.0 %all-to-all-done.4.x_ref = bf16[32,32,384]{2,1,0:T(8,128)(2,1)S(1)} async-done(((bf16[32,32,384]{2,1,0:T(8,128)(2,1)}), bf16[32,32,384]{2,1,0:T(8,128)(2,1)S(1)}, u32[]{:S(2)}, u32[]{:S(2)}) %all-to-all-start.4) | async-done | bytes 786464 | tf_op jit(solution)/shard_map/all_to_all | solution.py:137
  203.3 0.7 shard_map.115
  (13 shorter events, 0.1 us)
Async XLA Ops:
  7.2 17.8 %copy-start = (s32[8,1]{0,1:T(1,128)S(1)}, s32[8,1]{0,1:T(1,128)}, u32[]{:S(2)}) copy-start(s32[8,1]{0,1:T(1,128)} %param.14) | copy-start | bytes 100
  11.1 13.9 %copy-start.13 = (s32[1024]{0:T(1024)S(1)}, s32[1024]{0:T(1024)}, u32[]{:S(2)}) copy-start(s32[1024]{0:T(1024)} %param.13) | copy-start | bytes 12292
  11.1 50.7 %copy-start.3 = (bf16[2,384,512]{2,1,0:T(8,128)(2,1)S(1)}, bf16[2,384,512]{2,1,0:T(8,128)(2,1)}, u32[]{:S(2)}) copy-start(bf16[2,384,512]{2,1,0:T(8,128)(2,1)} %gate_ref.3) | copy-start | bytes 2359300
  11.1 50.7 %all-to-all-start = ((bf16[32,2,32,384]{3,2,1,0:T(8,128)(2,1)}), bf16[32,2,32,384]{3,2,1,0:T(8,128)(2,1)S(1)}, u32[]{:S(2)}, u32[]{:S(2)}) async-start(bf16[32,2,32,384]{3,2,1,0:T(8,128)(2,1)} %broadcast_in_dim.83), calls=%async_computation | async-start | bytes 3145728 | tf_op jit(solution)/shard_map/all_to_all | solution.py:137
  61.7 1.1 copy-start.4
  62.9 1.1 copy-start.9
  66.7 7.3 %collective-permute-start = (bf16[8,64,768]{2,1,0:T(8,128)(2,1)S(1)}, bf16[8,64,768]{2,1,0:T(8,128)(2,1)S(1)}, u32[]{:S(2)}, u32[]{:S(2)}) collective-permute-start(bf16[8,64,768]{2,1,0:T(8,128)(2,1)S(1)} %get-tuple-element.11), channel_id=1, source_target_pairs={{0,32},{32,0},{1,33},{33,1},{2,34},{34,2},{3,35},{35,3},{4,36},{36... | collective-permute-start | bytes 2359304 | tf_op jit(solution)/shard_map/ppermute | solution.py:157
  75.1 30.5 %all-to-all-start.1 = ((bf16[8,64,768]{2,1,0:T(8,128)(2,1)}), bf16[8,64,768]{2,1,0:T(8,128)(2,1)}, u32[]{:S(2)}, u32[]{:S(2)}) async-start(bf16[8,64,768]{2,1,0:T(8,128)(2,1)} %add_convert_fusion.1), calls=%async_computation.1 | async-start | bytes 1572864 | tf_op jit(solution)/shard_map/all_to_all | solution.py:137
  81.9 1.1 copy-start.5
  83.1 1.1 copy-start.10
  86.9 4.5 %collective-permute-start.1 = (bf16[8,64,768]{2,1,0:T(8,128)(2,1)S(1)}, bf16[8,64,768]{2,1,0:T(8,128)(2,1)S(1)}, u32[]{:S(2)}, u32[]{:S(2)}) collective-permute-start(bf16[8,64,768]{2,1,0:T(8,128)(2,1)S(1)} %get-tuple-element.13), channel_id=1, source_target_pairs={{0,32},{32,0},{1,33},{33,1},{2,34},{34,2},{3,35},{35,3},{4,36},{36... | collective-permute-start | bytes 2359304 | tf_op jit(solution)/shard_map/ppermute | solution.py:157
  105.6 27.8 %all-to-all-start.2 = ((bf16[8,64,768]{2,1,0:T(8,128)(2,1)}), bf16[8,64,768]{2,1,0:T(8,128)(2,1)}, u32[]{:S(2)}, u32[]{:S(2)}) async-start(bf16[8,64,768]{2,1,0:T(8,128)(2,1)} %add_convert_fusion), calls=%async_computation.2 | async-start | bytes 1572864 | tf_op jit(solution)/shard_map/all_to_all | solution.py:137
  109.8 57.9 %all-gather.2.cloned.1.call-start = ((), (), s32[]{:S(2)}) async-start(), calls=%async_computation.5 | async-start | bytes 1671168 | tf_op jit(solution)/shard_map/all_gather | solution.py:169
  163.4 8.7 %collective-permute-start.2 = (bf16[8,64,768]{2,1,0:T(8,128)(2,1)}, bf16[8,64,768]{2,1,0:T(8,128)(2,1)}, u32[]{:S(2)}, u32[]{:S(2)}) collective-permute-start(bf16[8,64,768]{2,1,0:T(8,128)(2,1)} %all_to_all.25.own_ref), channel_id=1, source_target_pairs={{0,32},{32,0},{1,33},{33,1},{2,34},{34,2},{3,35},{35,3},{4,36},{36... | collective-permute-start | bytes 2359304 | tf_op jit(solution)/shard_map/ppermute | solution.py:171
  167.7 1.4 copy-start.1
  169.1 1.1 copy-start.6
  176.5 1.1 copy-start.7
  177.7 5.3 %copy-start.11 = (bf16[32,1,32,384]{3,2,1,0:T(8,128)(2,1)S(1)}, bf16[32,1,32,384]{3,2,1,0:T(8,128)(2,1)}, u32[]{:S(2)}) copy-start(bf16[32,1,32,384]{3,2,1,0:T(8,128)(2,1)} %get-tuple-element.22) | copy-start | bytes 2359300
  177.7 5.3 %copy-start.12 = (bf16[32,1,32,384]{3,2,1,0:T(8,128)(2,1)S(1)}, bf16[32,1,32,384]{3,2,1,0:T(8,128)(2,1)}, u32[]{:S(2)}) copy-start(bf16[32,1,32,384]{3,2,1,0:T(8,128)(2,1)} %get-tuple-element.23) | copy-start | bytes 2359300
  177.7 25.6 %all-to-all-start.4 = ((bf16[32,32,384]{2,1,0:T(8,128)(2,1)}), bf16[32,32,384]{2,1,0:T(8,128)(2,1)S(1)}, u32[]{:S(2)}, u32[]{:S(2)}) async-start(bf16[32,32,384]{2,1,0:T(8,128)(2,1)} %bitcast.6), calls=%async_computation.4 | async-start | bytes 1572864 | tf_op jit(solution)/shard_map/all_to_all | solution.py:137
  183.0 1.4 copy-start.2
  183.0 1.9 copy-start.8
Sparse Core Ops, SparseCore 0:
  113.4 43.8 all-gather.1

commit v4 on v1

v4 whole, which is shorter than its diff:
```python
import functools

import jax
import jax.numpy as jnp
from jax import lax
from jax.experimental import pallas as pl
from jax.experimental.pallas import tpu as pltpu
from jax.sharding import Mesh
from jax.sharding import PartitionSpec as P

BF = jnp.bfloat16
F32 = jnp.float32
ROWS = 256
VMEM_BYTES = 20 * 2**20


def dot(a, b, ca, cb):
    return lax.dot_general(a, b, (((ca,), (cb,)), ((), ())), preferred_element_type=F32)


def activate(gate_pre, up_pre, down_grad):
    sigmoid_val = jax.nn.sigmoid(gate_pre)
    swish_val = gate_pre * sigmoid_val
    hidden = (swish_val * up_pre).astype(BF)
    slope_val = sigmoid_val * (1.0 + gate_pre * (1.0 - sigmoid_val))
    gate_grad = (down_grad * up_pre * slope_val).astype(BF)
    up_grad = (down_grad * swish_val).astype(BF)
    return hidden, gate_grad, up_grad


def call(body, outs, flops, args):
    spaces = [pltpu.SMEM if a.ndim == 1 else pltpu.VMEM for a in args]
    in_specs = [pl.BlockSpec(memory_space=space) for space in spaces]
    moved = sum(a.size * a.dtype.itemsize for a in (*args, *outs))
    return pl.pallas_call(
        body,
        out_shape=outs,
        in_specs=in_specs,
        out_specs=[pl.BlockSpec(memory_space=pltpu.VMEM) for _ in outs],
        compiler_params=pltpu.CompilerParams(vmem_limit_bytes=VMEM_BYTES),
        cost_estimate=pl.CostEstimate(flops=flops, bytes_accessed=moved, transcendentals=0),
    )(*args)


def by_expert(rows, expert, experts):
    return [jnp.where(expert == e, rows, jnp.zeros_like(rows)) for e in range(experts)]


def forward_body(at_ref, expert_ref, got_ref, wg_ref, wu_ref, wd_ref, keep_ref, give_ref):
    _, n_yh, part, width = keep_ref.shape
    experts = wg_ref.shape[0]
    _, _, own, cols = got_ref.shape
    hid = width // 3
    parity, core = at_ref[0], at_ref[1]
    owners = ROWS // own
    for k, w_ref in enumerate((wg_ref, wu_ref, wd_ref)):
        side, cb = k // 2, k // 2
        to = slice(k * hid, (k + 1) * hid)

        @pl.loop(0, n_yh)
        def _(i):
            expert = expert_ref[pl.ds(pl.multiple_of(i * ROWS, ROWS), ROWS), :]
            rows = got_ref[pl.ds(i * owners, owners), side].reshape(ROWS, cols)
            out = 0.0
            for e, x in enumerate(by_expert(rows, expert, experts)):
                out = out + dot(x, w_ref[e], 1, cb)
            for p in range(2):
                even = out[2 * p * part : (2 * p + 1) * part]
                odd = out[(2 * p + 1) * part : (2 * p + 2) * part]
                slot = lax.rem(parity + p, 2)
                keep_ref[slot, i, :, to] = jnp.where(core == 0, even, odd)
                give_ref[slot, i, :, to] = jnp.where(core == 0, odd, even).astype(BF)


def terms_body(at_ref, expert_ref, gate_ref, up_ref, mine_ref, other_ref, grads_ref, out_ref):
    n_yh, n_yl, n_core, part, width = grads_ref.shape
    experts, _, hid = gate_ref.shape
    parity, core = at_ref[0], at_ref[1]

    @pl.loop(0, n_yh)
    def _(i):
        for p in range(n_yl):
            grads_ref[i, lax.rem(parity + p, 2), core] = mine_ref[p, i]
            grads_ref[i, lax.rem(parity + p, 2), 1 - core] = other_ref[p, i]
        at = pl.ds(pl.multiple_of(i * ROWS, ROWS), ROWS)
        expert = expert_ref[at, :]
        rows = grads_ref[i].reshape(ROWS, width)
        gates = by_expert(rows[:, :hid], expert, experts)
        ups = by_expert(rows[:, hid:], expert, experts)
        out = 0.0
        for e in range(experts):
            out = out + dot(gates[e], gate_ref[e], 1, 1) + dot(ups[e], up_ref[e], 1, 1)
        out_ref[at, :] = out.astype(BF)


def total_body(x_ref, out_ref):
    out = x_ref[0].astype(F32)
    for i in range(1, x_ref.shape[0]):
        out = out + x_ref[i].astype(F32)
    out_ref[...] = out.astype(BF)


def make(n_yh, n_yl, n_core, n_x, n_z):
    along_y, dp, cuts = ("yh", "yl"), ("yh", "yl", "core"), ("x", "z")
    n_y = n_yh * n_yl
    n_dp, n_cuts = n_y * n_core, n_x * n_z
    swap = [(i, n_core - 1 - i) for i in range(n_core)]
    left = [(i, i ^ 1) for i in range(n_y)]
    right = [(i, (i + 1) % n_y if i % 2 else (i - 1) % n_y) for i in range(n_y)]

    def per_device(tokens, cotangent, w_gate, w_up, w_down, row_token, block_expert, gate_weight):
        own, cols = tokens.shape
        n_tok = row_token.shape[0]
        experts, _, hid = w_gate.shape
        blk = n_tok // block_expert.shape[0]
        part = n_tok // n_dp
        at = jnp.stack([lax.axis_index("yl"), lax.axis_index("core")]).astype(jnp.int32)
        work = 2 * n_tok * experts * cols * hid

        def exchange(v, axes):
            return lax.all_to_all(v, axes, split_axis=0, concat_axis=0, tiled=True)

        def spread(v, n):
            return jnp.broadcast_to(v[None], (n,) + v.shape)

        def neighbours(v):
            half = v.shape[-1] // 2
            return (
                lax.ppermute(v[..., :half], along_y, left),
                lax.ppermute(v[..., half:], along_y, right),
            )

        first = (lax.axis_index("x") * n_z + lax.axis_index("z")) * own
        holds_own = row_token[None, :] == first + jnp.arange(own, dtype=jnp.int32)[:, None]
        weight_own = jnp.sum(jnp.where(holds_own, gate_weight[None, :], 0.0), axis=1)
        expert_row = jnp.repeat(block_expert[:, 0], blk)
        holds = row_token[None, :] == jnp.arange(n_tok, dtype=jnp.int32)[:, None]
        expert_tok = jnp.sum(jnp.where(holds, expert_row[None, :], 0), axis=1)[:, None]

        cot_own = (cotangent.astype(F32) * weight_own[:, None]).astype(BF)
        got = exchange(spread(jnp.stack([tokens, cot_own]), n_z), "z")
        got = exchange(spread(got.reshape(n_z, 2, own, cols), n_x), "x")
        got = got.reshape(n_cuts, 2, own, cols)

        shape = (n_yl, n_yh, part, 3 * hid)
        outs = [jax.ShapeDtypeStruct(shape, F32), jax.ShapeDtypeStruct(shape, BF)]
        args = (at, expert_tok, got, w_gate, w_up, w_down)
        keep, give = call(forward_body, outs, 3 * work, args)
        came = lax.ppermute(give, "core", swap)
        near = neighbours((keep[1] + came[1].astype(F32)).astype(BF))
        near = jnp.concatenate(near, axis=-1)
        chips = (keep[0] + came[0].astype(F32) + near.astype(F32)).astype(BF)
        pre = jnp.sum(exchange(chips, "yh").astype(F32), axis=0)
        hidden, gate_grad, up_grad = activate(
            pre[:, :hid], pre[:, hid : 2 * hid], pre[:, 2 * hid :]
        )
        hidden = lax.all_gather(hidden, dp, axis=0, tiled=True)
        grads = exchange(spread(jnp.concatenate([gate_grad, up_grad], axis=1), n_yh), "yh")
        grads = grads.reshape(n_yh, part, 2 * hid)
        mine = jnp.stack([grads, jnp.concatenate(neighbours(grads), axis=-1)])
        other = lax.ppermute(mine, "core", swap)

        outs = [
            jax.ShapeDtypeStruct((n_yh, n_yl, n_core, part, 2 * hid), BF),
            jax.ShapeDtypeStruct((n_tok, cols), BF),
        ]
        args = (at, expert_tok, w_gate, w_up, mine, other)
        grads, terms = call(terms_body, outs, 2 * work, args)
        grads, hidden = lax.optimization_barrier((grads.reshape(n_tok, 2 * hid), hidden))
        terms = exchange(terms.reshape(n_cuts, own, cols), cuts)
        outs = [jax.ShapeDtypeStruct((own, cols), BF)]
        (token_grad,) = call(total_body, outs, terms.size, (terms,))

        tok, cot = got[:, 0].reshape(n_tok, cols), got[:, 1].reshape(n_tok, cols)
        masks = [expert_tok == e for e in range(experts)]
        tok_by = jnp.concatenate([jnp.where(m, tok, 0) for m in masks], axis=1)
        grad_gate = dot(tok_by, grads[:, :hid], 0, 0).astype(BF).reshape(w_gate.shape)
        grad_up = dot(tok_by, grads[:, hid:], 0, 0).astype(BF).reshape(w_up.shape)
        grad_down = [dot(hidden, jnp.where(m, cot, 0), 0, 0).astype(BF) for m in masks]
        return token_grad, grad_gate, grad_up, jnp.stack(grad_down)

    return per_device


def solution(mesh):
    sizes, axes = (4, 2, 2, 4, 8), ("yh", "yl", "core", "x", "z")
    fine = Mesh(mesh.devices.reshape(sizes), axes)
    dp, cuts = ("yh", "yl", "core"), ("x", "z")
    return jax.shard_map(
        make(*sizes),
        mesh=fine,
        in_specs=(
            P(cuts, dp),
            P(cuts, dp),
            P(None, dp, cuts),
            P(None, dp, cuts),
            P(None, cuts, dp),
            P(),
            P(),
            P(),
        ),
        out_specs=(P(cuts, dp), P(None, dp, cuts), P(None, dp, cuts), P(None, cuts, dp)),
        check_vma=False,
    )
```

time: 225 us -> 194 us (0.86)
  waiting for transfers between devices: 124 us -> 45.1 us
  blocking collectives: 0 us -> 64.8 us
  starting transfers between devices: 52.6 us -> 33.2 us
    all_to_all x0 -> x3, blocking collectives: none -> 64.8 us  [exchange(): return lax.all_to_all(v, axes, split_axis=0, concat_axis=0, tiled=True)]
    all_gather x1 -> x0, waiting for transfers between devices: 46 us -> none  [per_device(): grads = lax.all_gather(grads, dp, axis=0, tiled=True)]
    all_to_all x5 -> x2, starting transfers between devices: 42.4 us -> 8.19 us  [exchange(): return lax.all_to_all(v, axes, split_axis=0, concat_axis=0, tiled=True)]
    all_to_all x5 -> x2, waiting for transfers between devices: 50.1 us -> 17.7 us  [exchange(): return lax.all_to_all(v, axes, split_axis=0, concat_axis=0, tiled=True)]
    ppermute x2 -> x6, starting transfers between devices: 10 us -> 25 us  [the longest x2 7.01 us: neighbours(): lax.ppermute(v[..., half:], along_y, right)]
    ppermute x2 -> x6, waiting for transfers between devices: 3.78 us -> 18.3 us  [the longest x2 9.32 us: neighbours(): lax.ppermute(v[..., half:], along_y, right)]
    all_gather x1, waiting for transfers between devices: 23.5 us -> 9.1 us  [per_device(): hidden = lax.all_gather(hidden, dp, axis=0, tiled=True)]
    convert_element_type x5 -> x3, other arithmetic: 4.08 us -> 1.19 us  [the longest x1 0.71 us: activate(): hidden = (swish_val * up_pre).astype(BF)]
  transfers between devices with their start and end apart: 9 -> 9, of which waited for: 8 -> 9; matrix products, arithmetic and copies ran while one was open for 7% -> 7% of each run, Pallas kernels for 4% -> 2%
where the time goes in v4:
time: 194 us; the launch traced here: 192 us
  blocking collectives  64.8 us (33%)
  waiting for transfers between devices  45.1 us (23%)
  starting transfers between devices  33.2 us (17%)
  between operations  14.3 us (7%)
  Pallas kernels  11.8 us (6%)
  other arithmetic  8.68 us (4%)
  local copies, waits for them, and re-layouts  7.13 us (4%)
  matrix products  6.79 us (4%)
    all_to_all x3, blocking collectives, exchange(): return lax.all_to_all(v, axes, split_axis=0, concat_axis=0, tiled=True)  64.8 us
    all_to_all x2, waiting for transfers between devices, exchange(): return lax.all_to_all(v, axes, split_axis=0, concat_axis=0, tiled=True)  17.7 us
    pallas_call x3, Pallas kernels, call(): pl.pallas_call(body, out_shape=outs, in_specs=in_specs, out_specs=[pl.Blo...  11.8 us
    ppermute x2, waiting for transfers between devices, neighbours(): lax.ppermute(v[..., half:], along_y, right)  9.32 us
    all_gather x1, waiting for transfers between devices, per_device(): hidden = lax.all_gather(hidden, dp, axis=0, tiled=True)  9.1 us
    all_to_all x2, starting transfers between devices, exchange(): return lax.all_to_all(v, axes, split_axis=0, concat_axis=0, tiled=True)  8.19 us
    ppermute x2, starting transfers between devices, neighbours(): lax.ppermute(v[..., half:], along_y, right)  7.01 us
    dot_general x4, matrix products, dot(): lax.dot_general(a, b, (((ca,), (cb,)), ((), ())), preferred_element_type=...  6.79 us
  transfers between devices with their start and end apart: 9, of which 9 were waited for; matrix products, arithmetic and copies ran while one was open for 7% of the time, Pallas kernels for 2%

profile of v4, /device:TPU:1, one launch (start us, length us, event | category | flops | bytes accessed | tf_op | source)
XLA Modules:
  0.0 191.8 jit_solution(15600670468372380864)
XLA Ops:
  7.2 0.0 copy-start
  7.2 0.9 select_reduce_fusion.1
  8.1 0.8 fusion.7
  8.9 0.7 pad_maximum_fusion.6
  9.7 24.2 %all_to_all.25 = bf16[8,2,32,384]{3,2,1,0:T(8,128)(2,1)S(1)} all-to-all(bf16[8,2,32,384]{3,2,1,0:T(8,128)(2,1)S(1)} %broadcast_in_dim.89), channel_id=1, replica_groups=mesh['yh'=4,'yl'=2,'core'=2,'x'=4,'z'=8] {'z'}, dimensions={0} | all-to-all | bytes 786432 | tf_op jit(solution)/shard_map/all_to_all | solution.py:121
  33.9 1.4 broadcast_in_dim.90
  35.3 4.1 %all-to-all-start.1 = ((bf16[4,8,2,32,384]{4,3,2,1,0:T(8,128)(2,1)}), bf16[4,8,2,32,384]{4,3,2,1,0:T(8,128)(2,1)S(1)}, u32[]{:S(2)}, u32[]{:S(2)}) async-start(bf16[4,8,2,32,384]{4,3,2,1,0:T(8,128)(2,1)} %broadcast_in_dim.90), calls=%async_computation.1 | async-start | bytes 3145728 | tf_op jit(solution)/shard_map/all_to_all | solution.py:121
  39.5 0.0 all-gather.2.cloned.1.call-start
  39.5 0.0 copy-done
  39.5 0.1 broadcast_bitcast_fusion
  39.6 0.5 select_reduce_fusion
  40.1 0.2 copy.15.expert_ref
  40.3 0.1 pad_add_fusion.at_ref
  40.4 17.5 %all-to-all-done.1 = bf16[4,8,2,32,384]{4,3,2,1,0:T(8,128)(2,1)S(1)} async-done(((bf16[4,8,2,32,384]{4,3,2,1,0:T(8,128)(2,1)}), bf16[4,8,2,32,384]{4,3,2,1,0:T(8,128)(2,1)S(1)}, u32[]{:S(2)}, u32[]{:S(2)}) %all-to-all-start.1) | async-done | bytes 1572896 | tf_op jit(solution)/shard_map/all_to_all | solution.py:121
  57.8 0.0 copy-done.1
  57.8 1.1 copy-done.2
  59.0 1.1 copy-done.4
  60.1 6.5 %shard_map.111 = (f32[2,4,64,1536]{3,2,1,0:T(8,128)S(1)}, bf16[2,4,64,1536]{3,2,1,0:T(8,128)(2,1)S(1)}) custom-call(s32[2]{0:T(128)S(1)} %pad_add_fusion.at_ref, s32[1024,1]{1,0:T(8,128)S(1)} %copy.15.expert_ref, bf16[32,2,32,384]{3,2,1,0:T(8,128)(2,1)S(1)} %bitcast.38, bf16[2,384,512]{2,1,0:T(8,128)(2,1)S(1)} %copy-done.2, ...), custom_call_target="tpu_custom_call" | custom-call | flops 2415919104 | bytes 8654856 | tf_op jit(solution)/shard_map/pallas_call | solution.py:35
  66.6 5.2 %collective-permute-start = (bf16[2,4,64,1536]{3,2,1,0:T(8,128)(2,1)S(1)}, bf16[2,4,64,1536]{3,2,1,0:T(8,128)(2,1)S(1)}, u32[]{:S(2)}, u32[]{:S(2)}) collective-permute-start(bf16[2,4,64,1536]{3,2,1,0:T(8,128)(2,1)S(1)} %get-tuple-element.11), channel_id=1, source_target_pairs={{0,32},{32,0},{1,33},{33,1},{2,34},{34,2},{3,35},{35,3},{4,36},{36... | collective-permute-start | bytes 4718600 | tf_op jit(solution)/shard_map/ppermute | solution.py:149
  71.8 3.0 %collective-permute-done = bf16[2,4,64,1536]{3,2,1,0:T(8,128)(2,1)S(1)} collective-permute-done((bf16[2,4,64,1536]{3,2,1,0:T(8,128)(2,1)S(1)}, bf16[2,4,64,1536]{3,2,1,0:T(8,128)(2,1)S(1)}, u32[]{:S(2)}, u32[]{:S(2)}) %collective-permute-start) | collective-permute-done | bytes 1572896 | tf_op jit(solution)/shard_map/ppermute | solution.py:149
  74.8 0.2 fusion.5
  75.0 0.1 fusion.11
  75.1 5.1 %collective-permute-start.2 = (bf16[4,64,768]{2,1,0:T(8,128)(2,1)S(1)}, bf16[4,64,768]{2,1,0:T(8,128)(2,1)S(1)}, u32[]{:S(2)}, u32[]{:S(2)}) collective-permute-start(bf16[4,64,768]{2,1,0:T(8,128)(2,1)S(1)} %get-tuple-element.23), channel_id=1, source_target_pairs={{0,448},{64,128},{128,64},{192,256},{256,192},{320,384},{384,320},... | collective-permute-start | bytes 1179656 | tf_op jit(solution)/shard_map/ppermute | solution.py:130
  80.2 1.9 %collective-permute-start.1 = (bf16[4,64,768]{2,1,0:T(8,128)(2,1)S(1)}, bf16[4,64,768]{2,1,0:T(8,128)(2,1)S(1)}, u32[]{:S(2)}, u32[]{:S(2)}) collective-permute-start(bf16[4,64,768]{2,1,0:T(8,128)(2,1)S(1)} %get-tuple-element.22), channel_id=1, source_target_pairs={{0,64},{64,0},{128,192},{192,128},{256,320},{320,256},{384,448},{4... | collective-permute-start | bytes 1179656 | tf_op jit(solution)/shard_map/ppermute | solution.py:129
  82.1 7.2 %collective-permute-done.2 = bf16[4,64,768]{2,1,0:T(8,128)(2,1)S(1)} collective-permute-done((bf16[4,64,768]{2,1,0:T(8,128)(2,1)S(1)}, bf16[4,64,768]{2,1,0:T(8,128)(2,1)S(1)}, u32[]{:S(2)}, u32[]{:S(2)}) %collective-permute-start.2) | collective-permute-done | bytes 393248 | tf_op jit(solution)/shard_map/ppermute | solution.py:130
  89.4 2.7 %collective-permute-done.1 = bf16[4,64,768]{2,1,0:T(8,128)(2,1)S(1)} collective-permute-done((bf16[4,64,768]{2,1,0:T(8,128)(2,1)S(1)}, bf16[4,64,768]{2,1,0:T(8,128)(2,1)S(1)}, u32[]{:S(2)}, u32[]{:S(2)}) %collective-permute-start.1) | collective-permute-done | bytes 393248 | tf_op jit(solution)/shard_map/ppermute | solution.py:129
  92.1 0.3 fusion
  92.4 23.1 %all_to_all.26 = bf16[4,64,1536]{2,1,0:T(8,128)(2,1)S(1)} all-to-all(bf16[4,64,1536]{2,1,0:T(8,128)(2,1)S(1)} %fusion), channel_id=1, replica_groups=mesh['yh'=4,'yl'=2,'core'=2,'x'=4,'z'=8] {'yh'}, dimensions={0} | all-to-all | bytes 1572864 | tf_op jit(solution)/shard_map/all_to_all | solution.py:121
  115.4 0.1 convert_reduce_fusion
  115.6 0.7 multiply_convert_fusion
  116.3 0.1 broadcast_in_dim.91
  116.3 17.5 %all_to_all.27 = bf16[4,64,1024]{2,1,0:T(8,128)(2,1)S(1)} all-to-all(bf16[4,64,1024]{2,1,0:T(8,128)(2,1)S(1)} %broadcast_in_dim.91), channel_id=1, replica_groups=mesh['yh'=4,'yl'=2,'core'=2,'x'=4,'z'=8] {'yh'}, dimensions={0} | all-to-all | bytes 1048576 | tf_op jit(solution)/shard_map/all_to_all | solution.py:121
  133.9 1.9 %collective-permute-start.4 = (bf16[4,64,512]{2,1,0:T(8,128)(2,1)S(1)}, bf16[4,64,512]{2,1,0:T(8,128)(2,1)S(1)}, u32[]{:S(2)}, u32[]{:S(2)}) collective-permute-start(bf16[4,64,512]{2,1,0:T(8,128)(2,1)S(1)} %get-tuple-element.25), channel_id=1, source_target_pairs={{0,448},{64,128},{128,64},{192,256},{256,192},{320,384},{384,320},... | collective-permute-start | bytes 786440 | tf_op jit(solution)/shard_map/ppermute | solution.py:130
  135.8 4.3 %collective-permute-start.3 = (bf16[4,64,512]{2,1,0:T(8,128)(2,1)S(1)}, bf16[4,64,512]{2,1,0:T(8,128)(2,1)}, u32[]{:S(2)}, u32[]{:S(2)}) collective-permute-start(bf16[4,64,512]{2,1,0:T(8,128)(2,1)S(1)} %get-tuple-element.24), channel_id=1, source_target_pairs={{0,64},{64,0},{128,192},{192,128},{256,320},{320,256},{384,448},{4... | collective-permute-start | bytes 786440 | tf_op jit(solution)/shard_map/ppermute | solution.py:129
  140.1 0.0 all-gather.2.cloned.1.call-update
  140.2 2.1 %collective-permute-done.4 = bf16[4,64,512]{2,1,0:T(8,128)(2,1)S(1)} collective-permute-done((bf16[4,64,512]{2,1,0:T(8,128)(2,1)S(1)}, bf16[4,64,512]{2,1,0:T(8,128)(2,1)S(1)}, u32[]{:S(2)}, u32[]{:S(2)}) %collective-permute-start.4) | collective-permute-done | bytes 262176 | tf_op jit(solution)/shard_map/ppermute | solution.py:130
  142.2 1.9 %collective-permute-done.3 = bf16[4,64,512]{2,1,0:T(8,128)(2,1)} collective-permute-done((bf16[4,64,512]{2,1,0:T(8,128)(2,1)S(1)}, bf16[4,64,512]{2,1,0:T(8,128)(2,1)}, u32[]{:S(2)}, u32[]{:S(2)}) %collective-permute-start.3) | collective-permute-done | bytes 262176 | tf_op jit(solution)/shard_map/ppermute | solution.py:129
  144.2 1.0 maximum_bitcast_fusion
  145.2 0.1 pad_maximum_fusion.1.mine_ref
  145.3 6.6 %collective-permute-start.5 = (bf16[2,4,64,1024]{3,2,1,0:T(8,128)(2,1)S(1)}, bf16[2,4,64,1024]{3,2,1,0:T(8,128)(2,1)S(1)}, u32[]{:S(2)}, u32[]{:S(2)}) collective-permute-start(bf16[2,4,64,1024]{3,2,1,0:T(8,128)(2,1)S(1)} %pad_maximum_fusion.1.mine_ref), channel_id=1, source_target_pairs={{0,32},{32,0},{1,33},{33,1},{2,34},{34,2},{3,35},{35,3},{4,36},{36... | collective-permute-start | bytes 3145736 | tf_op jit(solution)/shard_map/ppermute | solution.py:161
  151.9 0.0 copy-start.3
  151.9 0.0 copy-start.5
  151.9 1.0 fusion.10
  153.0 1.3 collective-permute-done.5.other_ref
  154.3 0.0 copy-done.3
  154.3 4.6 %shard_map.112 = (bf16[4,2,2,64,1024]{4,3,2,1,0:T(8,128)(2,1)S(1)}, bf16[1024,384]{1,0:T(8,128)(2,1)}) custom-call(s32[2]{0:T(128)S(1)} %pad_add_fusion.at_ref, s32[1024,1]{1,0:T(8,128)S(1)} %copy.15.expert_ref, bf16[2,384,512]{2,1,0:T(8,128)(2,1)S(1)} %copy-done.3, bf16[2,384,512]{2,1,0:T(8,128)(2,1)S(1)} %copy-done.5, ...), custom_call_target="tpu_custom_call" | custom-call | flops 1610612736 | bytes 6557704 | tf_op jit(solution)/shard_map/pallas_call | solution.py:35
  158.8 1.3 copy-done.6
  160.2 4.0 %all-to-all-start.4 = ((bf16[32,32,384]{2,1,0:T(8,128)(2,1)}), bf16[32,32,384]{2,1,0:T(8,128)(2,1)S(1)}, u32[]{:S(2)}, u32[]{:S(2)}) async-start(bf16[32,32,384]{2,1,0:T(8,128)(2,1)} %bitcast.12), calls=%async_computation.4 | async-start | bytes 1572864 | tf_op jit(solution)/shard_map/all_to_all | solution.py:121
  164.2 2.2 %bitcast_select_fusion.3 = (bf16[1024,384]{1,0:T(8,128)(2,1)}, bf16[1024,384]{1,0:T(8,128)(2,1)}, bf16[1024,384]{1,0:T(8,128)(2,1)}, bf16[1024,384]{1,0:T(8,128)(2,1)}) fusion(bf16[32,1,32,384]{3,2,1,0:T(8,128)(2,1)S(1)} %copy-done.8, pred[1024]{0:T(1024)(128)(4,1)S(1)} %get-tuple-element.29, pred[1024]{0:T(1024)(128)(4,1)S(1)} %get-tuple-element.30, ...), kind=kLoop, calls=%fused_computation.21 | loop fusion | flops 1572864 | bytes 4720640 | tf_op jit(solution)/shard_map/jit(_where)/select_n | solution.py:176
  166.5 9.1 %all-gather.2.cloned.1.call-done = bf16[1024,512]{1,0:T(8,128)(2,1)} async-done(((bf16[64,512]{1,0:T(8,128)(2,1)}), bf16[1024,512]{1,0:T(8,128)(2,1)}) %all-gather.2.cloned.1.call-update) | async-done | bytes 1048592 | tf_op jit(solution)/shard_map/all_gather | solution.py:157
  175.6 2.3 %fusion.2 = bf16[1,512,384]{2,1,0:T(8,128)(2,1)S(1)} fusion(bf16[1024,512]{1,0:T(8,128)(2,1)} %all-gather.2.cloned.1.call-done, bf16[1024,384]{1,0:T(8,128)(2,1)} %get-tuple-element.31), kind=kOutput, calls=%fused_computation.12 | convolution fusion | flops 402849792 | bytes 2228224 | tf_op jit(solution)/shard_map/dot_general | solution.py:18
  177.9 0.0 copy-done.11
  177.9 0.0 copy-done.13
  177.9 0.0 copy-start.7
  177.9 0.0 copy-start.9
  177.9 0.0 copy-start.10
  177.9 0.7 fusion.1
  178.7 1.0 pad_maximum_fusion.4
  179.6 0.0 copy-done.9
  179.6 0.5 copy-done.10
  180.2 1.9 convolution_convert_fusion.1
  182.0 1.9 convolution_convert_fusion
  183.9 0.3 all-to-all-done.4.x_ref
  184.2 0.7 shard_map.113
  (17 shorter events, 0.1 us)
Async XLA Ops:
  7.2 32.3 %copy-start = (s32[8,1]{0,1:T(1,128)S(1)}, s32[8,1]{0,1:T(1,128)}, u32[]{:S(2)}) copy-start(s32[8,1]{0,1:T(1,128)} %param.14) | copy-start | bytes 100
  35.3 4.2 %copy-start.12 = (s32[1024]{0:T(1024)S(1)}, s32[1024]{0:T(1024)}, u32[]{:S(2)}) copy-start(s32[1024]{0:T(1024)} %param.13) | copy-start | bytes 12292
  35.3 22.5 %copy-start.1 = (bf16[2,512,384]{2,1,0:T(8,128)(2,1)S(1)}, bf16[2,512,384]{2,1,0:T(8,128)(2,1)}, u32[]{:S(2)}) copy-start(bf16[2,512,384]{2,1,0:T(8,128)(2,1)} %wd_ref.1) | copy-start | bytes 2359300
  35.3 22.5 %all-to-all-start.1 = ((bf16[4,8,2,32,384]{4,3,2,1,0:T(8,128)(2,1)}), bf16[4,8,2,32,384]{4,3,2,1,0:T(8,128)(2,1)S(1)}, u32[]{:S(2)}, u32[]{:S(2)}) async-start(bf16[4,8,2,32,384]{4,3,2,1,0:T(8,128)(2,1)} %broadcast_in_dim.90), calls=%async_computation.1 | async-start | bytes 3145728 | tf_op jit(solution)/shard_map/all_to_all | solution.py:121
  39.5 136.1 %all-gather.2.cloned.1.call-start = ((), (), s32[]{:S(2)}) async-start(), calls=%async_computation.5 | async-start | bytes 1114112 | tf_op jit(solution)/shard_map/all_gather | solution.py:157
  57.8 1.1 copy-start.2
  59.0 1.1 copy-start.4
  66.6 8.3 %collective-permute-start = (bf16[2,4,64,1536]{3,2,1,0:T(8,128)(2,1)S(1)}, bf16[2,4,64,1536]{3,2,1,0:T(8,128)(2,1)S(1)}, u32[]{:S(2)}, u32[]{:S(2)}) collective-permute-start(bf16[2,4,64,1536]{3,2,1,0:T(8,128)(2,1)S(1)} %get-tuple-element.11), channel_id=1, source_target_pairs={{0,32},{32,0},{1,33},{33,1},{2,34},{34,2},{3,35},{35,3},{4,36},{36... | collective-permute-start | bytes 4718600 | tf_op jit(solution)/shard_map/ppermute | solution.py:149
  75.1 14.3 %collective-permute-start.2 = (bf16[4,64,768]{2,1,0:T(8,128)(2,1)S(1)}, bf16[4,64,768]{2,1,0:T(8,128)(2,1)S(1)}, u32[]{:S(2)}, u32[]{:S(2)}) collective-permute-start(bf16[4,64,768]{2,1,0:T(8,128)(2,1)S(1)} %get-tuple-element.23), channel_id=1, source_target_pairs={{0,448},{64,128},{128,64},{192,256},{256,192},{320,384},{384,320},... | collective-permute-start | bytes 1179656 | tf_op jit(solution)/shard_map/ppermute | solution.py:130
  80.2 11.9 %collective-permute-start.1 = (bf16[4,64,768]{2,1,0:T(8,128)(2,1)S(1)}, bf16[4,64,768]{2,1,0:T(8,128)(2,1)S(1)}, u32[]{:S(2)}, u32[]{:S(2)}) collective-permute-start(bf16[4,64,768]{2,1,0:T(8,128)(2,1)S(1)} %get-tuple-element.22), channel_id=1, source_target_pairs={{0,64},{64,0},{128,192},{192,128},{256,320},{320,256},{384,448},{4... | collective-permute-start | bytes 1179656 | tf_op jit(solution)/shard_map/ppermute | solution.py:129
  133.9 8.3 %collective-permute-start.4 = (bf16[4,64,512]{2,1,0:T(8,128)(2,1)S(1)}, bf16[4,64,512]{2,1,0:T(8,128)(2,1)S(1)}, u32[]{:S(2)}, u32[]{:S(2)}) collective-permute-start(bf16[4,64,512]{2,1,0:T(8,128)(2,1)S(1)} %get-tuple-element.25), channel_id=1, source_target_pairs={{0,448},{64,128},{128,64},{192,256},{256,192},{320,384},{384,320},... | collective-permute-start | bytes 786440 | tf_op jit(solution)/shard_map/ppermute | solution.py:130
  135.8 8.3 %collective-permute-start.3 = (bf16[4,64,512]{2,1,0:T(8,128)(2,1)S(1)}, bf16[4,64,512]{2,1,0:T(8,128)(2,1)}, u32[]{:S(2)}, u32[]{:S(2)}) collective-permute-start(bf16[4,64,512]{2,1,0:T(8,128)(2,1)S(1)} %get-tuple-element.24), channel_id=1, source_target_pairs={{0,64},{64,0},{128,192},{192,128},{256,320},{320,256},{384,448},{4... | collective-permute-start | bytes 786440 | tf_op jit(solution)/shard_map/ppermute | solution.py:129
  145.3 9.0 %collective-permute-start.5 = (bf16[2,4,64,1024]{3,2,1,0:T(8,128)(2,1)S(1)}, bf16[2,4,64,1024]{3,2,1,0:T(8,128)(2,1)S(1)}, u32[]{:S(2)}, u32[]{:S(2)}) collective-permute-start(bf16[2,4,64,1024]{3,2,1,0:T(8,128)(2,1)S(1)} %pad_maximum_fusion.1.mine_ref), channel_id=1, source_target_pairs={{0,32},{32,0},{1,33},{33,1},{2,34},{34,2},{3,35},{35,3},{4,36},{36... | collective-permute-start | bytes 3145736 | tf_op jit(solution)/shard_map/ppermute | solution.py:161
  151.9 2.3 %copy-start.3 = (bf16[2,384,512]{2,1,0:T(8,128)(2,1)S(1)}, bf16[2,384,512]{2,1,0:T(8,128)(2,1)}, u32[]{:S(2)}) copy-start(bf16[2,384,512]{2,1,0:T(8,128)(2,1)} %gate_ref.1) | copy-start | bytes 2359300
  151.9 2.3 %copy-start.5 = (bf16[2,384,512]{2,1,0:T(8,128)(2,1)S(1)}, bf16[2,384,512]{2,1,0:T(8,128)(2,1)}, u32[]{:S(2)}) copy-start(bf16[2,384,512]{2,1,0:T(8,128)(2,1)} %up_ref.1) | copy-start | bytes 2359300
  158.8 1.3 copy-start.6
  160.2 4.1 %copy-start.8 = (bf16[32,1,32,384]{3,2,1,0:T(8,128)(2,1)S(1)}, bf16[32,1,32,384]{3,2,1,0:T(8,128)(2,1)}, u32[]{:S(2)}) copy-start(bf16[32,1,32,384]{3,2,1,0:T(8,128)(2,1)} %get-tuple-element.17) | copy-start | bytes 2359300
  160.2 24.0 %all-to-all-start.4 = ((bf16[32,32,384]{2,1,0:T(8,128)(2,1)}), bf16[32,32,384]{2,1,0:T(8,128)(2,1)S(1)}, u32[]{:S(2)}, u32[]{:S(2)}) async-start(bf16[32,32,384]{2,1,0:T(8,128)(2,1)} %bitcast.12), calls=%async_computation.4 | async-start | bytes 1572864 | tf_op jit(solution)/shard_map/all_to_all | solution.py:121
  166.5 11.4 %copy-start.11 = (bf16[1024,384]{1,0:T(8,128)(2,1)S(1)}, bf16[1024,384]{1,0:T(8,128)(2,1)}, u32[]{:S(2)}) copy-start(bf16[1024,384]{1,0:T(8,128)(2,1)} %get-tuple-element.32) | copy-start | bytes 2359300
  175.6 2.3 %copy-start.13 = (bf16[1024,512]{1,0:T(8,128)(2,1)S(1)}, bf16[1024,512]{1,0:T(8,128)(2,1)}, u32[]{:S(2)}) copy-start(bf16[1024,512]{1,0:T(8,128)(2,1)} %all-gather.2.cloned.1.call-done) | copy-start | bytes 3145732
  177.9 1.8 copy-start.7
  177.9 1.8 copy-start.9
  177.9 2.3 %copy-start.10 = (bf16[1024,384]{1,0:T(8,128)(2,1)S(1)}, bf16[1024,384]{1,0:T(8,128)(2,1)}, u32[]{:S(2)}) copy-start(bf16[1024,384]{1,0:T(8,128)(2,1)} %get-tuple-element.21) | copy-start | bytes 2359300
Sparse Core Ops, SparseCore 0:
  140.3 35.2 all-gather.1

commit v5 on v4

--- a/solution.py
+++ b/solution.py
@@ -46,51 +46,79 @@
     return [jnp.where(expert == e, rows, jnp.zeros_like(rows)) for e in range(experts)]
 
 
-def forward_body(at_ref, expert_ref, got_ref, wg_ref, wu_ref, wd_ref, keep_ref, give_ref):
-    _, n_yh, part, width = keep_ref.shape
+def forward_body(side, at_ref, expert_ref, got_ref, wg_ref, wu_ref, wd_ref, keep_ref, give_ref):
+    n_yh, part, width = keep_ref.shape
     experts = wg_ref.shape[0]
     _, _, own, cols = got_ref.shape
     hid = width // 3
-    parity, core = at_ref[0], at_ref[1]
-    owners = ROWS // own
-    for k, w_ref in enumerate((wg_ref, wu_ref, wd_ref)):
-        side, cb = k // 2, k // 2
-        to = slice(k * hid, (k + 1) * hid)
-
-        @pl.loop(0, n_yh)
-        def _(i):
-            expert = expert_ref[pl.ds(pl.multiple_of(i * ROWS, ROWS), ROWS), :]
-            rows = got_ref[pl.ds(i * owners, owners), side].reshape(ROWS, cols)
+    parity, core = lax.rem(at_ref[0] + side, 2), at_ref[1]
+    per = 2 * part
+    owners = per // own
+    group = ROWS // per
+
+    @pl.loop(0, n_yh // group)
+    def _(i):
+        starts = [2 * (i * group + q) + parity for q in range(group)]
+        expert = jnp.concatenate(
+            [expert_ref[pl.ds(pl.multiple_of(s * per, per), per), :] for s in starts]
+        )
+        masked = []
+        for kind in range(2):
+            rows = [got_ref[pl.ds(s * owners, owners), kind].reshape(per, cols) for s in starts]
+            masked.append(by_expert(jnp.concatenate(rows), expert, experts))
+        for k, w_ref in enumerate((wg_ref, wu_ref, wd_ref)):
             out = 0.0
-            for e, x in enumerate(by_expert(rows, expert, experts)):
-                out = out + dot(x, w_ref[e], 1, cb)
-            for p in range(2):
-                even = out[2 * p * part : (2 * p + 1) * part]
-                odd = out[(2 * p + 1) * part : (2 * p + 2) * part]
-                slot = lax.rem(parity + p, 2)
-                keep_ref[slot, i, :, to] = jnp.where(core == 0, even, odd)
-                give_ref[slot, i, :, to] = jnp.where(core == 0, odd, even).astype(BF)
-
-
-def terms_body(at_ref, expert_ref, gate_ref, up_ref, mine_ref, other_ref, grads_ref, out_ref):
-    n_yh, n_yl, n_core, part, width = grads_ref.shape
+            for e in range(experts):
+                out = out + dot(masked[k // 2][e], w_ref[e], 1, k // 2)
+            to = slice(k * hid, (k + 1) * hid)
+            for q in range(group):
+                even = out[q * per : q * per + part]
+                odd = out[q * per + part : (q + 1) * per]
+                keep_ref[i * group + q, :, to] = jnp.where(core == 0, even, odd)
+                give_ref[i * group + q, :, to] = jnp.where(core == 0, odd, even).astype(BF)
+
+
+def terms_body(side, at_ref, expert_ref, gate_ref, up_ref, mine_ref, other_ref, *refs):
+    out_ref = refs[-1]
+    n_yh, part, width = mine_ref.shape
     experts, _, hid = gate_ref.shape
-    parity, core = at_ref[0], at_ref[1]
-
-    @pl.loop(0, n_yh)
+    parity, core = lax.rem(at_ref[0] + side, 2), at_ref[1]
+    per = 2 * part
+    group = ROWS // per
+
+    @pl.loop(0, n_yh // group)
     def _(i):
-        for p in range(n_yl):
-            grads_ref[i, lax.rem(parity + p, 2), core] = mine_ref[p, i]
-            grads_ref[i, lax.rem(parity + p, 2), 1 - core] = other_ref[p, i]
-        at = pl.ds(pl.multiple_of(i * ROWS, ROWS), ROWS)
-        expert = expert_ref[at, :]
-        rows = grads_ref[i].reshape(ROWS, width)
+        expert, rows = [], []
+        for q in range(group):
+            start = (2 * (i * group + q) + parity) * per
+            expert.append(expert_ref[pl.ds(pl.multiple_of(start, per), per), :])
+            mine, other = mine_ref[i * group + q], other_ref[i * group + q]
+            rows += [jnp.where(core == 0, mine, other), jnp.where(core == 0, other, mine)]
+        expert, rows = jnp.concatenate(expert), jnp.concatenate(rows)
         gates = by_expert(rows[:, :hid], expert, experts)
         ups = by_expert(rows[:, hid:], expert, experts)
         out = 0.0
         for e in range(experts):
             out = out + dot(gates[e], gate_ref[e], 1, 1) + dot(ups[e], up_ref[e], 1, 1)
-        out_ref[at, :] = out.astype(BF)
+        out = out.astype(BF)
+        for q in range(group):
+            piece = out[q * per : (q + 1) * per]
+            if side:
+                out_ref[i * group + q, parity] = piece
+                out_ref[i * group + q, 1 - parity] = refs[0][i * group + q]
+            else:
+                out_ref[i * group + q] = piece
+
+
+def order_body(at_ref, mine_ref, other_ref, far_mine_ref, far_other_ref, out_ref):
+    parity, core = at_ref[0], at_ref[1]
+
+    @pl.loop(0, mine_ref.shape[0])
+    def _(i):
+        out_ref[i, parity, core] = mine_ref[i]
+        out_ref[i, parity, 1 - core] = other_ref[i]
+        out_ref[i, 1 - parity, core] = far_mine_ref[i]
+        out_ref[i, 1 - parity, 1 - core] = far_other_ref[i]
 
 
 def total_body(x_ref, out_ref):
@@ -123,12 +151,12 @@
         def spread(v, n):
             return jnp.broadcast_to(v[None], (n,) + v.shape)
 
+        def halves(v):
+            half = v.shape[-1] // 2
+            return v[..., :half], v[..., half:]
+
         def neighbours(v):
-            half = v.shape[-1] // 2
-            return (
-                lax.ppermute(v[..., :half], along_y, left),
-                lax.ppermute(v[..., half:], along_y, right),
-            )
+            return lax.ppermute(v[0], along_y, left), lax.ppermute(v[1], along_y, right)
 
         first = (lax.axis_index("x") * n_z + lax.axis_index("z")) * own
         holds_own = row_token[None, :] == first + jnp.arange(own, dtype=jnp.int32)[:, None]
@@ -142,14 +170,22 @@
         got = exchange(spread(got.reshape(n_z, 2, own, cols), n_x), "x")
         got = got.reshape(n_cuts, 2, own, cols)
 
-        shape = (n_yl, n_yh, part, 3 * hid)
+        shape = (n_yh, part, 3 * hid)
         outs = [jax.ShapeDtypeStruct(shape, F32), jax.ShapeDtypeStruct(shape, BF)]
-        args = (at, expert_tok, got, w_gate, w_up, w_down)
-        keep, give = call(forward_body, outs, 3 * work, args)
+
+        def forward(side):
+            args = (at, expert_tok, got, w_gate, w_up, w_down)
+            return call(functools.partial(forward_body, side), outs, 3 * work // 2, args)
+
+        far_keep, far_give = forward(1)
+        far_came = lax.ppermute(far_give, "core", swap)
+        keep, give = forward(0)
+        far = halves((far_keep + far_came.astype(F32)).astype(BF))
+        far, give = lax.optimization_barrier((far, give))
+        near = neighbours(far)
         came = lax.ppermute(give, "core", swap)
-        near = neighbours((keep[1] + came[1].astype(F32)).astype(BF))
-        near = jnp.concatenate(near, axis=-1)
-        chips = (keep[0] + came[0].astype(F32) + near.astype(F32)).astype(BF)
+        chips = keep + came.astype(F32) + jnp.concatenate(near, axis=-1).astype(F32)
+        chips = chips.astype(BF)
         pre = jnp.sum(exchange(chips, "yh").astype(F32), axis=0)
         hidden, gate_grad, up_grad = activate(
             pre[:, :hid], pre[:, hid : 2 * hid], pre[:, 2 * hid :]
@@ -157,24 +193,28 @@
         hidden = lax.all_gather(hidden, dp, axis=0, tiled=True)
         grads = exchange(spread(jnp.concatenate([gate_grad, up_grad], axis=1), n_yh), "yh")
         grads = grads.reshape(n_yh, part, 2 * hid)
-        mine = jnp.stack([grads, jnp.concatenate(neighbours(grads), axis=-1)])
-        other = lax.ppermute(mine, "core", swap)
-
-        outs = [
-            jax.ShapeDtypeStruct((n_yh, n_yl, n_core, part, 2 * hid), BF),
-            jax.ShapeDtypeStruct((n_tok, cols), BF),
-        ]
-        args = (at, expert_tok, w_gate, w_up, mine, other)
-        grads, terms = call(terms_body, outs, 2 * work, args)
-        grads, hidden = lax.optimization_barrier((grads.reshape(n_tok, 2 * hid), hidden))
+        near = neighbours(halves(grads))
+        other = lax.ppermute(grads, "core", swap)
+        outs = [jax.ShapeDtypeStruct((n_yh, n_core * part, cols), BF)]
+        args = (at, expert_tok, w_gate, w_up, grads, other)
+        (own_terms,) = call(functools.partial(terms_body, 0), outs, work, args)
+        far = jnp.concatenate(near, axis=-1)
+        far_other = lax.ppermute(far, "core", swap)
+        outs = [jax.ShapeDtypeStruct((n_yh, n_yl, n_core * part, cols), BF)]
+        args = (at, expert_tok, w_gate, w_up, far, far_other, own_terms)
+        (terms,) = call(functools.partial(terms_body, 1), outs, work, args)
         terms = exchange(terms.reshape(n_cuts, own, cols), cuts)
         outs = [jax.ShapeDtypeStruct((own, cols), BF)]
         (token_grad,) = call(total_body, outs, terms.size, (terms,))
 
+        outs = [jax.ShapeDtypeStruct((n_yh, n_yl, n_core, part, 2 * hid), BF)]
+        (grads,) = call(order_body, outs, grads.size, (at, grads, other, far, far_other))
+        grads = grads.reshape(n_tok, 2 * hid)
         tok, cot = got[:, 0].reshape(n_tok, cols), got[:, 1].reshape(n_tok, cols)
         masks = [expert_tok == e for e in range(experts)]
         tok_by = jnp.concatenate([jnp.where(m, tok, 0) for m in masks], axis=1)
         grad_gate = dot(tok_by, grads[:, :hid], 0, 0).astype(BF).reshape(w_gate.shape)
+        grads, hidden = lax.optimization_barrier((grads, hidden))
         grad_up = dot(tok_by, grads[:, hid:], 0, 0).astype(BF).reshape(w_up.shape)
         grad_down = [dot(hidden, jnp.where(m, cot, 0), 0, 0).astype(BF) for m in masks]
         return token_grad, grad_gate, grad_up, jnp.stack(grad_down)

time: 194 us -> 192 us (0.990)
  blocking collectives: 64.8 us -> 47.2 us
  starting transfers between devices: 33.2 us -> 47 us
    all_to_all x2 -> x3, waiting for transfers between devices: 17.7 us -> 36.3 us  [exchange(): return lax.all_to_all(v, axes, split_axis=0, concat_axis=0, tiled=True)]
    all_to_all x3 -> x2, blocking collectives: 64.8 us -> 47.2 us  [exchange(): return lax.all_to_all(v, axes, split_axis=0, concat_axis=0, tiled=True)]
    ppermute x5 -> x7, starting transfers between devices: 19.8 us -> 32.3 us  [the longest x2 8.25 us: neighbours(): lax.ppermute(v[1], along_y, right)]
    all_gather x1, waiting for transfers between devices: 9.1 us -> 0.01 us  [per_device(): hidden = lax.all_gather(hidden, dp, axis=0, tiled=True)]
    ppermute x5 -> x7, waiting for transfers between devices: 15.3 us -> 9.84 us  [the longest x2 7.1 us: neighbours(): lax.ppermute(v[1], along_y, right)]
    all_to_all x2 -> x3, starting transfers between devices: 8.19 us -> 12.8 us  [exchange(): return lax.all_to_all(v, axes, split_axis=0, concat_axis=0, tiled=True)]
    ppermute x1, starting transfers between devices: 5.23 us -> 1.92 us  [per_device(): came = lax.ppermute(give, 'core', swap)]
    ppermute x1, waiting for transfers between devices: 3.01 us -> 0.01 us  [per_device(): came = lax.ppermute(give, 'core', swap)]
  transfers between devices with their start and end apart: 9 -> 12, of which waited for: 9 -> 5; matrix products, arithmetic and copies ran while one was open for 7% -> 7% of each run, Pallas kernels for 2% -> 4%
where the time goes in v5:
time: 192 us; the launch traced here: 191 us
  blocking collectives  47.2 us (25%)
  starting transfers between devices  47 us (24%)
  waiting for transfers between devices  46.8 us (24%)
  between operations  14.4 us (8%)
  Pallas kernels  11.6 us (6%)
  local copies, waits for them, and re-layouts  8.87 us (5%)
  other arithmetic  8.23 us (4%)
  matrix products  6.61 us (3%)
    all_to_all x2, blocking collectives, exchange(): return lax.all_to_all(v, axes, split_axis=0, concat_axis=0, tiled=True)  47.2 us
    all_to_all x3, waiting for transfers between devices, exchange(): return lax.all_to_all(v, axes, split_axis=0, concat_axis=0, tiled=True)  36.3 us
    all_to_all x3, starting transfers between devices, exchange(): return lax.all_to_all(v, axes, split_axis=0, concat_axis=0, tiled=True)  12.8 us
    pallas_call x6, Pallas kernels, call(): pl.pallas_call(body, out_shape=outs, in_specs=in_specs, out_specs=[pl.Blo...  11.6 us
    ppermute x2, starting transfers between devices, neighbours(): lax.ppermute(v[1], along_y, right)  8.25 us
    ppermute x1, starting transfers between devices, per_device(): other = lax.ppermute(grads, 'core', swap)  7.78 us
    ppermute x1, starting transfers between devices, per_device(): far_other = lax.ppermute(far, 'core', swap)  7.23 us
    ppermute x2, waiting for transfers between devices, neighbours(): lax.ppermute(v[1], along_y, right)  7.1 us
  transfers between devices with their start and end apart: 12, of which 5 were waited for; matrix products, arithmetic and copies ran while one was open for 7% of the time, Pallas kernels for 4%

profile of v5, /device:TPU:1, one launch (start us, length us, event | category | flops | bytes accessed | tf_op | source)
XLA Modules:
  0.0 190.8 jit_solution(11030153917495966447)
XLA Ops:
  7.2 0.0 copy-start
  7.2 0.9 select_reduce_fusion.1
  8.1 0.8 fusion.5
  8.9 0.7 pad_maximum_fusion.5
  9.7 24.2 %all_to_all.25 = bf16[8,2,32,384]{3,2,1,0:T(8,128)(2,1)S(1)} all-to-all(bf16[8,2,32,384]{3,2,1,0:T(8,128)(2,1)S(1)} %broadcast_in_dim.89), channel_id=1, replica_groups=mesh['yh'=4,'yl'=2,'core'=2,'x'=4,'z'=8] {'z'}, dimensions={0} | all-to-all | bytes 786432 | tf_op jit(solution)/shard_map/all_to_all | solution.py:149
  33.9 1.4 broadcast_in_dim.90
  35.3 4.1 %all-to-all-start.1 = ((bf16[4,8,2,32,384]{4,3,2,1,0:T(8,128)(2,1)}), bf16[4,8,2,32,384]{4,3,2,1,0:T(8,128)(2,1)S(1)}, u32[]{:S(2)}, u32[]{:S(2)}) async-start(bf16[4,8,2,32,384]{4,3,2,1,0:T(8,128)(2,1)} %broadcast_in_dim.90), calls=%async_computation.1 | async-start | bytes 3145728 | tf_op jit(solution)/shard_map/all_to_all | solution.py:149
  39.5 0.1 broadcast_bitcast_fusion
  39.5 0.5 select_reduce_fusion
  40.0 0.2 copy.19.expert_ref
  40.3 0.1 pad_add_fusion.at_ref
  40.4 17.5 %all-to-all-done.1 = bf16[4,8,2,32,384]{4,3,2,1,0:T(8,128)(2,1)S(1)} async-done(((bf16[4,8,2,32,384]{4,3,2,1,0:T(8,128)(2,1)}), bf16[4,8,2,32,384]{4,3,2,1,0:T(8,128)(2,1)S(1)}, u32[]{:S(2)}, u32[]{:S(2)}) %all-to-all-start.1) | async-done | bytes 1572896 | tf_op jit(solution)/shard_map/all_to_all | solution.py:149
  57.8 1.1 copy-done.3
  59.0 1.1 copy-done.11
  60.1 2.6 %shard_map.112 = (f32[4,64,1536]{2,1,0:T(8,128)S(1)}, bf16[4,64,1536]{2,1,0:T(8,128)(2,1)S(1)}) custom-call(s32[2]{0:T(128)S(1)} %pad_add_fusion.at_ref, s32[1024,1]{1,0:T(8,128)S(1)} %copy.19.expert_ref, bf16[32,2,32,384]{3,2,1,0:T(8,128)(2,1)S(1)} %bitcast.29, bf16[2,384,512]{2,1,0:T(8,128)(2,1)S(1)} %copy-done.1, bf16[2,384,512]{2,1,0:T(8,128)(2,1)S(1)} %copy-done.3, ...), custom_call_target="tpu_custom_call" | custom-call | flops 1207959552 | bytes 6295560 | tf_op jit(solution)/shard_map/pallas_call | solution.py:35
  62.7 5.2 %collective-permute-start = (bf16[4,64,1536]{2,1,0:T(8,128)(2,1)S(1)}, bf16[4,64,1536]{2,1,0:T(8,128)(2,1)S(1)}, u32[]{:S(2)}, u32[]{:S(2)}) collective-permute-start(bf16[4,64,1536]{2,1,0:T(8,128)(2,1)S(1)} %get-tuple-element.15), channel_id=1, source_target_pairs={{0,32},{32,0},{1,33},{33,1},{2,34},{34,2},{3,35},{35,3},{4,36},{36... | collective-permute-start | bytes 2359304 | tf_op jit(solution)/shard_map/ppermute | solution.py:181
  67.9 2.6 %shard_map.111 = (f32[4,64,1536]{2,1,0:T(8,128)S(1)}, bf16[4,64,1536]{2,1,0:T(8,128)(2,1)S(1)}) custom-call(s32[2]{0:T(128)S(1)} %pad_add_fusion.at_ref, s32[1024,1]{1,0:T(8,128)S(1)} %copy.19.expert_ref, bf16[32,2,32,384]{3,2,1,0:T(8,128)(2,1)S(1)} %bitcast.30, bf16[2,384,512]{2,1,0:T(8,128)(2,1)S(1)} %copy-done.1, bf16[2,384,512]{2,1,0:T(8,128)(2,1)S(1)} %copy-done.3, ...), custom_call_target="tpu_custom_call" | custom-call | flops 1207959552 | bytes 6295560 | tf_op jit(solution)/shard_map/pallas_call | solution.py:35
  70.5 0.0 collective-permute-done
  70.6 0.2 add_convert_fusion.1
  70.8 0.1 fusion.9
  70.8 1.9 %collective-permute-start.1 = (bf16[4,64,1536]{2,1,0:T(8,128)(2,1)S(1)}, bf16[4,64,1536]{2,1,0:T(8,128)(2,1)S(1)}, u32[]{:S(2)}, u32[]{:S(2)}) collective-permute-start(bf16[4,64,1536]{2,1,0:T(8,128)(2,1)S(1)} %get-tuple-element.17), channel_id=1, source_target_pairs={{0,32},{32,0},{1,33},{33,1},{2,34},{34,2},{3,35},{35,3},{4,36},{36... | collective-permute-start | bytes 2359304 | tf_op jit(solution)/shard_map/ppermute | solution.py:186
  72.7 5.1 %collective-permute-start.3 = (bf16[4,64,768]{2,1,0:T(8,128)(2,1)S(1)}, bf16[4,64,768]{2,1,0:T(8,128)(2,1)S(1)}, u32[]{:S(2)}, u32[]{:S(2)}) collective-permute-start(bf16[4,64,768]{2,1,0:T(8,128)(2,1)S(1)} %get-tuple-element.19), channel_id=1, source_target_pairs={{0,448},{64,128},{128,64},{192,256},{256,192},{320,384},{384,320},... | collective-permute-start | bytes 1179656 | tf_op jit(solution)/shard_map/ppermute | solution.py:159
  77.9 1.9 %collective-permute-start.2 = (bf16[4,64,768]{2,1,0:T(8,128)(2,1)S(1)}, bf16[4,64,768]{2,1,0:T(8,128)(2,1)S(1)}, u32[]{:S(2)}, u32[]{:S(2)}) collective-permute-start(bf16[4,64,768]{2,1,0:T(8,128)(2,1)S(1)} %get-tuple-element.18), channel_id=1, source_target_pairs={{0,64},{64,0},{128,192},{192,128},{256,320},{320,256},{384,448},{4... | collective-permute-start | bytes 1179656 | tf_op jit(solution)/shard_map/ppermute | solution.py:159
  79.8 7.1 %collective-permute-done.3 = bf16[4,64,768]{2,1,0:T(8,128)(2,1)S(1)} collective-permute-done((bf16[4,64,768]{2,1,0:T(8,128)(2,1)S(1)}, bf16[4,64,768]{2,1,0:T(8,128)(2,1)S(1)}, u32[]{:S(2)}, u32[]{:S(2)}) %collective-permute-start.3) | collective-permute-done | bytes 393248 | tf_op jit(solution)/shard_map/ppermute | solution.py:159
  86.9 2.7 %collective-permute-done.2 = bf16[4,64,768]{2,1,0:T(8,128)(2,1)S(1)} collective-permute-done((bf16[4,64,768]{2,1,0:T(8,128)(2,1)S(1)}, bf16[4,64,768]{2,1,0:T(8,128)(2,1)S(1)}, u32[]{:S(2)}, u32[]{:S(2)}) %collective-permute-start.2) | collective-permute-done | bytes 393248 | tf_op jit(solution)/shard_map/ppermute | solution.py:159
  89.6 0.0 collective-permute-done.1
  89.6 0.3 add_convert_fusion
  89.9 23.1 %all_to_all.26 = bf16[4,64,1536]{2,1,0:T(8,128)(2,1)S(1)} all-to-all(bf16[4,64,1536]{2,1,0:T(8,128)(2,1)S(1)} %add_convert_fusion), channel_id=1, replica_groups=mesh['yh'=4,'yl'=2,'core'=2,'x'=4,'z'=8] {'yh'}, dimensions={0} | all-to-all | bytes 1572864 | tf_op jit(solution)/shard_map/all_to_all | solution.py:149
  113.0 0.1 convert_reduce_fusion
  113.1 0.7 multiply_convert_fusion
  113.8 0.9 broadcast_in_dim.91
  114.7 4.7 %all-to-all-start.3 = ((bf16[4,64,1024]{2,1,0:T(8,128)(2,1)}), bf16[4,64,1024]{2,1,0:T(8,128)(2,1)S(1)}, u32[]{:S(2)}, u32[]{:S(2)}) async-start(bf16[4,64,1024]{2,1,0:T(8,128)(2,1)} %broadcast_in_dim.91), calls=%async_computation.3 | async-start | bytes 1048576 | tf_op jit(solution)/shard_map/all_to_all | solution.py:149
  119.4 0.7 all-gather.2.cloned.1.call-update
  120.1 10.4 %all-to-all-done.3.mine_ref = bf16[4,64,1024]{2,1,0:T(8,128)(2,1)S(1)} async-done(((bf16[4,64,1024]{2,1,0:T(8,128)(2,1)}), bf16[4,64,1024]{2,1,0:T(8,128)(2,1)S(1)}, u32[]{:S(2)}, u32[]{:S(2)}) %all-to-all-start.3) | async-done | bytes 524320 | tf_op jit(solution)/shard_map/all_to_all | solution.py:149
  130.5 1.9 %collective-permute-start.4 = (bf16[4,64,512]{2,1,0:T(8,128)(2,1)S(1)}, bf16[4,64,512]{2,1,0:T(8,128)(2,1)S(1)}, u32[]{:S(2)}, u32[]{:S(2)}) collective-permute-start(bf16[4,64,512]{2,1,0:T(8,128)(2,1)S(1)} %get-tuple-element.31), channel_id=1, source_target_pairs={{0,64},{64,0},{128,192},{192,128},{256,320},{320,256},{384,448},{4... | collective-permute-start | bytes 786440 | tf_op jit(solution)/shard_map/ppermute | solution.py:159
  132.4 3.1 %collective-permute-start.5 = (bf16[4,64,512]{2,1,0:T(8,128)(2,1)S(1)}, bf16[4,64,512]{2,1,0:T(8,128)(2,1)S(1)}, u32[]{:S(2)}, u32[]{:S(2)}) collective-permute-start(bf16[4,64,512]{2,1,0:T(8,128)(2,1)S(1)} %get-tuple-element.30), channel_id=1, source_target_pairs={{0,448},{64,128},{128,64},{192,256},{256,192},{320,384},{384,320},... | collective-permute-start | bytes 786440 | tf_op jit(solution)/shard_map/ppermute | solution.py:159
  135.6 7.8 %collective-permute-start.7 = (bf16[4,64,1024]{2,1,0:T(8,128)(2,1)S(1)}, bf16[4,64,1024]{2,1,0:T(8,128)(2,1)S(1)}, u32[]{:S(2)}, u32[]{:S(2)}) collective-permute-start(bf16[4,64,1024]{2,1,0:T(8,128)(2,1)S(1)} %all-to-all-done.3.mine_ref), channel_id=1, source_target_pairs={{0,32},{32,0},{1,33},{33,1},{2,34},{34,2},{3,35},{35,3},{4,36},{36... | collective-permute-start | bytes 1572872 | tf_op jit(solution)/shard_map/ppermute | solution.py:197
  143.4 0.0 collective-permute-done.5
  143.5 7.2 %collective-permute-start.6 = (bf16[4,64,1024]{2,1,0:T(8,128)(2,1)S(1)}, bf16[4,64,1024]{2,1,0:T(8,128)(2,1)S(1)}, u32[]{:S(2)}, u32[]{:S(2)}) collective-permute-start(bf16[4,64,1024]{2,1,0:T(8,128)(2,1)S(1)} %constant_dynamic-update-slice_fusion.mine_ref.far_mine_ref), channel_id=1, source_target_pairs={{0,32},{32,0},{1,33},{33,1},{2,34},{34,2},{3,35},{35,3},{4,36},{36... | collective-permute-start | bytes 1572872 | tf_op jit(solution)/shard_map/ppermute | solution.py:202
  150.7 0.0 copy-start.2
  150.7 0.0 copy-start.4
  150.7 1.3 fusion.8
  152.0 0.6 copy-done.4
  152.7 2.0 %shard_map.113.refs_0_ = bf16[4,128,384]{2,1,0:T(8,128)(2,1)S(1)} custom-call(s32[2]{0:T(128)S(1)} %pad_add_fusion.at_ref, s32[1024,1]{1,0:T(8,128)S(1)} %copy.19.expert_ref, bf16[2,384,512]{2,1,0:T(8,128)(2,1)S(1)} %copy-done.2, bf16[2,384,512]{2,1,0:T(8,128)(2,1)S(1)} %copy-done.4, bf16[4,64,1024]{2,1,0:T(8,128)(2,1)S(1)} %all-to-all-done.3.mine_ref, ...), custom_call_target="tpu_custom_call" | custom-call | flops 805306368 | bytes 3018760 | tf_op jit(solution)/shard_map/pallas_call | solution.py:35
  154.7 0.0 collective-permute-done.6.other_ref.far_other_ref
  154.7 3.0 %shard_map.114 = bf16[4,2,128,384]{3,2,1,0:T(8,128)(2,1)} custom-call(s32[2]{0:T(128)S(1)} %pad_add_fusion.at_ref, s32[1024,1]{1,0:T(8,128)S(1)} %copy.19.expert_ref, bf16[2,384,512]{2,1,0:T(8,128)(2,1)S(1)} %copy-done.2, bf16[2,384,512]{2,1,0:T(8,128)(2,1)S(1)} %copy-done.4, ...), custom_call_target="tpu_custom_call" | custom-call | flops 805306368 | bytes 3805192 | tf_op jit(solution)/shard_map/pallas_call | solution.py:35
  157.7 3.9 %all-to-all-start.4 = ((bf16[32,32,384]{2,1,0:T(8,128)(2,1)}), bf16[32,32,384]{2,1,0:T(8,128)(2,1)S(1)}, u32[]{:S(2)}, u32[]{:S(2)}) async-start(bf16[32,32,384]{2,1,0:T(8,128)(2,1)} %bitcast.8), calls=%async_computation.4 | async-start | bytes 1572864 | tf_op jit(solution)/shard_map/all_to_all | solution.py:149
  161.6 0.0 copy-start.10
  161.6 2.9 %bitcast_select_fusion.3 = (bf16[1024,384]{1,0:T(8,128)(2,1)S(1)}, bf16[1024,384]{1,0:T(8,128)(2,1)S(1)}, bf16[1024,384]{1,0:T(8,128)(2,1)}, bf16[1024,384]{1,0:T(8,128)(2,1)}) fusion(bf16[32,1,32,384]{3,2,1,0:T(8,128)(2,1)} %get-tuple-element.23, pred[1024]{0:T(1024)(128)(4,1)S(1)} %get-tuple-element.35, pred[1024]{0:T(1024)(128)(4,1)S(1)} %get-tuple-element.36, ...), kind=kLoop, calls=%fused_computation.18 | loop fusion | flops 1572864 | bytes 4720640 | tf_op jit(solution)/shard_map/jit(_where)/select_n | solution.py:215
  164.6 0.0 copy-start.14
  164.6 0.7 shard_map.116
  165.3 0.2 copy-done.12
  165.4 0.2 copy-done.14
  165.7 0.9 copy-done.7
  166.6 1.9 convolution_convert_fusion.1
  168.5 2.1 %fusion.1 = bf16[1,512,384]{2,1,0:T(8,128)(2,1)S(1)} fusion(bf16[1024,512]{1,0:T(8,128)(2,1)} %all-gather.2.cloned.1.call-done, bf16[1024,384]{1,0:T(8,128)(2,1)S(1)} %copy-done.17), kind=kOutput, calls=%fused_computation.11 | convolution fusion | flops 402849792 | bytes 2228224 | tf_op jit(solution)/shard_map/dot_general | solution.py:18
  170.7 0.0 copy-start.15
  170.7 0.7 fusion
  171.4 1.0 pad_maximum_fusion.3
  172.4 0.0 copy-done.13
  172.4 0.5 copy-done.15
  172.9 1.9 convolution_convert_fusion
  174.8 8.4 %all-to-all-done.4.x_ref = bf16[32,32,384]{2,1,0:T(8,128)(2,1)S(1)} async-done(((bf16[32,32,384]{2,1,0:T(8,128)(2,1)}), bf16[32,32,384]{2,1,0:T(8,128)(2,1)S(1)}, u32[]{:S(2)}, u32[]{:S(2)}) %all-to-all-start.4) | async-done | bytes 786464 | tf_op jit(solution)/shard_map/all_to_all | solution.py:149
  183.3 0.7 shard_map.115
  (37 shorter events, 0.2 us)
Async XLA Ops:
  7.2 32.3 %copy-start = (s32[8,1]{0,1:T(1,128)S(1)}, s32[8,1]{0,1:T(1,128)}, u32[]{:S(2)}) copy-start(s32[8,1]{0,1:T(1,128)} %param.14) | copy-start | bytes 100
  35.3 4.2 %copy-start.18 = (s32[1024]{0:T(1024)S(1)}, s32[1024]{0:T(1024)}, u32[]{:S(2)}) copy-start(s32[1024]{0:T(1024)} %param.13) | copy-start | bytes 12292
  35.3 22.5 %copy-start.1 = (bf16[2,384,512]{2,1,0:T(8,128)(2,1)S(1)}, bf16[2,384,512]{2,1,0:T(8,128)(2,1)}, u32[]{:S(2)}) copy-start(bf16[2,384,512]{2,1,0:T(8,128)(2,1)} %gate_ref.3) | copy-start | bytes 2359300
  35.3 22.5 %all-to-all-start.1 = ((bf16[4,8,2,32,384]{4,3,2,1,0:T(8,128)(2,1)}), bf16[4,8,2,32,384]{4,3,2,1,0:T(8,128)(2,1)S(1)}, u32[]{:S(2)}, u32[]{:S(2)}) async-start(bf16[4,8,2,32,384]{4,3,2,1,0:T(8,128)(2,1)} %broadcast_in_dim.90), calls=%async_computation.1 | async-start | bytes 3145728 | tf_op jit(solution)/shard_map/all_to_all | solution.py:149
  57.8 1.1 copy-start.3
  58.9 1.1 copy-start.11
  62.7 7.9 %collective-permute-start = (bf16[4,64,1536]{2,1,0:T(8,128)(2,1)S(1)}, bf16[4,64,1536]{2,1,0:T(8,128)(2,1)S(1)}, u32[]{:S(2)}, u32[]{:S(2)}) collective-permute-start(bf16[4,64,1536]{2,1,0:T(8,128)(2,1)S(1)} %get-tuple-element.15), channel_id=1, source_target_pairs={{0,32},{32,0},{1,33},{33,1},{2,34},{34,2},{3,35},{35,3},{4,36},{36... | collective-permute-start | bytes 2359304 | tf_op jit(solution)/shard_map/ppermute | solution.py:181
  70.8 18.8 %collective-permute-start.1 = (bf16[4,64,1536]{2,1,0:T(8,128)(2,1)S(1)}, bf16[4,64,1536]{2,1,0:T(8,128)(2,1)S(1)}, u32[]{:S(2)}, u32[]{:S(2)}) collective-permute-start(bf16[4,64,1536]{2,1,0:T(8,128)(2,1)S(1)} %get-tuple-element.17), channel_id=1, source_target_pairs={{0,32},{32,0},{1,33},{33,1},{2,34},{34,2},{3,35},{35,3},{4,36},{36... | collective-permute-start | bytes 2359304 | tf_op jit(solution)/shard_map/ppermute | solution.py:186
  72.7 14.1 %collective-permute-start.3 = (bf16[4,64,768]{2,1,0:T(8,128)(2,1)S(1)}, bf16[4,64,768]{2,1,0:T(8,128)(2,1)S(1)}, u32[]{:S(2)}, u32[]{:S(2)}) collective-permute-start(bf16[4,64,768]{2,1,0:T(8,128)(2,1)S(1)} %get-tuple-element.19), channel_id=1, source_target_pairs={{0,448},{64,128},{128,64},{192,256},{256,192},{320,384},{384,320},... | collective-permute-start | bytes 1179656 | tf_op jit(solution)/shard_map/ppermute | solution.py:159
  77.9 11.8 %collective-permute-start.2 = (bf16[4,64,768]{2,1,0:T(8,128)(2,1)S(1)}, bf16[4,64,768]{2,1,0:T(8,128)(2,1)S(1)}, u32[]{:S(2)}, u32[]{:S(2)}) collective-permute-start(bf16[4,64,768]{2,1,0:T(8,128)(2,1)S(1)} %get-tuple-element.18), channel_id=1, source_target_pairs={{0,64},{64,0},{128,192},{192,128},{256,320},{320,256},{384,448},{4... | collective-permute-start | bytes 1179656 | tf_op jit(solution)/shard_map/ppermute | solution.py:159
  114.7 15.8 %all-to-all-start.3 = ((bf16[4,64,1024]{2,1,0:T(8,128)(2,1)}), bf16[4,64,1024]{2,1,0:T(8,128)(2,1)S(1)}, u32[]{:S(2)}, u32[]{:S(2)}) async-start(bf16[4,64,1024]{2,1,0:T(8,128)(2,1)} %broadcast_in_dim.91), calls=%async_computation.3 | async-start | bytes 1048576 | tf_op jit(solution)/shard_map/all_to_all | solution.py:149
  119.4 49.2 %all-gather.2.cloned.1.call-start = ((), (), s32[]{:S(2)}) async-start(), calls=%async_computation.5 | async-start | bytes 1114112 | tf_op jit(solution)/shard_map/all_gather | solution.py:193
  130.5 12.9 %collective-permute-start.4 = (bf16[4,64,512]{2,1,0:T(8,128)(2,1)S(1)}, bf16[4,64,512]{2,1,0:T(8,128)(2,1)S(1)}, u32[]{:S(2)}, u32[]{:S(2)}) collective-permute-start(bf16[4,64,512]{2,1,0:T(8,128)(2,1)S(1)} %get-tuple-element.31), channel_id=1, source_target_pairs={{0,64},{64,0},{128,192},{192,128},{256,320},{320,256},{384,448},{4... | collective-permute-start | bytes 786440 | tf_op jit(solution)/shard_map/ppermute | solution.py:159
  132.4 11.0 %collective-permute-start.5 = (bf16[4,64,512]{2,1,0:T(8,128)(2,1)S(1)}, bf16[4,64,512]{2,1,0:T(8,128)(2,1)S(1)}, u32[]{:S(2)}, u32[]{:S(2)}) collective-permute-start(bf16[4,64,512]{2,1,0:T(8,128)(2,1)S(1)} %get-tuple-element.30), channel_id=1, source_target_pairs={{0,448},{64,128},{128,64},{192,256},{256,192},{320,384},{384,320},... | collective-permute-start | bytes 786440 | tf_op jit(solution)/shard_map/ppermute | solution.py:159
  135.6 16.4 %collective-permute-start.7 = (bf16[4,64,1024]{2,1,0:T(8,128)(2,1)S(1)}, bf16[4,64,1024]{2,1,0:T(8,128)(2,1)S(1)}, u32[]{:S(2)}, u32[]{:S(2)}) collective-permute-start(bf16[4,64,1024]{2,1,0:T(8,128)(2,1)S(1)} %all-to-all-done.3.mine_ref), channel_id=1, source_target_pairs={{0,32},{32,0},{1,33},{33,1},{2,34},{34,2},{3,35},{35,3},{4,36},{36... | collective-permute-start | bytes 1572872 | tf_op jit(solution)/shard_map/ppermute | solution.py:197
  143.5 11.3 %collective-permute-start.6 = (bf16[4,64,1024]{2,1,0:T(8,128)(2,1)S(1)}, bf16[4,64,1024]{2,1,0:T(8,128)(2,1)S(1)}, u32[]{:S(2)}, u32[]{:S(2)}) collective-permute-start(bf16[4,64,1024]{2,1,0:T(8,128)(2,1)S(1)} %constant_dynamic-update-slice_fusion.mine_ref.far_mine_ref), channel_id=1, source_target_pairs={{0,32},{32,0},{1,33},{33,1},{2,34},{34,2},{3,35},{35,3},{4,36},{36... | collective-permute-start | bytes 1572872 | tf_op jit(solution)/shard_map/ppermute | solution.py:202
  150.7 1.3 copy-start.2
  150.7 1.9 %copy-start.4 = (bf16[2,384,512]{2,1,0:T(8,128)(2,1)S(1)}, bf16[2,384,512]{2,1,0:T(8,128)(2,1)}, u32[]{:S(2)}) copy-start(bf16[2,384,512]{2,1,0:T(8,128)(2,1)} %up_ref.3) | copy-start | bytes 2359300
  152.7 2.1 %copy-start.9 = (bf16[4,64,1024]{2,1,0:T(8,128)(2,1)}, bf16[4,64,1024]{2,1,0:T(8,128)(2,1)S(1)}, u32[]{:S(2)}) copy-start(bf16[4,64,1024]{2,1,0:T(8,128)(2,1)S(1)} %collective-permute-done.7.other_ref) | copy-start | bytes 1572868
  154.7 3.0 %copy-start.5 = (bf16[4,64,1024]{2,1,0:T(8,128)(2,1)}, bf16[4,64,1024]{2,1,0:T(8,128)(2,1)S(1)}, u32[]{:S(2)}) copy-start(bf16[4,64,1024]{2,1,0:T(8,128)(2,1)S(1)} %collective-permute-done.6.other_ref.far_other_ref) | copy-start | bytes 1572868
  157.7 25.6 %all-to-all-start.4 = ((bf16[32,32,384]{2,1,0:T(8,128)(2,1)}), bf16[32,32,384]{2,1,0:T(8,128)(2,1)S(1)}, u32[]{:S(2)}, u32[]{:S(2)}) async-start(bf16[32,32,384]{2,1,0:T(8,128)(2,1)} %bitcast.8), calls=%async_computation.4 | async-start | bytes 1572864 | tf_op jit(solution)/shard_map/all_to_all | solution.py:149
  161.6 2.9 %copy-start.6 = (bf16[4,64,1024]{2,1,0:T(8,128)(2,1)S(1)}, bf16[4,64,1024]{2,1,0:T(8,128)(2,1)}, u32[]{:S(2)}) copy-start(bf16[4,64,1024]{2,1,0:T(8,128)(2,1)} %copy-done.5) | copy-start | bytes 1572868
  161.6 2.9 %copy-start.10 = (bf16[4,64,1024]{2,1,0:T(8,128)(2,1)S(1)}, bf16[4,64,1024]{2,1,0:T(8,128)(2,1)}, u32[]{:S(2)}) copy-start(bf16[4,64,1024]{2,1,0:T(8,128)(2,1)} %copy-done.9) | copy-start | bytes 1572868
  164.6 0.9 copy-start.12
  164.6 1.1 copy-start.14
  165.3 1.3 copy-start.7
  166.6 1.9 copy-start.17
  168.5 2.1 %copy-start.16 = (bf16[1024,384]{1,0:T(8,128)(2,1)S(1)}, bf16[1024,384]{1,0:T(8,128)(2,1)}, u32[]{:S(2)}) copy-start(bf16[1024,384]{1,0:T(8,128)(2,1)} %get-tuple-element.38) | copy-start | bytes 2359300
  168.5 2.1 %copy-start.19 = (bf16[1024,512]{1,0:T(8,128)(2,1)S(1)}, bf16[1024,512]{1,0:T(8,128)(2,1)}, u32[]{:S(2)}) copy-start(bf16[1024,512]{1,0:T(8,128)(2,1)} %all-gather.2.cloned.1.call-done) | copy-start | bytes 3145732
  170.7 1.8 copy-start.8
  170.7 1.8 copy-start.13
  170.7 2.3 %copy-start.15 = (bf16[1024,384]{1,0:T(8,128)(2,1)S(1)}, bf16[1024,384]{1,0:T(8,128)(2,1)}, u32[]{:S(2)}) copy-start(bf16[1024,384]{1,0:T(8,128)(2,1)} %copy-done.14) | copy-start | bytes 2359300
Sparse Core Ops, SparseCore 0:
  122.3 39.0 all-gather.1

commit v6 on v5

--- a/solution.py
+++ b/solution.py
@@ -11,7 +11,7 @@
 BF = jnp.bfloat16
 F32 = jnp.float32
 ROWS = 256
-VMEM_BYTES = 20 * 2**20
+VMEM_BYTES = 14 * 2**20
 
 
 def dot(a, b, ca, cb):
@@ -46,9 +46,9 @@
     return [jnp.where(expert == e, rows, jnp.zeros_like(rows)) for e in range(experts)]
 
 
-def forward_body(side, at_ref, expert_ref, got_ref, wg_ref, wu_ref, wd_ref, keep_ref, give_ref):
+def forward_body(side, at_ref, expert_ref, got_ref, pair_ref, wd_ref, keep_ref, *give_refs):
     n_yh, part, width = keep_ref.shape
-    experts = wg_ref.shape[0]
+    experts = wd_ref.shape[0]
     _, _, own, cols = got_ref.shape
     hid = width // 3
     parity, core = lax.rem(at_ref[0] + side, 2), at_ref[1]
@@ -66,7 +66,8 @@
         for kind in range(2):
             rows = [got_ref[pl.ds(s * owners, owners), kind].reshape(per, cols) for s in starts]
             masked.append(by_expert(jnp.concatenate(rows), expert, experts))
-        for k, w_ref in enumerate((wg_ref, wu_ref, wd_ref)):
+        for k in range(3):
+            w_ref = wd_ref if k == 2 else pair_ref.at[k]
             out = 0.0
             for e in range(experts):
                 out = out + dot(masked[k // 2][e], w_ref[e], 1, k // 2)
@@ -75,13 +76,17 @@
                 even = out[q * per : q * per + part]
                 odd = out[q * per + part : (q + 1) * per]
                 keep_ref[i * group + q, :, to] = jnp.where(core == 0, even, odd)
-                give_ref[i * group + q, :, to] = jnp.where(core == 0, odd, even).astype(BF)
-
-
-def terms_body(side, at_ref, expert_ref, gate_ref, up_ref, mine_ref, other_ref, *refs):
+                give = jnp.where(core == 0, odd, even).astype(BF)
+                if len(give_refs) == 1:
+                    give_refs[0][i * group + q, :, to] = give
+                else:
+                    give_refs[k][i * group + q] = give
+
+
+def terms_body(side, at_ref, expert_ref, pair_ref, mine_ref, other_ref, *refs):
     out_ref = refs[-1]
     n_yh, part, width = mine_ref.shape
-    experts, _, hid = gate_ref.shape
+    _, experts, _, hid = pair_ref.shape
     parity, core = lax.rem(at_ref[0] + side, 2), at_ref[1]
     per = 2 * part
     group = ROWS // per
@@ -99,7 +104,7 @@
         ups = by_expert(rows[:, hid:], expert, experts)
         out = 0.0
         for e in range(experts):
-            out = out + dot(gates[e], gate_ref[e], 1, 1) + dot(ups[e], up_ref[e], 1, 1)
+            out = out + dot(gates[e], pair_ref[0, e], 1, 1) + dot(ups[e], pair_ref[1, e], 1, 1)
         out = out.astype(BF)
         for q in range(group):
             piece = out[q * per : (q + 1) * per]
@@ -159,31 +164,32 @@
             return lax.ppermute(v[0], along_y, left), lax.ppermute(v[1], along_y, right)
 
         first = (lax.axis_index("x") * n_z + lax.axis_index("z")) * own
-        holds_own = row_token[None, :] == first + jnp.arange(own, dtype=jnp.int32)[:, None]
-        weight_own = jnp.sum(jnp.where(holds_own, gate_weight[None, :], 0.0), axis=1)
         expert_row = jnp.repeat(block_expert[:, 0], blk)
         holds = row_token[None, :] == jnp.arange(n_tok, dtype=jnp.int32)[:, None]
         expert_tok = jnp.sum(jnp.where(holds, expert_row[None, :], 0), axis=1)[:, None]
 
+        holds_own = row_token[None, :] == first + jnp.arange(own, dtype=jnp.int32)[:, None]
+        weight_own = jnp.sum(jnp.where(holds_own, gate_weight[None, :], 0.0), axis=1)
         cot_own = (cotangent.astype(F32) * weight_own[:, None]).astype(BF)
         got = exchange(spread(jnp.stack([tokens, cot_own]), n_z), "z")
+        pair = jnp.stack([w_gate, w_up])
         got = exchange(spread(got.reshape(n_z, 2, own, cols), n_x), "x")
         got = got.reshape(n_cuts, 2, own, cols)
 
-        shape = (n_yh, part, 3 * hid)
-        outs = [jax.ShapeDtypeStruct(shape, F32), jax.ShapeDtypeStruct(shape, BF)]
-
-        def forward(side):
-            args = (at, expert_tok, got, w_gate, w_up, w_down)
+        def forward(side, pieces):
+            width = 3 * hid // pieces
+            outs = [jax.ShapeDtypeStruct((n_yh, part, 3 * hid), F32)]
+            outs += [jax.ShapeDtypeStruct((n_yh, part, width), BF)] * pieces
+            args = (at, expert_tok, got, pair, w_down)
             return call(functools.partial(forward_body, side), outs, 3 * work // 2, args)
 
-        far_keep, far_give = forward(1)
+        far_keep, far_give = forward(1, 1)
         far_came = lax.ppermute(far_give, "core", swap)
-        keep, give = forward(0)
+        keep, *give = forward(0, 3)
         far = halves((far_keep + far_came.astype(F32)).astype(BF))
         far, give = lax.optimization_barrier((far, give))
         near = neighbours(far)
-        came = lax.ppermute(give, "core", swap)
+        came = jnp.concatenate([lax.ppermute(g, "core", swap) for g in give], axis=-1)
         chips = keep + came.astype(F32) + jnp.concatenate(near, axis=-1).astype(F32)
         chips = chips.astype(BF)
         pre = jnp.sum(exchange(chips, "yh").astype(F32), axis=0)
@@ -196,12 +202,12 @@
         near = neighbours(halves(grads))
         other = lax.ppermute(grads, "core", swap)
         outs = [jax.ShapeDtypeStruct((n_yh, n_core * part, cols), BF)]
-        args = (at, expert_tok, w_gate, w_up, grads, other)
+        args = (at, expert_tok, pair, grads, other)
         (own_terms,) = call(functools.partial(terms_body, 0), outs, work, args)
         far = jnp.concatenate(near, axis=-1)
         far_other = lax.ppermute(far, "core", swap)
         outs = [jax.ShapeDtypeStruct((n_yh, n_yl, n_core * part, cols), BF)]
-        args = (at, expert_tok, w_gate, w_up, far, far_other, own_terms)
+        args = (at, expert_tok, pair, far, far_other, own_terms)
         (terms,) = call(functools.partial(terms_body, 1), outs, work, args)
         terms = exchange(terms.reshape(n_cuts, own, cols), cuts)
         outs = [jax.ShapeDtypeStruct((own, cols), BF)]

time: 192 us -> 190 us (0.990)
  waiting for transfers between devices: 46.8 us -> 39.4 us
  starting transfers between devices: 47 us -> 50.5 us
    ppermute x2, waiting for transfers between devices: 7.1 us -> 0.01 us  [neighbours(): lax.ppermute(v[1], along_y, right)]
    ppermute x1 -> x3, starting transfers between devices: 1.92 us -> 6.53 us  [per_device(): lax.ppermute(g, 'core', swap)]
    unnamed x41 -> x37, local copies, waits for them, and re-layouts: 4.84 us -> 4.48 us
  transfers between devices with their start and end apart: 12 -> 14, of which waited for: 5 -> 5; matrix products, arithmetic and copies ran while one was open for 7% -> 8% of each run, Pallas kernels for 4% -> 4%
where the time goes in v6:
time: 190 us; the launch traced here: 189 us
  starting transfers between devices  50.5 us (27%)
  blocking collectives  47.2 us (25%)
  waiting for transfers between devices  39.4 us (21%)
  between operations  14.4 us (8%)
  Pallas kernels  11.7 us (6%)
  other arithmetic  9.72 us (5%)
  local copies, waits for them, and re-layouts  9.32 us (5%)
  matrix products  6.61 us (3%)
    all_to_all x2, blocking collectives, exchange(): return lax.all_to_all(v, axes, split_axis=0, concat_axis=0, tiled=True)  47.2 us
    all_to_all x3, waiting for transfers between devices, exchange(): return lax.all_to_all(v, axes, split_axis=0, concat_axis=0, tiled=True)  34.9 us
    all_to_all x3, starting transfers between devices, exchange(): return lax.all_to_all(v, axes, split_axis=0, concat_axis=0, tiled=True)  13.1 us
    pallas_call x6, Pallas kernels, call(): pl.pallas_call(body, out_shape=outs, in_specs=in_specs, out_specs=[pl.Blo...  11.7 us
    ppermute x2, starting transfers between devices, neighbours(): lax.ppermute(v[1], along_y, right)  8.25 us
    ppermute x1, starting transfers between devices, per_device(): other = lax.ppermute(grads, 'core', swap)  6.84 us
    dot_general x4, matrix products, dot(): lax.dot_general(a, b, (((ca,), (cb,)), ((), ())), preferred_element_type=...  6.61 us
    ppermute x1, starting transfers between devices, per_device(): far_other = lax.ppermute(far, 'core', swap)  6.56 us
  transfers between devices with their start and end apart: 14, of which 5 were waited for; matrix products, arithmetic and copies ran while one was open for 8% of the time, Pallas kernels for 4%

profile of v6, /device:TPU:1, one launch (start us, length us, event | category | flops | bytes accessed | tf_op | source)
XLA Modules:
  0.0 188.9 jit_solution(8160326392378448806)
XLA Ops:
  7.2 0.0 copy-start
  7.2 0.9 select_reduce_fusion.1
  8.1 0.8 fusion.5
  8.9 0.7 pad_maximum_fusion.6
  9.7 24.2 %all_to_all.25 = bf16[8,2,32,384]{3,2,1,0:T(8,128)(2,1)S(1)} all-to-all(bf16[8,2,32,384]{3,2,1,0:T(8,128)(2,1)S(1)} %broadcast_in_dim.89), channel_id=1, replica_groups=mesh['yh'=4,'yl'=2,'core'=2,'x'=4,'z'=8] {'z'}, dimensions={0} | all-to-all | bytes 786432 | tf_op jit(solution)/shard_map/all_to_all | solution.py:154
  33.9 1.4 broadcast_in_dim.90
  35.3 4.1 %all-to-all-start.1 = ((bf16[4,8,2,32,384]{4,3,2,1,0:T(8,128)(2,1)}), bf16[4,8,2,32,384]{4,3,2,1,0:T(8,128)(2,1)S(1)}, u32[]{:S(2)}, u32[]{:S(2)}) async-start(bf16[4,8,2,32,384]{4,3,2,1,0:T(8,128)(2,1)} %broadcast_in_dim.90), calls=%async_computation.1 | async-start | bytes 3145728 | tf_op jit(solution)/shard_map/all_to_all | solution.py:154
  39.5 0.1 broadcast_bitcast_fusion
  39.5 0.5 select_reduce_fusion
  40.0 1.0 copy.19.expert_ref
  41.1 0.1 pad_add_fusion.at_ref
  41.1 1.5 pad_maximum_fusion.pair_ref
  42.7 15.1 %all-to-all-done.1 = bf16[4,8,2,32,384]{4,3,2,1,0:T(8,128)(2,1)S(1)} async-done(((bf16[4,8,2,32,384]{4,3,2,1,0:T(8,128)(2,1)}), bf16[4,8,2,32,384]{4,3,2,1,0:T(8,128)(2,1)S(1)}, u32[]{:S(2)}, u32[]{:S(2)}) %all-to-all-start.1) | async-done | bytes 1572896 | tf_op jit(solution)/shard_map/all_to_all | solution.py:154
  57.8 1.4 copy-done.3
  59.2 1.1 copy-done.9
  60.3 2.6 %shard_map.112 = (f32[4,64,1536]{2,1,0:T(8,128)S(1)}, bf16[4,64,1536]{2,1,0:T(8,128)(2,1)S(1)}) custom-call(s32[2]{0:T(128)S(1)} %pad_add_fusion.at_ref, s32[1024,1]{1,0:T(8,128)S(1)} %copy-done.3, bf16[32,2,32,384]{3,2,1,0:T(8,128)(2,1)S(1)} %bitcast.31, bf16[2,2,384,512]{3,2,1,0:T(8,128)(2,1)S(1)} %pad_maximum_fusion.pair_ref, ...), custom_call_target="tpu_custom_call" | custom-call | flops 1207959552 | bytes 6295560 | tf_op jit(solution)/shard_map/pallas_call | solution.py:35
  63.0 5.2 %collective-permute-start = (bf16[4,64,1536]{2,1,0:T(8,128)(2,1)S(1)}, bf16[4,64,1536]{2,1,0:T(8,128)(2,1)S(1)}, u32[]{:S(2)}, u32[]{:S(2)}) collective-permute-start(bf16[4,64,1536]{2,1,0:T(8,128)(2,1)S(1)} %get-tuple-element.19), channel_id=1, source_target_pairs={{0,32},{32,0},{1,33},{33,1},{2,34},{34,2},{3,35},{35,3},{4,36},{36... | collective-permute-start | bytes 2359304 | tf_op jit(solution)/shard_map/ppermute | solution.py:187
  68.2 2.6 %shard_map.111 = (f32[4,64,1536]{2,1,0:T(8,128)S(1)}, bf16[4,64,512]{2,1,0:T(8,128)(2,1)S(1)}, bf16[4,64,512]{2,1,0:T(8,128)(2,1)S(1)}, bf16[4,64,512]{2,1,0:T(8,128)(2,1)S(1)}) custom-call(s32[2]{0:T(128)S(1)} %pad_add_fusion.at_ref, s32[1024,1]{1,0:T(8,128)S(1)} %copy-done.3, bf16[32,2,32,384]{3,2,1,0:T(8,128)(2,1)S(1)} %bitcast.32, ...), custom_call_target="tpu_custom_call" | custom-call | flops 1207959552 | bytes 6295560 | tf_op jit(solution)/shard_map/pallas_call | solution.py:35
  70.8 0.2 add_convert_fusion.1
  71.1 0.1 fusion.9
  71.1 5.1 %collective-permute-start.5 = (bf16[4,64,768]{2,1,0:T(8,128)(2,1)S(1)}, bf16[4,64,768]{2,1,0:T(8,128)(2,1)S(1)}, u32[]{:S(2)}, u32[]{:S(2)}) collective-permute-start(bf16[4,64,768]{2,1,0:T(8,128)(2,1)S(1)} %get-tuple-element.27), channel_id=1, source_target_pairs={{0,448},{64,128},{128,64},{192,256},{256,192},{320,384},{384,320},... | collective-permute-start | bytes 1179656 | tf_op jit(solution)/shard_map/ppermute | solution.py:164
  76.2 1.9 %collective-permute-start.4 = (bf16[4,64,768]{2,1,0:T(8,128)(2,1)S(1)}, bf16[4,64,768]{2,1,0:T(8,128)(2,1)S(1)}, u32[]{:S(2)}, u32[]{:S(2)}) collective-permute-start(bf16[4,64,768]{2,1,0:T(8,128)(2,1)S(1)} %get-tuple-element.26), channel_id=1, source_target_pairs={{0,64},{64,0},{128,192},{192,128},{256,320},{320,256},{384,448},{4... | collective-permute-start | bytes 1179656 | tf_op jit(solution)/shard_map/ppermute | solution.py:164
  78.2 2.2 %collective-permute-start.3 = (bf16[4,64,512]{2,1,0:T(8,128)(2,1)S(1)}, bf16[4,64,512]{2,1,0:T(8,128)(2,1)S(1)}, u32[]{:S(2)}, u32[]{:S(2)}) collective-permute-start(bf16[4,64,512]{2,1,0:T(8,128)(2,1)S(1)} %get-tuple-element.25), channel_id=1, source_target_pairs={{0,32},{32,0},{1,33},{33,1},{2,34},{34,2},{3,35},{35,3},{4,36},{36... | collective-permute-start | bytes 786440 | tf_op jit(solution)/shard_map/ppermute | solution.py:192
  80.4 2.1 %collective-permute-start.2 = (bf16[4,64,512]{2,1,0:T(8,128)(2,1)S(1)}, bf16[4,64,512]{2,1,0:T(8,128)(2,1)S(1)}, u32[]{:S(2)}, u32[]{:S(2)}) collective-permute-start(bf16[4,64,512]{2,1,0:T(8,128)(2,1)S(1)} %get-tuple-element.24), channel_id=1, source_target_pairs={{0,32},{32,0},{1,33},{33,1},{2,34},{34,2},{3,35},{35,3},{4,36},{36... | collective-permute-start | bytes 786440 | tf_op jit(solution)/shard_map/ppermute | solution.py:192
  82.5 2.2 %collective-permute-start.1 = (bf16[4,64,512]{2,1,0:T(8,128)(2,1)S(1)}, bf16[4,64,512]{2,1,0:T(8,128)(2,1)S(1)}, u32[]{:S(2)}, u32[]{:S(2)}) collective-permute-start(bf16[4,64,512]{2,1,0:T(8,128)(2,1)S(1)} %get-tuple-element.23), channel_id=1, source_target_pairs={{0,32},{32,0},{1,33},{33,1},{2,34},{34,2},{3,35},{35,3},{4,36},{36... | collective-permute-start | bytes 786440 | tf_op jit(solution)/shard_map/ppermute | solution.py:192
  84.7 1.2 collective-permute-done.1
  85.9 2.6 %collective-permute-done.4 = bf16[4,64,768]{2,1,0:T(8,128)(2,1)S(1)} collective-permute-done((bf16[4,64,768]{2,1,0:T(8,128)(2,1)S(1)}, bf16[4,64,768]{2,1,0:T(8,128)(2,1)S(1)}, u32[]{:S(2)}, u32[]{:S(2)}) %collective-permute-start.4) | collective-permute-done | bytes 393248 | tf_op jit(solution)/shard_map/ppermute | solution.py:164
  88.5 0.3 add_convert_fusion
  88.8 23.1 %all_to_all.26 = bf16[4,64,1536]{2,1,0:T(8,128)(2,1)S(1)} all-to-all(bf16[4,64,1536]{2,1,0:T(8,128)(2,1)S(1)} %add_convert_fusion), channel_id=1, replica_groups=mesh['yh'=4,'yl'=2,'core'=2,'x'=4,'z'=8] {'yh'}, dimensions={0} | all-to-all | bytes 1572864 | tf_op jit(solution)/shard_map/all_to_all | solution.py:154
  111.9 0.1 convert_reduce_fusion
  112.0 0.7 multiply_convert_fusion
  112.7 0.9 broadcast_in_dim.91
  113.6 5.0 %all-to-all-start.3 = ((bf16[4,64,1024]{2,1,0:T(8,128)(2,1)}), bf16[4,64,1024]{2,1,0:T(8,128)(2,1)S(1)}, u32[]{:S(2)}, u32[]{:S(2)}) async-start(bf16[4,64,1024]{2,1,0:T(8,128)(2,1)} %broadcast_in_dim.91), calls=%async_computation.3 | async-start | bytes 1048576 | tf_op jit(solution)/shard_map/all_to_all | solution.py:154
  118.6 0.7 all-gather.2.cloned.1.call-update
  119.3 11.3 %all-to-all-done.3.mine_ref = bf16[4,64,1024]{2,1,0:T(8,128)(2,1)S(1)} async-done(((bf16[4,64,1024]{2,1,0:T(8,128)(2,1)}), bf16[4,64,1024]{2,1,0:T(8,128)(2,1)S(1)}, u32[]{:S(2)}, u32[]{:S(2)}) %all-to-all-start.3) | async-done | bytes 524320 | tf_op jit(solution)/shard_map/all_to_all | solution.py:154
  130.7 2.1 %collective-permute-start.6 = (bf16[4,64,512]{2,1,0:T(8,128)(2,1)S(1)}, bf16[4,64,512]{2,1,0:T(8,128)(2,1)S(1)}, u32[]{:S(2)}, u32[]{:S(2)}) collective-permute-start(bf16[4,64,512]{2,1,0:T(8,128)(2,1)S(1)} %get-tuple-element.39), channel_id=1, source_target_pairs={{0,64},{64,0},{128,192},{192,128},{256,320},{320,256},{384,448},{4... | collective-permute-start | bytes 786440 | tf_op jit(solution)/shard_map/ppermute | solution.py:164
  132.7 3.2 %collective-permute-start.7 = (bf16[4,64,512]{2,1,0:T(8,128)(2,1)S(1)}, bf16[4,64,512]{2,1,0:T(8,128)(2,1)S(1)}, u32[]{:S(2)}, u32[]{:S(2)}) collective-permute-start(bf16[4,64,512]{2,1,0:T(8,128)(2,1)S(1)} %get-tuple-element.38), channel_id=1, source_target_pairs={{0,448},{64,128},{128,64},{192,256},{256,192},{320,384},{384,320},... | collective-permute-start | bytes 786440 | tf_op jit(solution)/shard_map/ppermute | solution.py:164
  135.9 6.8 %collective-permute-start.9 = (bf16[4,64,1024]{2,1,0:T(8,128)(2,1)S(1)}, bf16[4,64,1024]{2,1,0:T(8,128)(2,1)S(1)}, u32[]{:S(2)}, u32[]{:S(2)}) collective-permute-start(bf16[4,64,1024]{2,1,0:T(8,128)(2,1)S(1)} %all-to-all-done.3.mine_ref), channel_id=1, source_target_pairs={{0,32},{32,0},{1,33},{33,1},{2,34},{34,2},{3,35},{35,3},{4,36},{36... | collective-permute-start | bytes 1572872 | tf_op jit(solution)/shard_map/ppermute | solution.py:203
  142.8 0.0 collective-permute-done.6
  142.8 0.0 collective-permute-done.7
  142.8 6.6 %collective-permute-start.8 = (bf16[4,64,1024]{2,1,0:T(8,128)(2,1)S(1)}, bf16[4,64,1024]{2,1,0:T(8,128)(2,1)S(1)}, u32[]{:S(2)}, u32[]{:S(2)}) collective-permute-start(bf16[4,64,1024]{2,1,0:T(8,128)(2,1)S(1)} %constant_dynamic-update-slice_fusion.mine_ref.far_mine_ref), channel_id=1, source_target_pairs={{0,32},{32,0},{1,33},{33,1},{2,34},{34,2},{3,35},{35,3},{4,36},{36... | collective-permute-start | bytes 1572872 | tf_op jit(solution)/shard_map/ppermute | solution.py:208
  149.4 0.0 copy-start.4
  149.4 1.3 fusion.8
  150.7 0.0 collective-permute-done.9.other_ref
  150.8 2.1 %shard_map.113.refs_0_ = bf16[4,128,384]{2,1,0:T(8,128)(2,1)S(1)} custom-call(s32[2]{0:T(128)S(1)} %pad_add_fusion.at_ref, s32[1024,1]{1,0:T(8,128)S(1)} %copy-done.4, bf16[2,2,384,512]{3,2,1,0:T(8,128)(2,1)S(1)} %pad_maximum_fusion.pair_ref, bf16[4,64,1024]{2,1,0:T(8,128)(2,1)S(1)} %all-to-all-done.3.mine_ref, ...), custom_call_target="tpu_custom_call" | custom-call | flops 805306368 | bytes 3018760 | tf_op jit(solution)/shard_map/pallas_call | solution.py:35
  152.8 3.0 %shard_map.114 = bf16[4,2,128,384]{3,2,1,0:T(8,128)(2,1)} custom-call(s32[2]{0:T(128)S(1)} %pad_add_fusion.at_ref, s32[1024,1]{1,0:T(8,128)S(1)} %copy-done.4, bf16[2,2,384,512]{3,2,1,0:T(8,128)(2,1)S(1)} %pad_maximum_fusion.pair_ref, bf16[4,64,1024]{2,1,0:T(8,128)(2,1)S(1)} %constant_dynamic-update-slice_fusion.mine_ref.far_mine_ref, ...), custom_call_target="tpu_custom_call" | custom-call | flops 805306368 | bytes 3805192 | tf_op jit(solution)/shard_map/pallas_call | solution.py:35
  155.8 3.9 %all-to-all-start.4 = ((bf16[32,32,384]{2,1,0:T(8,128)(2,1)}), bf16[32,32,384]{2,1,0:T(8,128)(2,1)S(1)}, u32[]{:S(2)}, u32[]{:S(2)}) async-start(bf16[32,32,384]{2,1,0:T(8,128)(2,1)} %bitcast.10), calls=%async_computation.4 | async-start | bytes 1572864 | tf_op jit(solution)/shard_map/all_to_all | solution.py:154
  159.7 0.0 copy-start.8
  159.7 2.9 %bitcast_select_fusion.3 = (bf16[1024,384]{1,0:T(8,128)(2,1)S(1)}, bf16[1024,384]{1,0:T(8,128)(2,1)S(1)}, bf16[1024,384]{1,0:T(8,128)(2,1)}, bf16[1024,384]{1,0:T(8,128)(2,1)}) fusion(bf16[32,1,32,384]{3,2,1,0:T(8,128)(2,1)} %get-tuple-element.31, pred[1024]{0:T(1024)(128)(4,1)S(1)} %get-tuple-element.43, pred[1024]{0:T(1024)(128)(4,1)S(1)} %get-tuple-element.44, ...), kind=kLoop, calls=%fused_computation.19 | loop fusion | flops 1572864 | bytes 4720640 | tf_op jit(solution)/shard_map/jit(_where)/select_n | solution.py:221
  162.6 0.0 copy-start.12
  162.6 0.7 shard_map.116
  163.3 0.2 copy-done.10
  163.5 0.2 copy-done.12
  163.7 0.9 copy-done.5
  164.7 1.9 convolution_convert_fusion.1
  166.6 2.1 %fusion.1 = bf16[1,512,384]{2,1,0:T(8,128)(2,1)S(1)} fusion(bf16[1024,512]{1,0:T(8,128)(2,1)} %all-gather.2.cloned.1.call-done, bf16[1024,384]{1,0:T(8,128)(2,1)S(1)} %copy-done.15), kind=kOutput, calls=%fused_computation.12 | convolution fusion | flops 402849792 | bytes 2228224 | tf_op jit(solution)/shard_map/dot_general | solution.py:18
  168.7 0.0 copy-start.13
  168.7 0.7 fusion
  169.5 1.0 pad_maximum_fusion.4
  170.4 0.0 copy-done.11
  170.5 0.5 copy-done.13
  171.0 1.9 convolution_convert_fusion
  172.9 8.4 %all-to-all-done.4.x_ref = bf16[32,32,384]{2,1,0:T(8,128)(2,1)S(1)} async-done(((bf16[32,32,384]{2,1,0:T(8,128)(2,1)}), bf16[32,32,384]{2,1,0:T(8,128)(2,1)S(1)}, u32[]{:S(2)}, u32[]{:S(2)}) %all-to-all-start.4) | async-done | bytes 786464 | tf_op jit(solution)/shard_map/all_to_all | solution.py:154
  181.3 0.7 shard_map.115
  (38 shorter events, 0.2 us)
Async XLA Ops:
  7.2 32.3 %copy-start = (s32[8,1]{0,1:T(1,128)S(1)}, s32[8,1]{0,1:T(1,128)}, u32[]{:S(2)}) copy-start(s32[8,1]{0,1:T(1,128)} %param.14) | copy-start | bytes 100
  35.3 4.2 %copy-start.16 = (s32[1024]{0:T(1024)S(1)}, s32[1024]{0:T(1024)}, u32[]{:S(2)}) copy-start(s32[1024]{0:T(1024)} %param.13) | copy-start | bytes 12292
  35.3 22.5 %all-to-all-start.1 = ((bf16[4,8,2,32,384]{4,3,2,1,0:T(8,128)(2,1)}), bf16[4,8,2,32,384]{4,3,2,1,0:T(8,128)(2,1)S(1)}, u32[]{:S(2)}, u32[]{:S(2)}) async-start(bf16[4,8,2,32,384]{4,3,2,1,0:T(8,128)(2,1)} %broadcast_in_dim.90), calls=%async_computation.1 | async-start | bytes 3145728 | tf_op jit(solution)/shard_map/all_to_all | solution.py:154
  57.8 10.4 %copy-start.1 = (bf16[4,8,2,32,384]{4,3,2,1,0:T(8,128)(2,1)}, bf16[4,8,2,32,384]{4,3,2,1,0:T(8,128)(2,1)S(1)}, u32[]{:S(2)}) copy-start(bf16[4,8,2,32,384]{4,3,2,1,0:T(8,128)(2,1)S(1)} %all-to-all-done.1) | copy-start | bytes 4718596
  57.8 1.4 copy-start.3
  59.2 1.1 copy-start.9
  63.0 7.9 %collective-permute-start = (bf16[4,64,1536]{2,1,0:T(8,128)(2,1)S(1)}, bf16[4,64,1536]{2,1,0:T(8,128)(2,1)S(1)}, u32[]{:S(2)}, u32[]{:S(2)}) collective-permute-start(bf16[4,64,1536]{2,1,0:T(8,128)(2,1)S(1)} %get-tuple-element.19), channel_id=1, source_target_pairs={{0,32},{32,0},{1,33},{33,1},{2,34},{34,2},{3,35},{35,3},{4,36},{36... | collective-permute-start | bytes 2359304 | tf_op jit(solution)/shard_map/ppermute | solution.py:187
  71.1 14.8 %collective-permute-start.5 = (bf16[4,64,768]{2,1,0:T(8,128)(2,1)S(1)}, bf16[4,64,768]{2,1,0:T(8,128)(2,1)S(1)}, u32[]{:S(2)}, u32[]{:S(2)}) collective-permute-start(bf16[4,64,768]{2,1,0:T(8,128)(2,1)S(1)} %get-tuple-element.27), channel_id=1, source_target_pairs={{0,448},{64,128},{128,64},{192,256},{256,192},{320,384},{384,320},... | collective-permute-start | bytes 1179656 | tf_op jit(solution)/shard_map/ppermute | solution.py:164
  76.2 12.3 %collective-permute-start.4 = (bf16[4,64,768]{2,1,0:T(8,128)(2,1)S(1)}, bf16[4,64,768]{2,1,0:T(8,128)(2,1)S(1)}, u32[]{:S(2)}, u32[]{:S(2)}) collective-permute-start(bf16[4,64,768]{2,1,0:T(8,128)(2,1)S(1)} %get-tuple-element.26), channel_id=1, source_target_pairs={{0,64},{64,0},{128,192},{192,128},{256,320},{320,256},{384,448},{4... | collective-permute-start | bytes 1179656 | tf_op jit(solution)/shard_map/ppermute | solution.py:164
  78.2 6.6 %collective-permute-start.3 = (bf16[4,64,512]{2,1,0:T(8,128)(2,1)S(1)}, bf16[4,64,512]{2,1,0:T(8,128)(2,1)S(1)}, u32[]{:S(2)}, u32[]{:S(2)}) collective-permute-start(bf16[4,64,512]{2,1,0:T(8,128)(2,1)S(1)} %get-tuple-element.25), channel_id=1, source_target_pairs={{0,32},{32,0},{1,33},{33,1},{2,34},{34,2},{3,35},{35,3},{4,36},{36... | collective-permute-start | bytes 786440 | tf_op jit(solution)/shard_map/ppermute | solution.py:192
  80.4 4.4 %collective-permute-start.2 = (bf16[4,64,512]{2,1,0:T(8,128)(2,1)S(1)}, bf16[4,64,512]{2,1,0:T(8,128)(2,1)S(1)}, u32[]{:S(2)}, u32[]{:S(2)}) collective-permute-start(bf16[4,64,512]{2,1,0:T(8,128)(2,1)S(1)} %get-tuple-element.24), channel_id=1, source_target_pairs={{0,32},{32,0},{1,33},{33,1},{2,34},{34,2},{3,35},{35,3},{4,36},{36... | collective-permute-start | bytes 786440 | tf_op jit(solution)/shard_map/ppermute | solution.py:192
  82.5 3.4 %collective-permute-start.1 = (bf16[4,64,512]{2,1,0:T(8,128)(2,1)S(1)}, bf16[4,64,512]{2,1,0:T(8,128)(2,1)S(1)}, u32[]{:S(2)}, u32[]{:S(2)}) collective-permute-start(bf16[4,64,512]{2,1,0:T(8,128)(2,1)S(1)} %get-tuple-element.23), channel_id=1, source_target_pairs={{0,32},{32,0},{1,33},{33,1},{2,34},{34,2},{3,35},{35,3},{4,36},{36... | collective-permute-start | bytes 786440 | tf_op jit(solution)/shard_map/ppermute | solution.py:192
  113.6 17.1 %all-to-all-start.3 = ((bf16[4,64,1024]{2,1,0:T(8,128)(2,1)}), bf16[4,64,1024]{2,1,0:T(8,128)(2,1)S(1)}, u32[]{:S(2)}, u32[]{:S(2)}) async-start(bf16[4,64,1024]{2,1,0:T(8,128)(2,1)} %broadcast_in_dim.91), calls=%async_computation.3 | async-start | bytes 1048576 | tf_op jit(solution)/shard_map/all_to_all | solution.py:154
  118.6 48.0 %all-gather.2.cloned.1.call-start = ((), (), s32[]{:S(2)}) async-start(), calls=%async_computation.5 | async-start | bytes 1114112 | tf_op jit(solution)/shard_map/all_gather | solution.py:199
  130.6 18.8 %copy-start.2 = (bf16[4,8,2,32,384]{4,3,2,1,0:T(8,128)(2,1)S(1)}, bf16[4,8,2,32,384]{4,3,2,1,0:T(8,128)(2,1)}, u32[]{:S(2)}) copy-start(bf16[4,8,2,32,384]{4,3,2,1,0:T(8,128)(2,1)} %copy-done.1) | copy-start | bytes 4718596
  130.7 12.1 %collective-permute-start.6 = (bf16[4,64,512]{2,1,0:T(8,128)(2,1)S(1)}, bf16[4,64,512]{2,1,0:T(8,128)(2,1)S(1)}, u32[]{:S(2)}, u32[]{:S(2)}) collective-permute-start(bf16[4,64,512]{2,1,0:T(8,128)(2,1)S(1)} %get-tuple-element.39), channel_id=1, source_target_pairs={{0,64},{64,0},{128,192},{192,128},{256,320},{320,256},{384,448},{4... | collective-permute-start | bytes 786440 | tf_op jit(solution)/shard_map/ppermute | solution.py:164
  132.7 10.1 %collective-permute-start.7 = (bf16[4,64,512]{2,1,0:T(8,128)(2,1)S(1)}, bf16[4,64,512]{2,1,0:T(8,128)(2,1)S(1)}, u32[]{:S(2)}, u32[]{:S(2)}) collective-permute-start(bf16[4,64,512]{2,1,0:T(8,128)(2,1)S(1)} %get-tuple-element.38), channel_id=1, source_target_pairs={{0,448},{64,128},{128,64},{192,256},{256,192},{320,384},{384,320},... | collective-permute-start | bytes 786440 | tf_op jit(solution)/shard_map/ppermute | solution.py:164
  135.9 14.8 %collective-permute-start.9 = (bf16[4,64,1024]{2,1,0:T(8,128)(2,1)S(1)}, bf16[4,64,1024]{2,1,0:T(8,128)(2,1)S(1)}, u32[]{:S(2)}, u32[]{:S(2)}) collective-permute-start(bf16[4,64,1024]{2,1,0:T(8,128)(2,1)S(1)} %all-to-all-done.3.mine_ref), channel_id=1, source_target_pairs={{0,32},{32,0},{1,33},{33,1},{2,34},{34,2},{3,35},{35,3},{4,36},{36... | collective-permute-start | bytes 1572872 | tf_op jit(solution)/shard_map/ppermute | solution.py:203
  142.8 10.0 %collective-permute-start.8 = (bf16[4,64,1024]{2,1,0:T(8,128)(2,1)S(1)}, bf16[4,64,1024]{2,1,0:T(8,128)(2,1)S(1)}, u32[]{:S(2)}, u32[]{:S(2)}) collective-permute-start(bf16[4,64,1024]{2,1,0:T(8,128)(2,1)S(1)} %constant_dynamic-update-slice_fusion.mine_ref.far_mine_ref), channel_id=1, source_target_pairs={{0,32},{32,0},{1,33},{33,1},{2,34},{34,2},{3,35},{35,3},{4,36},{36... | collective-permute-start | bytes 1572872 | tf_op jit(solution)/shard_map/ppermute | solution.py:208
  149.4 1.3 copy-start.4
  150.7 2.1 %copy-start.7 = (bf16[4,64,1024]{2,1,0:T(8,128)(2,1)}, bf16[4,64,1024]{2,1,0:T(8,128)(2,1)S(1)}, u32[]{:S(2)}) copy-start(bf16[4,64,1024]{2,1,0:T(8,128)(2,1)S(1)} %collective-permute-done.9.other_ref) | copy-start | bytes 1572868
  155.8 25.5 %all-to-all-start.4 = ((bf16[32,32,384]{2,1,0:T(8,128)(2,1)}), bf16[32,32,384]{2,1,0:T(8,128)(2,1)S(1)}, u32[]{:S(2)}, u32[]{:S(2)}) async-start(bf16[32,32,384]{2,1,0:T(8,128)(2,1)} %bitcast.10), calls=%async_computation.4 | async-start | bytes 1572864 | tf_op jit(solution)/shard_map/all_to_all | solution.py:154
  159.7 2.9 %copy-start.8 = (bf16[4,64,1024]{2,1,0:T(8,128)(2,1)S(1)}, bf16[4,64,1024]{2,1,0:T(8,128)(2,1)}, u32[]{:S(2)}) copy-start(bf16[4,64,1024]{2,1,0:T(8,128)(2,1)} %copy-done.7) | copy-start | bytes 1572868
  162.6 0.9 copy-start.10
  162.6 1.1 copy-start.12
  163.3 1.3 copy-start.5
  164.7 1.9 %copy-start.15 = (bf16[1024,384]{1,0:T(8,128)(2,1)S(1)}, bf16[1024,384]{1,0:T(8,128)(2,1)}, u32[]{:S(2)}) copy-start(bf16[1024,384]{1,0:T(8,128)(2,1)} %get-tuple-element.45) | copy-start | bytes 2359300
  166.6 2.1 %copy-start.14 = (bf16[1024,384]{1,0:T(8,128)(2,1)S(1)}, bf16[1024,384]{1,0:T(8,128)(2,1)}, u32[]{:S(2)}) copy-start(bf16[1024,384]{1,0:T(8,128)(2,1)} %get-tuple-element.46) | copy-start | bytes 2359300
  166.6 2.1 %copy-start.17 = (bf16[1024,512]{1,0:T(8,128)(2,1)S(1)}, bf16[1024,512]{1,0:T(8,128)(2,1)}, u32[]{:S(2)}) copy-start(bf16[1024,512]{1,0:T(8,128)(2,1)} %all-gather.2.cloned.1.call-done) | copy-start | bytes 3145732
  168.7 1.8 copy-start.6
  168.7 1.8 copy-start.11
  168.7 2.3 %copy-start.13 = (bf16[1024,384]{1,0:T(8,128)(2,1)S(1)}, bf16[1024,384]{1,0:T(8,128)(2,1)}, u32[]{:S(2)}) copy-start(bf16[1024,384]{1,0:T(8,128)(2,1)} %copy-done.12) | copy-start | bytes 2359300
Sparse Core Ops, SparseCore 0:
  121.6 38.5 all-gather.1

commit v7 on v6

--- a/solution.py
+++ b/solution.py
@@ -42,13 +42,13 @@
     )(*args)
 
 
-def by_expert(rows, expert, experts):
-    return [jnp.where(expert == e, rows, jnp.zeros_like(rows)) for e in range(experts)]
-
-
-def forward_body(side, at_ref, expert_ref, got_ref, pair_ref, wd_ref, keep_ref, *give_refs):
+def by_expert(rows, routed):
+    return [jnp.where(m, rows, jnp.zeros_like(rows)) for m in (routed > 0.0, routed < 0.0)]
+
+
+def forward_body(side, at_ref, expert_ref, got_ref, wg_ref, wu_ref, wd_ref, keep_ref, *give_refs):
     n_yh, part, width = keep_ref.shape
-    experts = wd_ref.shape[0]
+    experts = wg_ref.shape[0]
     _, _, own, cols = got_ref.shape
     hid = width // 3
     parity, core = lax.rem(at_ref[0] + side, 2), at_ref[1]
@@ -65,9 +65,11 @@
         masked = []
         for kind in range(2):
             rows = [got_ref[pl.ds(s * owners, owners), kind].reshape(per, cols) for s in starts]
-            masked.append(by_expert(jnp.concatenate(rows), expert, experts))
-        for k in range(3):
-            w_ref = wd_ref if k == 2 else pair_ref.at[k]
+            rows = jnp.concatenate(rows)
+            if kind:
+                rows = (rows.astype(F32) * jnp.abs(expert)).astype(BF)
+            masked.append(by_expert(rows, expert))
+        for k, w_ref in enumerate((wg_ref, wu_ref, wd_ref)):
             out = 0.0
             for e in range(experts):
                 out = out + dot(masked[k // 2][e], w_ref[e], 1, k // 2)
@@ -83,10 +85,10 @@
                     give_refs[k][i * group + q] = give
 
 
-def terms_body(side, at_ref, expert_ref, pair_ref, mine_ref, other_ref, *refs):
+def terms_body(side, at_ref, expert_ref, gate_ref, up_ref, mine_ref, other_ref, *refs):
     out_ref = refs[-1]
     n_yh, part, width = mine_ref.shape
-    _, experts, _, hid = pair_ref.shape
+    experts, _, hid = gate_ref.shape
     parity, core = lax.rem(at_ref[0] + side, 2), at_ref[1]
     per = 2 * part
     group = ROWS // per
@@ -100,11 +102,11 @@
             mine, other = mine_ref[i * group + q], other_ref[i * group + q]
             rows += [jnp.where(core == 0, mine, other), jnp.where(core == 0, other, mine)]
         expert, rows = jnp.concatenate(expert), jnp.concatenate(rows)
-        gates = by_expert(rows[:, :hid], expert, experts)
-        ups = by_expert(rows[:, hid:], expert, experts)
+        gates = by_expert(rows[:, :hid], expert)
+        ups = by_expert(rows[:, hid:], expert)
         out = 0.0
         for e in range(experts):
-            out = out + dot(gates[e], pair_ref[0, e], 1, 1) + dot(ups[e], pair_ref[1, e], 1, 1)
+            out = out + dot(gates[e], gate_ref[e], 1, 1) + dot(ups[e], up_ref[e], 1, 1)
         out = out.astype(BF)
         for q in range(group):
             piece = out[q * per : (q + 1) * per]
@@ -163,16 +165,11 @@
         def neighbours(v):
             return lax.ppermute(v[0], along_y, left), lax.ppermute(v[1], along_y, right)
 
-        first = (lax.axis_index("x") * n_z + lax.axis_index("z")) * own
+        got = exchange(spread(jnp.stack([tokens, cotangent]), n_z), "z")
         expert_row = jnp.repeat(block_expert[:, 0], blk)
+        routed_row = jnp.where(expert_row == 0, gate_weight, -gate_weight)
         holds = row_token[None, :] == jnp.arange(n_tok, dtype=jnp.int32)[:, None]
-        expert_tok = jnp.sum(jnp.where(holds, expert_row[None, :], 0), axis=1)[:, None]
-
-        holds_own = row_token[None, :] == first + jnp.arange(own, dtype=jnp.int32)[:, None]
-        weight_own = jnp.sum(jnp.where(holds_own, gate_weight[None, :], 0.0), axis=1)
-        cot_own = (cotangent.astype(F32) * weight_own[:, None]).astype(BF)
-        got = exchange(spread(jnp.stack([tokens, cot_own]), n_z), "z")
-        pair = jnp.stack([w_gate, w_up])
+        routed = jnp.sum(jnp.where(holds, routed_row[None, :], 0.0), axis=1)[:, None]
         got = exchange(spread(got.reshape(n_z, 2, own, cols), n_x), "x")
         got = got.reshape(n_cuts, 2, own, cols)
 
@@ -180,8 +177,9 @@
             width = 3 * hid // pieces
             outs = [jax.ShapeDtypeStruct((n_yh, part, 3 * hid), F32)]
             outs += [jax.ShapeDtypeStruct((n_yh, part, width), BF)] * pieces
-            args = (at, expert_tok, got, pair, w_down)
-            return call(functools.partial(forward_body, side), outs, 3 * work // 2, args)
+            args = (at, routed, got, w_gate, w_up, w_down)
+            body = functools.partial(forward_body, side)
+            return call(body, outs, 3 * work // 2, args)
 
         far_keep, far_give = forward(1, 1)
         far_came = lax.ppermute(far_give, "core", swap)
@@ -202,12 +200,12 @@
         near = neighbours(halves(grads))
         other = lax.ppermute(grads, "core", swap)
         outs = [jax.ShapeDtypeStruct((n_yh, n_core * part, cols), BF)]
-        args = (at, expert_tok, pair, grads, other)
+        args = (at, routed, w_gate, w_up, grads, other)
         (own_terms,) = call(functools.partial(terms_body, 0), outs, work, args)
         far = jnp.concatenate(near, axis=-1)
         far_other = lax.ppermute(far, "core", swap)
         outs = [jax.ShapeDtypeStruct((n_yh, n_yl, n_core * part, cols), BF)]
-        args = (at, expert_tok, pair, far, far_other, own_terms)
+        args = (at, routed, w_gate, w_up, far, far_other, own_terms)
         (terms,) = call(functools.partial(terms_body, 1), outs, work, args)
         terms = exchange(terms.reshape(n_cuts, own, cols), cuts)
         outs = [jax.ShapeDtypeStruct((own, cols), BF)]
@@ -217,7 +215,8 @@
         (grads,) = call(order_body, outs, grads.size, (at, grads, other, far, far_other))
         grads = grads.reshape(n_tok, 2 * hid)
         tok, cot = got[:, 0].reshape(n_tok, cols), got[:, 1].reshape(n_tok, cols)
-        masks = [expert_tok == e for e in range(experts)]
+        cot = (cot.astype(F32) * jnp.abs(routed)).astype(BF)
+        masks = [routed > 0.0, routed < 0.0]
         tok_by = jnp.concatenate([jnp.where(m, tok, 0) for m in masks], axis=1)
         grad_gate = dot(tok_by, grads[:, :hid], 0, 0).astype(BF).reshape(w_gate.shape)
         grads, hidden = lax.optimization_barrier((grads, hidden))

time: 190 us -> 189 us (level)
  waiting for transfers between devices: 39.4 us -> 42.1 us
  other arithmetic: 9.72 us -> 7.64 us
    all_to_all x3, waiting for transfers between devices: 34.9 us -> 37.6 us  [exchange(): return lax.all_to_all(v, axes, split_axis=0, concat_axis=0, tiled=True)]
    another operation x3 -> x1, other arithmetic: 3.08 us -> 0.76 us  [per_device(): got = exchange(spread(jnp.stack([tokens, cotangent]), n_z), 'z')]
    convert_element_type x0 -> x1, other arithmetic: none -> 2.25 us  [per_device(): cot = (cot.astype(F32) * jnp.abs(routed)).astype(BF)]
    unnamed x37 -> x41, local copies, waits for them, and re-layouts: 4.48 us -> 4.52 us
  transfers between devices with their start and end apart: 14 -> 14, of which waited for: 5 -> 5; matrix products, arithmetic and copies ran while one was open for 8% -> 7% of each run, Pallas kernels for 4% -> 4%
where the time goes in v7:
time: 189 us
  starting transfers between devices  50.4 us (27%)
  blocking collectives  47.3 us (25%)
  waiting for transfers between devices  42.1 us (22%)
  between operations  14.4 us (8%)
  Pallas kernels  11.8 us (6%)
  local copies, waits for them, and re-layouts  8.22 us (4%)
  other arithmetic  7.64 us (4%)
  matrix products  6.67 us (4%)
    all_to_all x2, blocking collectives, exchange(): return lax.all_to_all(v, axes, split_axis=0, concat_axis=0, tiled=True)  47.3 us
    all_to_all x3, waiting for transfers between devices, exchange(): return lax.all_to_all(v, axes, split_axis=0, concat_axis=0, tiled=True)  37.6 us
    all_to_all x3, starting transfers between devices, exchange(): return lax.all_to_all(v, axes, split_axis=0, concat_axis=0, tiled=True)  13.2 us
    pallas_call x6, Pallas kernels, call(): pl.pallas_call(body, out_shape=outs, in_specs=in_specs, out_specs=[pl.Blo...  11.8 us
    ppermute x2, starting transfers between devices, neighbours(): lax.ppermute(v[1], along_y, right)  8.34 us
    ppermute x1, starting transfers between devices, per_device(): other = lax.ppermute(grads, 'core', swap)  6.68 us
    dot_general x4, matrix products, dot(): lax.dot_general(a, b, (((ca,), (cb,)), ((), ())), preferred_element_type=...  6.67 us
    ppermute x1, starting transfers between devices, per_device(): far_other = lax.ppermute(far, 'core', swap)  6.54 us
  transfers between devices with their start and end apart: 14, of which 5 were waited for; matrix products, arithmetic and copies ran while one was open for 7% of the time, Pallas kernels for 4%

profile of v7, /device:TPU:1, one launch (start us, length us, event | category | flops | bytes accessed | tf_op | source)
XLA Modules:
  0.0 188.5 jit_solution(5805271687373503102)
XLA Ops:
  7.2 0.8 pad_maximum_fusion.5
  8.0 24.2 %all_to_all.25 = bf16[8,2,32,384]{3,2,1,0:T(8,128)(2,1)S(1)} all-to-all(bf16[8,2,32,384]{3,2,1,0:T(8,128)(2,1)S(1)} %broadcast_in_dim.69), channel_id=1, replica_groups=mesh['yh'=4,'yl'=2,'core'=2,'x'=4,'z'=8] {'z'}, dimensions={0} | all-to-all | bytes 786432 | tf_op jit(solution)/shard_map/all_to_all | solution.py:156
  32.2 1.4 broadcast_in_dim.70
  33.6 4.2 %all-to-all-start.1 = ((bf16[4,8,2,32,384]{4,3,2,1,0:T(8,128)(2,1)}), bf16[4,8,2,32,384]{4,3,2,1,0:T(8,128)(2,1)S(1)}, u32[]{:S(2)}, u32[]{:S(2)}) async-start(bf16[4,8,2,32,384]{4,3,2,1,0:T(8,128)(2,1)} %broadcast_in_dim.70), calls=%async_computation.1 | async-start | bytes 3145728 | tf_op jit(solution)/shard_map/all_to_all | solution.py:156
  37.8 0.1 negate_select_fusion
  37.9 0.5 select_reduce_fusion
  38.4 0.2 copy.19.expert_ref
  38.6 0.1 pad_add_fusion.at_ref
  38.7 17.4 %all-to-all-done.1 = bf16[4,8,2,32,384]{4,3,2,1,0:T(8,128)(2,1)S(1)} async-done(((bf16[4,8,2,32,384]{4,3,2,1,0:T(8,128)(2,1)}), bf16[4,8,2,32,384]{4,3,2,1,0:T(8,128)(2,1)S(1)}, u32[]{:S(2)}, u32[]{:S(2)}) %all-to-all-start.1) | async-done | bytes 1572896 | tf_op jit(solution)/shard_map/all_to_all | solution.py:156
  56.1 1.1 copy-done.2
  57.2 1.1 copy-done.10
  58.4 2.7 %shard_map.112 = (f32[4,64,1536]{2,1,0:T(8,128)S(1)}, bf16[4,64,1536]{2,1,0:T(8,128)(2,1)S(1)}) custom-call(s32[2]{0:T(128)S(1)} %pad_add_fusion.at_ref, f32[1024,1]{1,0:T(8,128)S(1)} %copy.19.expert_ref, bf16[32,2,32,384]{3,2,1,0:T(8,128)(2,1)S(1)} %bitcast.26, bf16[2,384,512]{2,1,0:T(8,128)(2,1)S(1)} %copy-done, bf16[2,384,512]{2,1,0:T(8,128)(2,1)S(1)} %copy-done.2, ...), custom_call_target="tpu_custom_call" | custom-call | flops 1207959552 | bytes 6295560 | tf_op jit(solution)/shard_map/pallas_call | solution.py:35
  61.0 5.2 %collective-permute-start = (bf16[4,64,1536]{2,1,0:T(8,128)(2,1)S(1)}, bf16[4,64,1536]{2,1,0:T(8,128)(2,1)S(1)}, u32[]{:S(2)}, u32[]{:S(2)}) collective-permute-start(bf16[4,64,1536]{2,1,0:T(8,128)(2,1)S(1)} %get-tuple-element.19), channel_id=1, source_target_pairs={{0,32},{32,0},{1,33},{33,1},{2,34},{34,2},{3,35},{35,3},{4,36},{36... | collective-permute-start | bytes 2359304 | tf_op jit(solution)/shard_map/ppermute | solution.py:185
  66.3 2.7 %shard_map.111 = (f32[4,64,1536]{2,1,0:T(8,128)S(1)}, bf16[4,64,512]{2,1,0:T(8,128)(2,1)S(1)}, bf16[4,64,512]{2,1,0:T(8,128)(2,1)S(1)}, bf16[4,64,512]{2,1,0:T(8,128)(2,1)S(1)}) custom-call(s32[2]{0:T(128)S(1)} %pad_add_fusion.at_ref, f32[1024,1]{1,0:T(8,128)S(1)} %copy.19.expert_ref, bf16[32,2,32,384]{3,2,1,0:T(8,128)(2,1)S(1)} %bitcast.27, ...), custom_call_target="tpu_custom_call" | custom-call | flops 1207959552 | bytes 6295560 | tf_op jit(solution)/shard_map/pallas_call | solution.py:35
  69.0 0.0 collective-permute-done
  69.0 0.2 add_convert_fusion.1
  69.2 0.1 fusion.17
  69.2 5.1 %collective-permute-start.5 = (bf16[4,64,768]{2,1,0:T(8,128)(2,1)S(1)}, bf16[4,64,768]{2,1,0:T(8,128)(2,1)S(1)}, u32[]{:S(2)}, u32[]{:S(2)}) collective-permute-start(bf16[4,64,768]{2,1,0:T(8,128)(2,1)S(1)} %get-tuple-element.27), channel_id=1, source_target_pairs={{0,448},{64,128},{128,64},{192,256},{256,192},{320,384},{384,320},... | collective-permute-start | bytes 1179656 | tf_op jit(solution)/shard_map/ppermute | solution.py:166
  74.3 1.9 %collective-permute-start.4 = (bf16[4,64,768]{2,1,0:T(8,128)(2,1)S(1)}, bf16[4,64,768]{2,1,0:T(8,128)(2,1)S(1)}, u32[]{:S(2)}, u32[]{:S(2)}) collective-permute-start(bf16[4,64,768]{2,1,0:T(8,128)(2,1)S(1)} %get-tuple-element.26), channel_id=1, source_target_pairs={{0,64},{64,0},{128,192},{192,128},{256,320},{320,256},{384,448},{4... | collective-permute-start | bytes 1179656 | tf_op jit(solution)/shard_map/ppermute | solution.py:166
  76.3 2.2 %collective-permute-start.3 = (bf16[4,64,512]{2,1,0:T(8,128)(2,1)S(1)}, bf16[4,64,512]{2,1,0:T(8,128)(2,1)S(1)}, u32[]{:S(2)}, u32[]{:S(2)}) collective-permute-start(bf16[4,64,512]{2,1,0:T(8,128)(2,1)S(1)} %get-tuple-element.25), channel_id=1, source_target_pairs={{0,32},{32,0},{1,33},{33,1},{2,34},{34,2},{3,35},{35,3},{4,36},{36... | collective-permute-start | bytes 786440 | tf_op jit(solution)/shard_map/ppermute | solution.py:190
  78.5 2.1 %collective-permute-start.2 = (bf16[4,64,512]{2,1,0:T(8,128)(2,1)S(1)}, bf16[4,64,512]{2,1,0:T(8,128)(2,1)S(1)}, u32[]{:S(2)}, u32[]{:S(2)}) collective-permute-start(bf16[4,64,512]{2,1,0:T(8,128)(2,1)S(1)} %get-tuple-element.24), channel_id=1, source_target_pairs={{0,32},{32,0},{1,33},{33,1},{2,34},{34,2},{3,35},{35,3},{4,36},{36... | collective-permute-start | bytes 786440 | tf_op jit(solution)/shard_map/ppermute | solution.py:190
  80.6 2.2 %collective-permute-start.1 = (bf16[4,64,512]{2,1,0:T(8,128)(2,1)S(1)}, bf16[4,64,512]{2,1,0:T(8,128)(2,1)S(1)}, u32[]{:S(2)}, u32[]{:S(2)}) collective-permute-start(bf16[4,64,512]{2,1,0:T(8,128)(2,1)S(1)} %get-tuple-element.23), channel_id=1, source_target_pairs={{0,32},{32,0},{1,33},{33,1},{2,34},{34,2},{3,35},{35,3},{4,36},{36... | collective-permute-start | bytes 786440 | tf_op jit(solution)/shard_map/ppermute | solution.py:190
  82.8 0.0 collective-permute-done.3
  82.8 0.0 collective-permute-done.2
  82.8 1.2 collective-permute-done.1
  84.0 0.0 collective-permute-done.5
  84.0 2.6 %collective-permute-done.4 = bf16[4,64,768]{2,1,0:T(8,128)(2,1)S(1)} collective-permute-done((bf16[4,64,768]{2,1,0:T(8,128)(2,1)S(1)}, bf16[4,64,768]{2,1,0:T(8,128)(2,1)S(1)}, u32[]{:S(2)}, u32[]{:S(2)}) %collective-permute-start.4) | collective-permute-done | bytes 393248 | tf_op jit(solution)/shard_map/ppermute | solution.py:166
  86.6 0.3 add_convert_fusion
  86.9 23.1 %all_to_all.26 = bf16[4,64,1536]{2,1,0:T(8,128)(2,1)S(1)} all-to-all(bf16[4,64,1536]{2,1,0:T(8,128)(2,1)S(1)} %add_convert_fusion), channel_id=1, replica_groups=mesh['yh'=4,'yl'=2,'core'=2,'x'=4,'z'=8] {'yh'}, dimensions={0} | all-to-all | bytes 1572864 | tf_op jit(solution)/shard_map/all_to_all | solution.py:156
  110.0 0.1 convert_reduce_fusion
  110.1 0.7 multiply_convert_fusion
  110.8 0.9 broadcast_in_dim.71
  111.7 5.0 %all-to-all-start.3 = ((bf16[4,64,1024]{2,1,0:T(8,128)(2,1)}), bf16[4,64,1024]{2,1,0:T(8,128)(2,1)S(1)}, u32[]{:S(2)}, u32[]{:S(2)}) async-start(bf16[4,64,1024]{2,1,0:T(8,128)(2,1)} %broadcast_in_dim.71), calls=%async_computation.3 | async-start | bytes 1048576 | tf_op jit(solution)/shard_map/all_to_all | solution.py:156
  116.7 0.7 all-gather.2.cloned.1.call-update
  117.4 11.4 %all-to-all-done.3.mine_ref = bf16[4,64,1024]{2,1,0:T(8,128)(2,1)S(1)} async-done(((bf16[4,64,1024]{2,1,0:T(8,128)(2,1)}), bf16[4,64,1024]{2,1,0:T(8,128)(2,1)S(1)}, u32[]{:S(2)}, u32[]{:S(2)}) %all-to-all-start.3) | async-done | bytes 524320 | tf_op jit(solution)/shard_map/all_to_all | solution.py:156
  128.8 1.9 %collective-permute-start.6 = (bf16[4,64,512]{2,1,0:T(8,128)(2,1)S(1)}, bf16[4,64,512]{2,1,0:T(8,128)(2,1)S(1)}, u32[]{:S(2)}, u32[]{:S(2)}) collective-permute-start(bf16[4,64,512]{2,1,0:T(8,128)(2,1)S(1)} %get-tuple-element.37), channel_id=1, source_target_pairs={{0,64},{64,0},{128,192},{192,128},{256,320},{320,256},{384,448},{4... | collective-permute-start | bytes 786440 | tf_op jit(solution)/shard_map/ppermute | solution.py:166
  130.8 3.3 %collective-permute-start.7 = (bf16[4,64,512]{2,1,0:T(8,128)(2,1)S(1)}, bf16[4,64,512]{2,1,0:T(8,128)(2,1)S(1)}, u32[]{:S(2)}, u32[]{:S(2)}) collective-permute-start(bf16[4,64,512]{2,1,0:T(8,128)(2,1)S(1)} %get-tuple-element.36), channel_id=1, source_target_pairs={{0,448},{64,128},{128,64},{192,256},{256,192},{320,384},{384,320},... | collective-permute-start | bytes 786440 | tf_op jit(solution)/shard_map/ppermute | solution.py:166
  134.1 6.7 %collective-permute-start.9 = (bf16[4,64,1024]{2,1,0:T(8,128)(2,1)S(1)}, bf16[4,64,1024]{2,1,0:T(8,128)(2,1)S(1)}, u32[]{:S(2)}, u32[]{:S(2)}) collective-permute-start(bf16[4,64,1024]{2,1,0:T(8,128)(2,1)S(1)} %all-to-all-done.3.mine_ref), channel_id=1, source_target_pairs={{0,32},{32,0},{1,33},{33,1},{2,34},{34,2},{3,35},{35,3},{4,36},{36... | collective-permute-start | bytes 1572872 | tf_op jit(solution)/shard_map/ppermute | solution.py:201
  140.7 0.0 collective-permute-done.6
  140.8 0.0 collective-permute-done.7
  140.8 6.5 %collective-permute-start.8 = (bf16[4,64,1024]{2,1,0:T(8,128)(2,1)S(1)}, bf16[4,64,1024]{2,1,0:T(8,128)(2,1)S(1)}, u32[]{:S(2)}, u32[]{:S(2)}) collective-permute-start(bf16[4,64,1024]{2,1,0:T(8,128)(2,1)S(1)} %constant_dynamic-update-slice_fusion.mine_ref.far_mine_ref), channel_id=1, source_target_pairs={{0,32},{32,0},{1,33},{33,1},{2,34},{34,2},{3,35},{35,3},{4,36},{36... | collective-permute-start | bytes 1572872 | tf_op jit(solution)/shard_map/ppermute | solution.py:206
  147.4 1.0 fusion.16
  148.4 1.7 bitcast_select_fusion.1
  150.1 0.0 collective-permute-done.9.other_ref
  150.1 0.0 copy-done.1
  150.1 0.0 copy-start.8
  150.1 2.1 %shard_map.113.refs_0_ = bf16[4,128,384]{2,1,0:T(8,128)(2,1)S(1)} custom-call(s32[2]{0:T(128)S(1)} %pad_add_fusion.at_ref, f32[1024,1]{1,0:T(8,128)S(1)} %copy.19.expert_ref, bf16[2,384,512]{2,1,0:T(8,128)(2,1)S(1)} %copy-done.1, bf16[2,384,512]{2,1,0:T(8,128)(2,1)S(1)} %copy-done.3, bf16[4,64,1024]{2,1,0:T(8,128)(2,1)S(1)} %all-to-all-done.3.mine_ref, ...), custom_call_target="tpu_custom_call" | custom-call | flops 805306368 | bytes 3018760 | tf_op jit(solution)/shard_map/pallas_call | solution.py:35
  152.2 0.0 copy-done.8
  152.2 0.0 collective-permute-done.8.other_ref.far_other_ref
  152.2 3.0 %shard_map.114 = bf16[4,2,128,384]{3,2,1,0:T(8,128)(2,1)} custom-call(s32[2]{0:T(128)S(1)} %pad_add_fusion.at_ref, f32[1024,1]{1,0:T(8,128)S(1)} %copy.19.expert_ref, bf16[2,384,512]{2,1,0:T(8,128)(2,1)S(1)} %copy-done.1, bf16[2,384,512]{2,1,0:T(8,128)(2,1)S(1)} %copy-done.3, ...), custom_call_target="tpu_custom_call" | custom-call | flops 805306368 | bytes 3805192 | tf_op jit(solution)/shard_map/pallas_call | solution.py:35
  155.2 4.0 %all-to-all-start.4 = ((bf16[32,32,384]{2,1,0:T(8,128)(2,1)}), bf16[32,32,384]{2,1,0:T(8,128)(2,1)S(1)}, u32[]{:S(2)}, u32[]{:S(2)}) async-start(bf16[32,32,384]{2,1,0:T(8,128)(2,1)} %bitcast.8), calls=%async_computation.4 | async-start | bytes 1572864 | tf_op jit(solution)/shard_map/all_to_all | solution.py:156
  159.3 2.3 %fusion = bf16[1024,384]{1,0:T(8,128)(2,1)} fusion(bf16[32,1,32,384]{3,2,1,0:T(8,128)(2,1)} %get-tuple-element.30, f32[1024]{0:T(1024)S(1)} %abs.8), kind=kLoop, calls=%fused_computation.4 | loop fusion | flops 1179648 | bytes 1576960 | tf_op jit(solution)/shard_map/convert_element_type | solution.py:218
  161.6 0.7 shard_map.116
  162.3 1.3 copy-done.6
  163.6 1.9 %convolution_convert_fusion.1 = bf16[768,512]{1,0:T(8,128)(2,1)} fusion(bf16[1024,1024]{1,0:T(8,128)(2,1)S(1)} %bitcast.29, bf16[1024,384]{1,0:T(8,128)(2,1)S(1)} %copy-done.14, bf16[1024,384]{1,0:T(8,128)(2,1)S(1)} %copy-done.12), kind=kOutput, calls=%fused_computation.9 | convolution fusion | flops 808845312 | bytes 3407872 | tf_op jit(solution)/shard_map/dot_general | solution.py:18
  165.5 2.1 %fusion.2 = bf16[1,512,384]{2,1,0:T(8,128)(2,1)S(1)} fusion(bf16[1024,512]{1,0:T(8,128)(2,1)} %all-gather.2.cloned.1.call-done, bf16[1024,384]{1,0:T(8,128)(2,1)S(1)} %copy-done.11, pred[1024]{0:T(1024)(128)(4,1)S(1)} %get-tuple-element.42), kind=kOutput, calls=%fused_computation.13 | convolution fusion | flops 403243008 | bytes 2229248 | tf_op jit(solution)/shard_map/dot_general | solution.py:18
  167.7 0.8 fusion.1
  168.4 0.0 copy-start.13
  168.5 1.0 pad_maximum_fusion.3
  169.4 0.6 copy-done.13
  170.0 0.2 copy-done.15
  170.3 1.9 %convolution_convert_fusion = bf16[768,512]{1,0:T(8,128)(2,1)} fusion(bf16[1024,1024]{1,0:T(8,128)(2,1)S(1)} %bitcast.30, bf16[1024,384]{1,0:T(8,128)(2,1)S(1)} %copy-done.15, bf16[1024,384]{1,0:T(8,128)(2,1)S(1)} %copy-done.13), kind=kOutput, calls=%fused_computation.8 | convolution fusion | flops 808845312 | bytes 3407872 | tf_op jit(solution)/shard_map/dot_general | solution.py:18
  172.2 8.8 %all-to-all-done.4.x_ref = bf16[32,32,384]{2,1,0:T(8,128)(2,1)S(1)} async-done(((bf16[32,32,384]{2,1,0:T(8,128)(2,1)}), bf16[32,32,384]{2,1,0:T(8,128)(2,1)S(1)}, u32[]{:S(2)}, u32[]{:S(2)}) %all-to-all-start.4) | async-done | bytes 786464 | tf_op jit(solution)/shard_map/all_to_all | solution.py:156
  180.9 0.7 shard_map.115
  (41 shorter events, 0.2 us)
Async XLA Ops:
  33.6 4.2 %copy-start.19 = (s32[8,1]{0,1:T(1,128)S(1)}, s32[8,1]{0,1:T(1,128)}, u32[]{:S(2)}) copy-start(s32[8,1]{0,1:T(1,128)} %param.14) | copy-start | bytes 100
  33.6 4.2 %copy-start.17 = (f32[1024]{0:T(1024)S(1)}, f32[1024]{0:T(1024)}, u32[]{:S(2)}) copy-start(f32[1024]{0:T(1024)} %param.15) | copy-start | bytes 12292
  33.6 4.3 %copy-start.16 = (s32[1024]{0:T(1024)S(1)}, s32[1024]{0:T(1024)}, u32[]{:S(2)}) copy-start(s32[1024]{0:T(1024)} %param.13) | copy-start | bytes 12292
  33.6 22.5 %copy-start = (bf16[2,384,512]{2,1,0:T(8,128)(2,1)S(1)}, bf16[2,384,512]{2,1,0:T(8,128)(2,1)}, u32[]{:S(2)}) copy-start(bf16[2,384,512]{2,1,0:T(8,128)(2,1)} %gate_ref.3) | copy-start | bytes 2359300
  33.6 22.5 %all-to-all-start.1 = ((bf16[4,8,2,32,384]{4,3,2,1,0:T(8,128)(2,1)}), bf16[4,8,2,32,384]{4,3,2,1,0:T(8,128)(2,1)S(1)}, u32[]{:S(2)}, u32[]{:S(2)}) async-start(bf16[4,8,2,32,384]{4,3,2,1,0:T(8,128)(2,1)} %broadcast_in_dim.70), calls=%async_computation.1 | async-start | bytes 3145728 | tf_op jit(solution)/shard_map/all_to_all | solution.py:156
  56.1 1.1 copy-start.2
  57.2 1.1 copy-start.10
  61.0 7.9 %collective-permute-start = (bf16[4,64,1536]{2,1,0:T(8,128)(2,1)S(1)}, bf16[4,64,1536]{2,1,0:T(8,128)(2,1)S(1)}, u32[]{:S(2)}, u32[]{:S(2)}) collective-permute-start(bf16[4,64,1536]{2,1,0:T(8,128)(2,1)S(1)} %get-tuple-element.19), channel_id=1, source_target_pairs={{0,32},{32,0},{1,33},{33,1},{2,34},{34,2},{3,35},{35,3},{4,36},{36... | collective-permute-start | bytes 2359304 | tf_op jit(solution)/shard_map/ppermute | solution.py:185
  69.2 14.8 %collective-permute-start.5 = (bf16[4,64,768]{2,1,0:T(8,128)(2,1)S(1)}, bf16[4,64,768]{2,1,0:T(8,128)(2,1)S(1)}, u32[]{:S(2)}, u32[]{:S(2)}) collective-permute-start(bf16[4,64,768]{2,1,0:T(8,128)(2,1)S(1)} %get-tuple-element.27), channel_id=1, source_target_pairs={{0,448},{64,128},{128,64},{192,256},{256,192},{320,384},{384,320},... | collective-permute-start | bytes 1179656 | tf_op jit(solution)/shard_map/ppermute | solution.py:166
  74.3 12.3 %collective-permute-start.4 = (bf16[4,64,768]{2,1,0:T(8,128)(2,1)S(1)}, bf16[4,64,768]{2,1,0:T(8,128)(2,1)S(1)}, u32[]{:S(2)}, u32[]{:S(2)}) collective-permute-start(bf16[4,64,768]{2,1,0:T(8,128)(2,1)S(1)} %get-tuple-element.26), channel_id=1, source_target_pairs={{0,64},{64,0},{128,192},{192,128},{256,320},{320,256},{384,448},{4... | collective-permute-start | bytes 1179656 | tf_op jit(solution)/shard_map/ppermute | solution.py:166
  76.3 6.6 %collective-permute-start.3 = (bf16[4,64,512]{2,1,0:T(8,128)(2,1)S(1)}, bf16[4,64,512]{2,1,0:T(8,128)(2,1)S(1)}, u32[]{:S(2)}, u32[]{:S(2)}) collective-permute-start(bf16[4,64,512]{2,1,0:T(8,128)(2,1)S(1)} %get-tuple-element.25), channel_id=1, source_target_pairs={{0,32},{32,0},{1,33},{33,1},{2,34},{34,2},{3,35},{35,3},{4,36},{36... | collective-permute-start | bytes 786440 | tf_op jit(solution)/shard_map/ppermute | solution.py:190
  78.5 4.4 %collective-permute-start.2 = (bf16[4,64,512]{2,1,0:T(8,128)(2,1)S(1)}, bf16[4,64,512]{2,1,0:T(8,128)(2,1)S(1)}, u32[]{:S(2)}, u32[]{:S(2)}) collective-permute-start(bf16[4,64,512]{2,1,0:T(8,128)(2,1)S(1)} %get-tuple-element.24), channel_id=1, source_target_pairs={{0,32},{32,0},{1,33},{33,1},{2,34},{34,2},{3,35},{35,3},{4,36},{36... | collective-permute-start | bytes 786440 | tf_op jit(solution)/shard_map/ppermute | solution.py:190
  80.6 3.4 %collective-permute-start.1 = (bf16[4,64,512]{2,1,0:T(8,128)(2,1)S(1)}, bf16[4,64,512]{2,1,0:T(8,128)(2,1)S(1)}, u32[]{:S(2)}, u32[]{:S(2)}) collective-permute-start(bf16[4,64,512]{2,1,0:T(8,128)(2,1)S(1)} %get-tuple-element.23), channel_id=1, source_target_pairs={{0,32},{32,0},{1,33},{33,1},{2,34},{34,2},{3,35},{35,3},{4,36},{36... | collective-permute-start | bytes 786440 | tf_op jit(solution)/shard_map/ppermute | solution.py:190
  111.7 17.1 %all-to-all-start.3 = ((bf16[4,64,1024]{2,1,0:T(8,128)(2,1)}), bf16[4,64,1024]{2,1,0:T(8,128)(2,1)S(1)}, u32[]{:S(2)}, u32[]{:S(2)}) async-start(bf16[4,64,1024]{2,1,0:T(8,128)(2,1)} %broadcast_in_dim.71), calls=%async_computation.3 | async-start | bytes 1048576 | tf_op jit(solution)/shard_map/all_to_all | solution.py:156
  116.7 48.8 %all-gather.2.cloned.1.call-start = ((), (), s32[]{:S(2)}) async-start(), calls=%async_computation.5 | async-start | bytes 1114112 | tf_op jit(solution)/shard_map/all_gather | solution.py:197
  128.8 11.9 %collective-permute-start.6 = (bf16[4,64,512]{2,1,0:T(8,128)(2,1)S(1)}, bf16[4,64,512]{2,1,0:T(8,128)(2,1)S(1)}, u32[]{:S(2)}, u32[]{:S(2)}) collective-permute-start(bf16[4,64,512]{2,1,0:T(8,128)(2,1)S(1)} %get-tuple-element.37), channel_id=1, source_target_pairs={{0,64},{64,0},{128,192},{192,128},{256,320},{320,256},{384,448},{4... | collective-permute-start | bytes 786440 | tf_op jit(solution)/shard_map/ppermute | solution.py:166
  130.8 10.0 %collective-permute-start.7 = (bf16[4,64,512]{2,1,0:T(8,128)(2,1)S(1)}, bf16[4,64,512]{2,1,0:T(8,128)(2,1)S(1)}, u32[]{:S(2)}, u32[]{:S(2)}) collective-permute-start(bf16[4,64,512]{2,1,0:T(8,128)(2,1)S(1)} %get-tuple-element.36), channel_id=1, source_target_pairs={{0,448},{64,128},{128,64},{192,256},{256,192},{320,384},{384,320},... | collective-permute-start | bytes 786440 | tf_op jit(solution)/shard_map/ppermute | solution.py:166
  134.1 16.1 %collective-permute-start.9 = (bf16[4,64,1024]{2,1,0:T(8,128)(2,1)S(1)}, bf16[4,64,1024]{2,1,0:T(8,128)(2,1)S(1)}, u32[]{:S(2)}, u32[]{:S(2)}) collective-permute-start(bf16[4,64,1024]{2,1,0:T(8,128)(2,1)S(1)} %all-to-all-done.3.mine_ref), channel_id=1, source_target_pairs={{0,32},{32,0},{1,33},{33,1},{2,34},{34,2},{3,35},{35,3},{4,36},{36... | collective-permute-start | bytes 1572872 | tf_op jit(solution)/shard_map/ppermute | solution.py:201
  140.8 11.4 %collective-permute-start.8 = (bf16[4,64,1024]{2,1,0:T(8,128)(2,1)S(1)}, bf16[4,64,1024]{2,1,0:T(8,128)(2,1)S(1)}, u32[]{:S(2)}, u32[]{:S(2)}) collective-permute-start(bf16[4,64,1024]{2,1,0:T(8,128)(2,1)S(1)} %constant_dynamic-update-slice_fusion.mine_ref.far_mine_ref), channel_id=1, source_target_pairs={{0,32},{32,0},{1,33},{33,1},{2,34},{34,2},{3,35},{35,3},{4,36},{36... | collective-permute-start | bytes 1572872 | tf_op jit(solution)/shard_map/ppermute | solution.py:206
  148.4 1.7 copy-start.1
  148.4 1.7 copy-start.3
  150.1 2.1 %copy-start.8 = (bf16[4,64,1024]{2,1,0:T(8,128)(2,1)}, bf16[4,64,1024]{2,1,0:T(8,128)(2,1)S(1)}, u32[]{:S(2)}) copy-start(bf16[4,64,1024]{2,1,0:T(8,128)(2,1)S(1)} %collective-permute-done.9.other_ref) | copy-start | bytes 1572868
  152.2 3.0 %copy-start.4 = (bf16[4,64,1024]{2,1,0:T(8,128)(2,1)}, bf16[4,64,1024]{2,1,0:T(8,128)(2,1)S(1)}, u32[]{:S(2)}) copy-start(bf16[4,64,1024]{2,1,0:T(8,128)(2,1)S(1)} %collective-permute-done.8.other_ref.far_other_ref) | copy-start | bytes 1572868
  155.2 6.3 %copy-start.5 = (bf16[4,64,1024]{2,1,0:T(8,128)(2,1)S(1)}, bf16[4,64,1024]{2,1,0:T(8,128)(2,1)}, u32[]{:S(2)}) copy-start(bf16[4,64,1024]{2,1,0:T(8,128)(2,1)} %copy-done.4) | copy-start | bytes 1572868
  155.2 6.3 %copy-start.9 = (bf16[4,64,1024]{2,1,0:T(8,128)(2,1)S(1)}, bf16[4,64,1024]{2,1,0:T(8,128)(2,1)}, u32[]{:S(2)}) copy-start(bf16[4,64,1024]{2,1,0:T(8,128)(2,1)} %copy-done.8) | copy-start | bytes 1572868
  155.2 25.7 %all-to-all-start.4 = ((bf16[32,32,384]{2,1,0:T(8,128)(2,1)}), bf16[32,32,384]{2,1,0:T(8,128)(2,1)S(1)}, u32[]{:S(2)}, u32[]{:S(2)}) async-start(bf16[32,32,384]{2,1,0:T(8,128)(2,1)} %bitcast.8), calls=%async_computation.4 | async-start | bytes 1572864 | tf_op jit(solution)/shard_map/all_to_all | solution.py:156
  161.6 2.1 %copy-start.12 = (bf16[1024,384]{1,0:T(8,128)(2,1)S(1)}, bf16[1024,384]{1,0:T(8,128)(2,1)}, u32[]{:S(2)}) copy-start(bf16[1024,384]{1,0:T(8,128)(2,1)} %get-tuple-element.32) | copy-start | bytes 2359300
  161.6 2.1 %copy-start.14 = (bf16[1024,384]{1,0:T(8,128)(2,1)S(1)}, bf16[1024,384]{1,0:T(8,128)(2,1)}, u32[]{:S(2)}) copy-start(bf16[1024,384]{1,0:T(8,128)(2,1)} %get-tuple-element.33) | copy-start | bytes 2359300
  162.3 1.4 copy-start.6
  163.6 1.9 %copy-start.11 = (bf16[1024,384]{1,0:T(8,128)(2,1)S(1)}, bf16[1024,384]{1,0:T(8,128)(2,1)}, u32[]{:S(2)}) copy-start(bf16[1024,384]{1,0:T(8,128)(2,1)} %fusion) | copy-start | bytes 2359300
  165.5 2.1 %copy-start.18 = (bf16[1024,512]{1,0:T(8,128)(2,1)S(1)}, bf16[1024,512]{1,0:T(8,128)(2,1)}, u32[]{:S(2)}) copy-start(bf16[1024,512]{1,0:T(8,128)(2,1)} %all-gather.2.cloned.1.call-done) | copy-start | bytes 3145732
  167.6 1.8 copy-start.7
  168.4 1.6 copy-start.13
  168.5 1.8 copy-start.15
Sparse Core Ops, SparseCore 0:
  119.6 38.4 all-gather.1

commit v8 on v7

--- a/solution.py
+++ b/solution.py
@@ -213,7 +213,7 @@
 
         outs = [jax.ShapeDtypeStruct((n_yh, n_yl, n_core, part, 2 * hid), BF)]
         (grads,) = call(order_body, outs, grads.size, (at, grads, other, far, far_other))
-        grads = grads.reshape(n_tok, 2 * hid)
+        grads, routed = lax.optimization_barrier((grads.reshape(n_tok, 2 * hid), routed))
         tok, cot = got[:, 0].reshape(n_tok, cols), got[:, 1].reshape(n_tok, cols)
         cot = (cot.astype(F32) * jnp.abs(routed)).astype(BF)
         masks = [routed > 0.0, routed < 0.0]

time: 189 us -> 187 us (0.989)
  blocking collectives: 47.3 us -> 65.6 us
  waiting for transfers between devices: 42.1 us -> 31.1 us
  starting transfers between devices: 50.4 us -> 43.5 us
  other arithmetic: 7.64 us -> 4.79 us
    all_to_all x2 -> x3, blocking collectives: 47.3 us -> 65.6 us  [exchange(): return lax.all_to_all(v, axes, split_axis=0, concat_axis=0, tiled=True)]
    all_to_all x3 -> x2, waiting for transfers between devices: 37.6 us -> 21.2 us  [exchange(): return lax.all_to_all(v, axes, split_axis=0, concat_axis=0, tiled=True)]
    all_gather x1, waiting for transfers between devices: 0.01 us -> 6.1 us  [per_device(): hidden = lax.all_gather(hidden, dp, axis=0, tiled=True)]
    all_to_all x3 -> x2, starting transfers between devices: 13.2 us -> 8.2 us  [exchange(): return lax.all_to_all(v, axes, split_axis=0, concat_axis=0, tiled=True)]
    convert_element_type x1, other arithmetic: 2.25 us -> 0.2 us  [per_device(): cot = (cot.astype(F32) * jnp.abs(routed)).astype(BF)]
    ppermute x1, starting transfers between devices: 6.68 us -> 4.65 us  [per_device(): other = lax.ppermute(grads, 'core', swap)]
    unnamed x41 -> x43, local copies, waits for them, and re-layouts: 4.52 us -> 4.42 us
  transfers between devices with their start and end apart: 14 -> 13, of which waited for: 5 -> 5; matrix products, arithmetic and copies ran while one was open for 7% -> 6% of each run, Pallas kernels for 4% -> 4%
where the time goes in v8:
time: 187 us; the launch traced here: 186 us
  blocking collectives  65.6 us (35%)
  starting transfers between devices  43.5 us (23%)
  waiting for transfers between devices  31.1 us (17%)
  between operations  14.5 us (8%)
  Pallas kernels  11.7 us (6%)
  local copies, waits for them, and re-layouts  8.31 us (4%)
  matrix products  6.68 us (4%)
  other arithmetic  4.79 us (3%)
    all_to_all x3, blocking collectives, exchange(): return lax.all_to_all(v, axes, split_axis=0, concat_axis=0, tiled=True)  65.6 us
    all_to_all x2, waiting for transfers between devices, exchange(): return lax.all_to_all(v, axes, split_axis=0, concat_axis=0, tiled=True)  21.2 us
    pallas_call x6, Pallas kernels, call(): pl.pallas_call(body, out_shape=outs, in_specs=in_specs, out_specs=[pl.Blo...  11.7 us
    ppermute x2, starting transfers between devices, neighbours(): lax.ppermute(v[1], along_y, right)  8.96 us
    all_to_all x2, starting transfers between devices, exchange(): return lax.all_to_all(v, axes, split_axis=0, concat_axis=0, tiled=True)  8.2 us
    dot_general x4, matrix products, dot(): lax.dot_general(a, b, (((ca,), (cb,)), ((), ())), preferred_element_type=...  6.68 us
    ppermute x3, starting transfers between devices, per_device(): lax.ppermute(g, 'core', swap)  6.53 us
    all_gather x1, waiting for transfers between devices, per_device(): hidden = lax.all_gather(hidden, dp, axis=0, tiled=True)  6.1 us
  transfers between devices with their start and end apart: 13, of which 5 were waited for; matrix products, arithmetic and copies ran while one was open for 6% of the time, Pallas kernels for 4%

profile of v8, /device:TPU:1, one launch (start us, length us, event | category | flops | bytes accessed | tf_op | source)
XLA Modules:
  0.0 186.2 jit_solution(5362006504206129993)
XLA Ops:
  7.2 0.8 pad_maximum_fusion.5
  8.0 24.2 %all_to_all.25 = bf16[8,2,32,384]{3,2,1,0:T(8,128)(2,1)S(1)} all-to-all(bf16[8,2,32,384]{3,2,1,0:T(8,128)(2,1)S(1)} %broadcast_in_dim.73), channel_id=1, replica_groups=mesh['yh'=4,'yl'=2,'core'=2,'x'=4,'z'=8] {'z'}, dimensions={0} | all-to-all | bytes 786432 | tf_op jit(solution)/shard_map/all_to_all | solution.py:156
  32.2 1.4 broadcast_in_dim.74
  33.6 4.2 %all-to-all-start.1 = ((bf16[4,8,2,32,384]{4,3,2,1,0:T(8,128)(2,1)}), bf16[4,8,2,32,384]{4,3,2,1,0:T(8,128)(2,1)S(1)}, u32[]{:S(2)}, u32[]{:S(2)}) async-start(bf16[4,8,2,32,384]{4,3,2,1,0:T(8,128)(2,1)} %broadcast_in_dim.74), calls=%async_computation.1 | async-start | bytes 3145728 | tf_op jit(solution)/shard_map/all_to_all | solution.py:156
  37.8 0.1 negate_select_fusion
  37.9 0.5 select_reduce_fusion
  38.4 0.2 copy.19.expert_ref
  38.6 0.1 pad_add_fusion.at_ref
  38.7 17.4 %all-to-all-done.1 = bf16[4,8,2,32,384]{4,3,2,1,0:T(8,128)(2,1)S(1)} async-done(((bf16[4,8,2,32,384]{4,3,2,1,0:T(8,128)(2,1)}), bf16[4,8,2,32,384]{4,3,2,1,0:T(8,128)(2,1)S(1)}, u32[]{:S(2)}, u32[]{:S(2)}) %all-to-all-start.1) | async-done | bytes 1572896 | tf_op jit(solution)/shard_map/all_to_all | solution.py:156
  56.1 1.1 copy-done.2
  57.3 1.1 copy-done.10
  58.4 2.6 %shard_map.112 = (f32[4,64,1536]{2,1,0:T(8,128)S(1)}, bf16[4,64,1536]{2,1,0:T(8,128)(2,1)S(1)}) custom-call(s32[2]{0:T(128)S(1)} %pad_add_fusion.at_ref, f32[1024,1]{1,0:T(8,128)S(1)} %copy.19.expert_ref, bf16[32,2,32,384]{3,2,1,0:T(8,128)(2,1)S(1)} %bitcast.27, bf16[2,384,512]{2,1,0:T(8,128)(2,1)S(1)} %copy-done, bf16[2,384,512]{2,1,0:T(8,128)(2,1)S(1)} %copy-done.2, ...), custom_call_target="tpu_custom_call" | custom-call | flops 1207959552 | bytes 6295560 | tf_op jit(solution)/shard_map/pallas_call | solution.py:35
  61.0 5.2 %collective-permute-start = (bf16[4,64,1536]{2,1,0:T(8,128)(2,1)S(1)}, bf16[4,64,1536]{2,1,0:T(8,128)(2,1)S(1)}, u32[]{:S(2)}, u32[]{:S(2)}) collective-permute-start(bf16[4,64,1536]{2,1,0:T(8,128)(2,1)S(1)} %get-tuple-element.21), channel_id=1, source_target_pairs={{0,32},{32,0},{1,33},{33,1},{2,34},{34,2},{3,35},{35,3},{4,36},{36... | collective-permute-start | bytes 2359304 | tf_op jit(solution)/shard_map/ppermute | solution.py:185
  66.3 2.6 %shard_map.111 = (f32[4,64,1536]{2,1,0:T(8,128)S(1)}, bf16[4,64,512]{2,1,0:T(8,128)(2,1)S(1)}, bf16[4,64,512]{2,1,0:T(8,128)(2,1)S(1)}, bf16[4,64,512]{2,1,0:T(8,128)(2,1)S(1)}) custom-call(s32[2]{0:T(128)S(1)} %pad_add_fusion.at_ref, f32[1024,1]{1,0:T(8,128)S(1)} %copy.19.expert_ref, bf16[32,2,32,384]{3,2,1,0:T(8,128)(2,1)S(1)} %bitcast.28, ...), custom_call_target="tpu_custom_call" | custom-call | flops 1207959552 | bytes 6295560 | tf_op jit(solution)/shard_map/pallas_call | solution.py:35
  68.9 0.2 add_convert_fusion.1
  69.1 0.1 fusion.17
  69.2 5.1 %collective-permute-start.5 = (bf16[4,64,768]{2,1,0:T(8,128)(2,1)S(1)}, bf16[4,64,768]{2,1,0:T(8,128)(2,1)S(1)}, u32[]{:S(2)}, u32[]{:S(2)}) collective-permute-start(bf16[4,64,768]{2,1,0:T(8,128)(2,1)S(1)} %get-tuple-element.29), channel_id=1, source_target_pairs={{0,448},{64,128},{128,64},{192,256},{256,192},{320,384},{384,320},... | collective-permute-start | bytes 1179656 | tf_op jit(solution)/shard_map/ppermute | solution.py:166
  74.3 1.9 %collective-permute-start.4 = (bf16[4,64,768]{2,1,0:T(8,128)(2,1)S(1)}, bf16[4,64,768]{2,1,0:T(8,128)(2,1)S(1)}, u32[]{:S(2)}, u32[]{:S(2)}) collective-permute-start(bf16[4,64,768]{2,1,0:T(8,128)(2,1)S(1)} %get-tuple-element.28), channel_id=1, source_target_pairs={{0,64},{64,0},{128,192},{192,128},{256,320},{320,256},{384,448},{4... | collective-permute-start | bytes 1179656 | tf_op jit(solution)/shard_map/ppermute | solution.py:166
  76.2 2.2 %collective-permute-start.3 = (bf16[4,64,512]{2,1,0:T(8,128)(2,1)S(1)}, bf16[4,64,512]{2,1,0:T(8,128)(2,1)S(1)}, u32[]{:S(2)}, u32[]{:S(2)}) collective-permute-start(bf16[4,64,512]{2,1,0:T(8,128)(2,1)S(1)} %get-tuple-element.27), channel_id=1, source_target_pairs={{0,32},{32,0},{1,33},{33,1},{2,34},{34,2},{3,35},{35,3},{4,36},{36... | collective-permute-start | bytes 786440 | tf_op jit(solution)/shard_map/ppermute | solution.py:190
  78.4 2.1 %collective-permute-start.2 = (bf16[4,64,512]{2,1,0:T(8,128)(2,1)S(1)}, bf16[4,64,512]{2,1,0:T(8,128)(2,1)S(1)}, u32[]{:S(2)}, u32[]{:S(2)}) collective-permute-start(bf16[4,64,512]{2,1,0:T(8,128)(2,1)S(1)} %get-tuple-element.26), channel_id=1, source_target_pairs={{0,32},{32,0},{1,33},{33,1},{2,34},{34,2},{3,35},{35,3},{4,36},{36... | collective-permute-start | bytes 786440 | tf_op jit(solution)/shard_map/ppermute | solution.py:190
  80.6 2.2 %collective-permute-start.1 = (bf16[4,64,512]{2,1,0:T(8,128)(2,1)S(1)}, bf16[4,64,512]{2,1,0:T(8,128)(2,1)S(1)}, u32[]{:S(2)}, u32[]{:S(2)}) collective-permute-start(bf16[4,64,512]{2,1,0:T(8,128)(2,1)S(1)} %get-tuple-element.25), channel_id=1, source_target_pairs={{0,32},{32,0},{1,33},{33,1},{2,34},{34,2},{3,35},{35,3},{4,36},{36... | collective-permute-start | bytes 786440 | tf_op jit(solution)/shard_map/ppermute | solution.py:190
  82.8 0.0 collective-permute-done.3
  82.8 1.2 collective-permute-done.1
  84.0 2.6 %collective-permute-done.4 = bf16[4,64,768]{2,1,0:T(8,128)(2,1)S(1)} collective-permute-done((bf16[4,64,768]{2,1,0:T(8,128)(2,1)S(1)}, bf16[4,64,768]{2,1,0:T(8,128)(2,1)S(1)}, u32[]{:S(2)}, u32[]{:S(2)}) %collective-permute-start.4) | collective-permute-done | bytes 393248 | tf_op jit(solution)/shard_map/ppermute | solution.py:166
  86.6 0.3 add_convert_fusion
  86.9 23.1 %all_to_all.26 = bf16[4,64,1536]{2,1,0:T(8,128)(2,1)S(1)} all-to-all(bf16[4,64,1536]{2,1,0:T(8,128)(2,1)S(1)} %add_convert_fusion), channel_id=1, replica_groups=mesh['yh'=4,'yl'=2,'core'=2,'x'=4,'z'=8] {'yh'}, dimensions={0} | all-to-all | bytes 1572864 | tf_op jit(solution)/shard_map/all_to_all | solution.py:156
  110.0 0.1 convert_reduce_fusion
  110.1 0.7 multiply_convert_fusion
  110.8 0.1 broadcast_in_dim.75
  110.9 18.3 %all_to_all.27.mine_ref = bf16[4,64,1024]{2,1,0:T(8,128)(2,1)S(1)} all-to-all(bf16[4,64,1024]{2,1,0:T(8,128)(2,1)S(1)} %broadcast_in_dim.75), channel_id=1, replica_groups=mesh['yh'=4,'yl'=2,'core'=2,'x'=4,'z'=8] {'yh'}, dimensions={0} | all-to-all | bytes 1048576 | tf_op jit(solution)/shard_map/all_to_all | solution.py:156
  129.2 0.8 fusion.18
  129.9 1.9 %collective-permute-start.6 = (bf16[4,64,512]{2,1,0:T(8,128)(2,1)S(1)}, bf16[4,64,512]{2,1,0:T(8,128)(2,1)S(1)}, u32[]{:S(2)}, u32[]{:S(2)}) collective-permute-start(bf16[4,64,512]{2,1,0:T(8,128)(2,1)S(1)} %get-tuple-element.43), channel_id=1, source_target_pairs={{0,64},{64,0},{128,192},{192,128},{256,320},{320,256},{384,448},{4... | collective-permute-start | bytes 786440 | tf_op jit(solution)/shard_map/ppermute | solution.py:166
  131.9 0.0 all-gather.2.cloned.1.call-update
  131.9 3.9 %collective-permute-start.7 = (bf16[4,64,512]{2,1,0:T(8,128)(2,1)}, bf16[4,64,512]{2,1,0:T(8,128)(2,1)S(1)}, u32[]{:S(2)}, u32[]{:S(2)}) collective-permute-start(bf16[4,64,512]{2,1,0:T(8,128)(2,1)} %get-tuple-element.42), channel_id=1, source_target_pairs={{0,448},{64,128},{128,64},{192,256},{256,192},{320,384},{384,320},... | collective-permute-start | bytes 786440 | tf_op jit(solution)/shard_map/ppermute | solution.py:166
  135.8 4.6 %collective-permute-start.9 = (bf16[4,64,1024]{2,1,0:T(8,128)(2,1)S(1)}, bf16[4,64,1024]{2,1,0:T(8,128)(2,1)S(1)}, u32[]{:S(2)}, u32[]{:S(2)}) collective-permute-start(bf16[4,64,1024]{2,1,0:T(8,128)(2,1)S(1)} %all_to_all.27.mine_ref), channel_id=1, source_target_pairs={{0,32},{32,0},{1,33},{33,1},{2,34},{34,2},{3,35},{35,3},{4,36},{36... | collective-permute-start | bytes 1572872 | tf_op jit(solution)/shard_map/ppermute | solution.py:201
  140.5 0.0 copy-start.1
  140.5 0.0 copy-start.3
  140.5 6.1 %collective-permute-start.8 = (bf16[4,64,1024]{2,1,0:T(8,128)(2,1)S(1)}, bf16[4,64,1024]{2,1,0:T(8,128)(2,1)S(1)}, u32[]{:S(2)}, u32[]{:S(2)}) collective-permute-start(bf16[4,64,1024]{2,1,0:T(8,128)(2,1)S(1)} %constant_dynamic-update-slice_fusion.mine_ref.far_mine_ref), channel_id=1, source_target_pairs={{0,32},{32,0},{1,33},{33,1},{2,34},{34,2},{3,35},{35,3},{4,36},{36... | collective-permute-start | bytes 1572872 | tf_op jit(solution)/shard_map/ppermute | solution.py:206
  146.6 1.3 fusion.16
  147.9 0.0 copy-start.8
  147.9 2.1 %shard_map.113.refs_0_ = bf16[4,128,384]{2,1,0:T(8,128)(2,1)S(1)} custom-call(s32[2]{0:T(128)S(1)} %pad_add_fusion.at_ref, f32[1024,1]{1,0:T(8,128)S(1)} %copy.19.expert_ref, bf16[2,384,512]{2,1,0:T(8,128)(2,1)S(1)} %copy-done.1, bf16[2,384,512]{2,1,0:T(8,128)(2,1)S(1)} %copy-done.3, bf16[4,64,1024]{2,1,0:T(8,128)(2,1)S(1)} %all_to_all.27.mine_ref, ...), custom_call_target="tpu_custom_call" | custom-call | flops 805306368 | bytes 3018760 | tf_op jit(solution)/shard_map/pallas_call | solution.py:35
  150.0 3.0 %shard_map.114 = bf16[4,2,128,384]{3,2,1,0:T(8,128)(2,1)} custom-call(s32[2]{0:T(128)S(1)} %pad_add_fusion.at_ref, f32[1024,1]{1,0:T(8,128)S(1)} %copy.19.expert_ref, bf16[2,384,512]{2,1,0:T(8,128)(2,1)S(1)} %copy-done.1, bf16[2,384,512]{2,1,0:T(8,128)(2,1)S(1)} %copy-done.3, ...), custom_call_target="tpu_custom_call" | custom-call | flops 805306368 | bytes 3805192 | tf_op jit(solution)/shard_map/pallas_call | solution.py:35
  153.0 4.0 %all-to-all-start.4 = ((bf16[32,32,384]{2,1,0:T(8,128)(2,1)}), bf16[32,32,384]{2,1,0:T(8,128)(2,1)S(1)}, u32[]{:S(2)}, u32[]{:S(2)}) async-start(bf16[32,32,384]{2,1,0:T(8,128)(2,1)} %bitcast.8), calls=%async_computation.4 | async-start | bytes 1572864 | tf_op jit(solution)/shard_map/all_to_all | solution.py:156
  157.1 0.0 copy-start.12
  157.1 0.7 shard_map.116
  157.8 0.0 copy-start.11
  157.9 0.3 copy-done.12
  158.2 0.8 bitcast_select_fusion.1
  159.1 0.0 copy-start.15
  159.1 0.5 copy-done.11
  159.6 0.2 fusion
  159.8 0.2 copy-done.13
  160.0 0.2 copy-done.15
  160.2 1.9 %convolution_convert_fusion.1 = bf16[768,512]{1,0:T(8,128)(2,1)} fusion(bf16[1024,1024]{1,0:T(8,128)(2,1)S(1)} %bitcast.30, bf16[1024,384]{1,0:T(8,128)(2,1)S(1)} %get-tuple-element.39, bf16[1024,384]{1,0:T(8,128)(2,1)S(1)} %get-tuple-element.38), kind=kOutput, calls=%fused_computation.9 | convolution fusion | flops 808845312 | bytes 3407872 | tf_op jit(solution)/shard_map/dot_general | solution.py:18
  162.1 6.1 %all-gather.2.cloned.1.call-done = bf16[1024,512]{1,0:T(8,128)(2,1)} async-done(((bf16[64,512]{1,0:T(8,128)(2,1)}), bf16[1024,512]{1,0:T(8,128)(2,1)}) %all-gather.2.cloned.1.call-update) | async-done | bytes 1048592 | tf_op jit(solution)/shard_map/all_gather | solution.py:197
  168.2 2.1 %fusion.2 = bf16[1,512,384]{2,1,0:T(8,128)(2,1)S(1)} fusion(bf16[1024,512]{1,0:T(8,128)(2,1)} %all-gather.2.cloned.1.call-done, bf16[1024,384]{1,0:T(8,128)(2,1)S(1)} %fusion, pred[1024]{0:T(1024)(128)(4,1)S(1)} %get-tuple-element.35), kind=kOutput, calls=%fused_computation.13 | convolution fusion | flops 403243008 | bytes 2229248 | tf_op jit(solution)/shard_map/dot_general | solution.py:18
  170.3 0.8 fusion.1
  171.1 0.0 copy-start.16
  171.2 1.0 pad_maximum_fusion.3
  172.1 0.6 copy-done.14
  172.7 0.3 copy-done.16
  172.9 1.9 %convolution_convert_fusion = bf16[768,512]{1,0:T(8,128)(2,1)} fusion(bf16[1024,1024]{1,0:T(8,128)(2,1)S(1)} %bitcast.31, bf16[1024,384]{1,0:T(8,128)(2,1)S(1)} %copy-done.16, bf16[1024,384]{1,0:T(8,128)(2,1)S(1)} %copy-done.14), kind=kOutput, calls=%fused_computation.8 | convolution fusion | flops 808845312 | bytes 3407872 | tf_op jit(solution)/shard_map/dot_general | solution.py:18
  174.8 3.8 %all-to-all-done.4.x_ref = bf16[32,32,384]{2,1,0:T(8,128)(2,1)S(1)} async-done(((bf16[32,32,384]{2,1,0:T(8,128)(2,1)}), bf16[32,32,384]{2,1,0:T(8,128)(2,1)S(1)}, u32[]{:S(2)}, u32[]{:S(2)}) %all-to-all-start.4) | async-done | bytes 786464 | tf_op jit(solution)/shard_map/all_to_all | solution.py:156
  178.6 0.7 shard_map.115
  (42 shorter events, 0.2 us)
Async XLA Ops:
  33.6 4.2 %copy-start.20 = (s32[8,1]{0,1:T(1,128)S(1)}, s32[8,1]{0,1:T(1,128)}, u32[]{:S(2)}) copy-start(s32[8,1]{0,1:T(1,128)} %param.14) | copy-start | bytes 100
  33.6 4.2 %copy-start.18 = (f32[1024]{0:T(1024)S(1)}, f32[1024]{0:T(1024)}, u32[]{:S(2)}) copy-start(f32[1024]{0:T(1024)} %param.15) | copy-start | bytes 12292
  33.6 4.3 %copy-start.17 = (s32[1024]{0:T(1024)S(1)}, s32[1024]{0:T(1024)}, u32[]{:S(2)}) copy-start(s32[1024]{0:T(1024)} %param.13) | copy-start | bytes 12292
  33.6 22.5 %copy-start = (bf16[2,384,512]{2,1,0:T(8,128)(2,1)S(1)}, bf16[2,384,512]{2,1,0:T(8,128)(2,1)}, u32[]{:S(2)}) copy-start(bf16[2,384,512]{2,1,0:T(8,128)(2,1)} %gate_ref.3) | copy-start | bytes 2359300
  33.6 22.5 %all-to-all-start.1 = ((bf16[4,8,2,32,384]{4,3,2,1,0:T(8,128)(2,1)}), bf16[4,8,2,32,384]{4,3,2,1,0:T(8,128)(2,1)S(1)}, u32[]{:S(2)}, u32[]{:S(2)}) async-start(bf16[4,8,2,32,384]{4,3,2,1,0:T(8,128)(2,1)} %broadcast_in_dim.74), calls=%async_computation.1 | async-start | bytes 3145728 | tf_op jit(solution)/shard_map/all_to_all | solution.py:156
  37.8 130.4 %all-gather.2.cloned.1.call-start = ((), (), s32[]{:S(2)}) async-start(), calls=%async_computation.5 | async-start | bytes 1114112 | tf_op jit(solution)/shard_map/all_gather | solution.py:197
  56.1 1.1 copy-start.2
  57.3 1.1 copy-start.10
  61.0 7.9 %collective-permute-start = (bf16[4,64,1536]{2,1,0:T(8,128)(2,1)S(1)}, bf16[4,64,1536]{2,1,0:T(8,128)(2,1)S(1)}, u32[]{:S(2)}, u32[]{:S(2)}) collective-permute-start(bf16[4,64,1536]{2,1,0:T(8,128)(2,1)S(1)} %get-tuple-element.21), channel_id=1, source_target_pairs={{0,32},{32,0},{1,33},{33,1},{2,34},{34,2},{3,35},{35,3},{4,36},{36... | collective-permute-start | bytes 2359304 | tf_op jit(solution)/shard_map/ppermute | solution.py:185
  69.2 14.8 %collective-permute-start.5 = (bf16[4,64,768]{2,1,0:T(8,128)(2,1)S(1)}, bf16[4,64,768]{2,1,0:T(8,128)(2,1)S(1)}, u32[]{:S(2)}, u32[]{:S(2)}) collective-permute-start(bf16[4,64,768]{2,1,0:T(8,128)(2,1)S(1)} %get-tuple-element.29), channel_id=1, source_target_pairs={{0,448},{64,128},{128,64},{192,256},{256,192},{320,384},{384,320},... | collective-permute-start | bytes 1179656 | tf_op jit(solution)/shard_map/ppermute | solution.py:166
  74.3 12.3 %collective-permute-start.4 = (bf16[4,64,768]{2,1,0:T(8,128)(2,1)S(1)}, bf16[4,64,768]{2,1,0:T(8,128)(2,1)S(1)}, u32[]{:S(2)}, u32[]{:S(2)}) collective-permute-start(bf16[4,64,768]{2,1,0:T(8,128)(2,1)S(1)} %get-tuple-element.28), channel_id=1, source_target_pairs={{0,64},{64,0},{128,192},{192,128},{256,320},{320,256},{384,448},{4... | collective-permute-start | bytes 1179656 | tf_op jit(solution)/shard_map/ppermute | solution.py:166
  76.2 6.6 %collective-permute-start.3 = (bf16[4,64,512]{2,1,0:T(8,128)(2,1)S(1)}, bf16[4,64,512]{2,1,0:T(8,128)(2,1)S(1)}, u32[]{:S(2)}, u32[]{:S(2)}) collective-permute-start(bf16[4,64,512]{2,1,0:T(8,128)(2,1)S(1)} %get-tuple-element.27), channel_id=1, source_target_pairs={{0,32},{32,0},{1,33},{33,1},{2,34},{34,2},{3,35},{35,3},{4,36},{36... | collective-permute-start | bytes 786440 | tf_op jit(solution)/shard_map/ppermute | solution.py:190
  78.4 4.4 %collective-permute-start.2 = (bf16[4,64,512]{2,1,0:T(8,128)(2,1)S(1)}, bf16[4,64,512]{2,1,0:T(8,128)(2,1)S(1)}, u32[]{:S(2)}, u32[]{:S(2)}) collective-permute-start(bf16[4,64,512]{2,1,0:T(8,128)(2,1)S(1)} %get-tuple-element.26), channel_id=1, source_target_pairs={{0,32},{32,0},{1,33},{33,1},{2,34},{34,2},{3,35},{35,3},{4,36},{36... | collective-permute-start | bytes 786440 | tf_op jit(solution)/shard_map/ppermute | solution.py:190
  80.6 3.4 %collective-permute-start.1 = (bf16[4,64,512]{2,1,0:T(8,128)(2,1)S(1)}, bf16[4,64,512]{2,1,0:T(8,128)(2,1)S(1)}, u32[]{:S(2)}, u32[]{:S(2)}) collective-permute-start(bf16[4,64,512]{2,1,0:T(8,128)(2,1)S(1)} %get-tuple-element.25), channel_id=1, source_target_pairs={{0,32},{32,0},{1,33},{33,1},{2,34},{34,2},{3,35},{35,3},{4,36},{36... | collective-permute-start | bytes 786440 | tf_op jit(solution)/shard_map/ppermute | solution.py:190
  129.9 10.5 %collective-permute-start.6 = (bf16[4,64,512]{2,1,0:T(8,128)(2,1)S(1)}, bf16[4,64,512]{2,1,0:T(8,128)(2,1)S(1)}, u32[]{:S(2)}, u32[]{:S(2)}) collective-permute-start(bf16[4,64,512]{2,1,0:T(8,128)(2,1)S(1)} %get-tuple-element.43), channel_id=1, source_target_pairs={{0,64},{64,0},{128,192},{192,128},{256,320},{320,256},{384,448},{4... | collective-permute-start | bytes 786440 | tf_op jit(solution)/shard_map/ppermute | solution.py:166
  131.9 8.6 %collective-permute-start.7 = (bf16[4,64,512]{2,1,0:T(8,128)(2,1)}, bf16[4,64,512]{2,1,0:T(8,128)(2,1)S(1)}, u32[]{:S(2)}, u32[]{:S(2)}) collective-permute-start(bf16[4,64,512]{2,1,0:T(8,128)(2,1)} %get-tuple-element.42), channel_id=1, source_target_pairs={{0,448},{64,128},{128,64},{192,256},{256,192},{320,384},{384,320},... | collective-permute-start | bytes 786440 | tf_op jit(solution)/shard_map/ppermute | solution.py:166
  135.8 12.1 %collective-permute-start.9 = (bf16[4,64,1024]{2,1,0:T(8,128)(2,1)S(1)}, bf16[4,64,1024]{2,1,0:T(8,128)(2,1)S(1)}, u32[]{:S(2)}, u32[]{:S(2)}) collective-permute-start(bf16[4,64,1024]{2,1,0:T(8,128)(2,1)S(1)} %all_to_all.27.mine_ref), channel_id=1, source_target_pairs={{0,32},{32,0},{1,33},{33,1},{2,34},{34,2},{3,35},{35,3},{4,36},{36... | collective-permute-start | bytes 1572872 | tf_op jit(solution)/shard_map/ppermute | solution.py:201
  140.5 7.4 %copy-start.1 = (bf16[2,384,512]{2,1,0:T(8,128)(2,1)S(1)}, bf16[2,384,512]{2,1,0:T(8,128)(2,1)}, u32[]{:S(2)}) copy-start(bf16[2,384,512]{2,1,0:T(8,128)(2,1)} %gate_ref.3) | copy-start | bytes 2359300
  140.5 7.4 %copy-start.3 = (bf16[2,384,512]{2,1,0:T(8,128)(2,1)S(1)}, bf16[2,384,512]{2,1,0:T(8,128)(2,1)}, u32[]{:S(2)}) copy-start(bf16[2,384,512]{2,1,0:T(8,128)(2,1)} %up_ref.3) | copy-start | bytes 2359300
  140.5 9.5 %collective-permute-start.8 = (bf16[4,64,1024]{2,1,0:T(8,128)(2,1)S(1)}, bf16[4,64,1024]{2,1,0:T(8,128)(2,1)S(1)}, u32[]{:S(2)}, u32[]{:S(2)}) collective-permute-start(bf16[4,64,1024]{2,1,0:T(8,128)(2,1)S(1)} %constant_dynamic-update-slice_fusion.mine_ref.far_mine_ref), channel_id=1, source_target_pairs={{0,32},{32,0},{1,33},{33,1},{2,34},{34,2},{3,35},{35,3},{4,36},{36... | collective-permute-start | bytes 1572872 | tf_op jit(solution)/shard_map/ppermute | solution.py:206
  147.9 2.1 %copy-start.8 = (bf16[4,64,1024]{2,1,0:T(8,128)(2,1)}, bf16[4,64,1024]{2,1,0:T(8,128)(2,1)S(1)}, u32[]{:S(2)}) copy-start(bf16[4,64,1024]{2,1,0:T(8,128)(2,1)S(1)} %collective-permute-done.9.other_ref) | copy-start | bytes 1572868
  150.0 3.0 %copy-start.4 = (bf16[4,64,1024]{2,1,0:T(8,128)(2,1)}, bf16[4,64,1024]{2,1,0:T(8,128)(2,1)S(1)}, u32[]{:S(2)}) copy-start(bf16[4,64,1024]{2,1,0:T(8,128)(2,1)S(1)} %collective-permute-done.8.other_ref.far_other_ref) | copy-start | bytes 1572868
  153.0 4.1 %copy-start.9 = (bf16[4,64,1024]{2,1,0:T(8,128)(2,1)S(1)}, bf16[4,64,1024]{2,1,0:T(8,128)(2,1)}, u32[]{:S(2)}) copy-start(bf16[4,64,1024]{2,1,0:T(8,128)(2,1)} %copy-done.8) | copy-start | bytes 1572868
  153.0 4.1 %copy-start.5 = (bf16[4,64,1024]{2,1,0:T(8,128)(2,1)S(1)}, bf16[4,64,1024]{2,1,0:T(8,128)(2,1)}, u32[]{:S(2)}) copy-start(bf16[4,64,1024]{2,1,0:T(8,128)(2,1)} %copy-done.4) | copy-start | bytes 1572868
  153.0 25.6 %all-to-all-start.4 = ((bf16[32,32,384]{2,1,0:T(8,128)(2,1)}), bf16[32,32,384]{2,1,0:T(8,128)(2,1)S(1)}, u32[]{:S(2)}, u32[]{:S(2)}) async-start(bf16[32,32,384]{2,1,0:T(8,128)(2,1)} %bitcast.8), calls=%async_computation.4 | async-start | bytes 1572864 | tf_op jit(solution)/shard_map/all_to_all | solution.py:156
  157.1 1.1 copy-start.12
  157.8 2.0 %copy-start.6 = (bf16[4,2,2,64,1024]{4,3,2,1,0:T(8,128)(2,1)}, bf16[4,2,2,64,1024]{4,3,2,1,0:T(8,128)(2,1)S(1)}, u32[]{:S(2)}) copy-start(bf16[4,2,2,64,1024]{4,3,2,1,0:T(8,128)(2,1)S(1)} %shard_map.116) | copy-start | bytes 6291460
  157.8 1.8 copy-start.11
  159.1 0.9 copy-start.13
  159.1 1.1 copy-start.15
  168.2 2.1 %copy-start.19 = (bf16[1024,512]{1,0:T(8,128)(2,1)S(1)}, bf16[1024,512]{1,0:T(8,128)(2,1)}, u32[]{:S(2)}) copy-start(bf16[1024,512]{1,0:T(8,128)(2,1)} %all-gather.2.cloned.1.call-done) | copy-start | bytes 3145732
  170.3 1.8 copy-start.7
  171.1 1.6 copy-start.14
  171.1 1.8 copy-start.16
Sparse Core Ops, SparseCore 0:
  132.0 36.1 all-gather.1
